TPU v7x, 256 devices: a whole 4x4x8 slice. The times are simulated.
256 devices in a mesh: phase: 2 (over core), tok: 32 (over z, x), mp: 4 (over y).
Axes of the slice: x: 4, y: 4, z: 8, core: 2. Of those that a mesh axis runs over, the one named last changes fastest.
Arguments:
- hidden: bfloat16 [2, 4096, 6656], P('phase', 'tok', 'mp'), may hold values from -30 to 30
- w_qkv: bfloat16 [2, 6656, 3, 4096], P('phase', 'mp', None, 'tok'), may hold values from -1 to 1
- segment_ids: int32 [2, 4096], P('phase'), may hold values from 0 to 3, never falling along the last dimension, each value on 1 to 2048 neighbouring positions
- exit_flags: int32 [2, 32], P('phase'), may hold values from 0 to 1, as said below
Outputs:
- attended: bfloat16 [2, 4096, 4096], P('phase', 'mp', 'tok')
- handed: bfloat16 [2, 4096, 4096], P('phase', 'mp', 'tok')
Inputs may be any that keep to these rules, and one draw needn't show every extreme that they name: `exit_flags`: in each micro-batch exactly 16 of the 32 blocks have flag 0.
All inputs are finite; a program needn't handle non-finite values.
Results may differ from a plain program's by a relative error of at most 0.0068.
Values may be sent and summed in bfloat16 or wider, within the bound.
No kernel may reach another device: no remote copies, remote signals or barrier semaphores. Data moves between devices by JAX's collectives and lax.ppermute only.
A program may use at most 64 MiB of HBM per device.

v0:
```python
import math

import jax
import jax.numpy as jnp
from jax import lax
from jax.sharding import PartitionSpec as P

HEAD = 128
BLOCK = 128


def shifted(block, axis, distance):
    devices = range(lax.axis_size(axis))
    route = [((i - distance) % len(devices), i) for i in devices]
    return lax.ppermute(block, axis, route)


def attend(query, keys, values, query_pos, segment, key_pos):
    heads_here = query.shape[1] // HEAD
    total = keys.shape[0]
    key_heads = keys.reshape(total, heads_here, HEAD)
    value_heads = values.reshape(total, heads_here, HEAD)
    key_segment = jnp.take(segment, key_pos)
    scale = 1.0 / math.sqrt(HEAD)
    block_rows = query.shape[0]
    scores = (
        jnp.einsum(
            "rhd,shd->hrs",
            query.reshape(block_rows, heads_here, HEAD),
            key_heads,
            preferred_element_type=jnp.float32,
        )
        * scale
    )
    own_segment = jnp.take(segment, query_pos)
    allowed = (key_pos[None, :] <= query_pos[:, None]) & (
        key_segment[None, :] == own_segment[:, None]
    )
    scores = jnp.where(allowed[None], scores, -1e30)
    peak = jnp.max(scores, axis=-1, keepdims=True)
    expo = jnp.exp(scores - peak)
    probs = (expo / jnp.sum(expo, axis=-1, keepdims=True)).astype(jnp.bfloat16)
    mixed = jnp.einsum("hrs,shd->rhd", probs, value_heads, preferred_element_type=jnp.float32)
    return mixed.reshape(block_rows, heads_here * HEAD).astype(jnp.bfloat16)


def local(hidden, w_qkv, segment_ids, exit_flags):
    rows_here = hidden[0]
    weights = w_qkv[0]
    width_here = rows_here.shape[1]
    head_cols = weights.shape[2]
    flat_weights = weights.reshape(width_here, 3 * head_cols)
    segment = segment_ids[0]
    flags = exit_flags[0]
    groups = lax.axis_size("mp")
    member = lax.axis_index("mp")
    partial_value = jnp.dot(
        lax.all_gather(rows_here, "tok", axis=0, tiled=True),
        flat_weights,
        preferred_element_type=jnp.float32,
    )
    total = partial_value.shape[0]
    quarter = total // groups
    query_part = partial_value[:, :head_cols]
    key_value_part = partial_value[:, head_cols:]
    my_pos = member * quarter + jnp.arange(quarter, dtype=jnp.int32)
    my_blocks = my_pos // BLOCK
    alive = jnp.take(flags, my_blocks) == 0
    query = lax.psum_scatter(query_part, "mp", scatter_dimension=0, tiled=True).astype(jnp.bfloat16)
    mine = lax.psum_scatter(key_value_part, "mp", scatter_dimension=0, tiled=True).astype(
        jnp.bfloat16
    )
    key_value = lax.all_gather(mine, "mp", axis=0, tiled=True)
    all_pos = jnp.arange(total, dtype=jnp.int32)
    mixed = attend(
        query, key_value[:, :head_cols], key_value[:, head_cols:], my_pos, segment, all_pos
    )
    zeros = jnp.zeros((quarter, head_cols), jnp.bfloat16)
    result = jnp.where(alive[:, None], mixed, zeros)
    handed = shifted(result, "phase", 1)
    return (result[None], handed[None])


def solution(mesh):
    in_specs = (
        P("phase", "tok", "mp"),
        P("phase", "mp", None, "tok"),
        P("phase", None),
        P("phase", None),
    )
    out_specs = (P("phase", "mp", "tok"), P("phase", "mp", "tok"))
    return jax.shard_map(local, mesh=mesh, in_specs=in_specs, out_specs=out_specs, check_vma=False)
```

profile of v0, /device:TPU:1, one launch (start us, length us, event | category | flops | bytes accessed | tf_op | source)
XLA Modules:
  0.0 305.8 jit_solution(11252812539057561447)
XLA Ops:
  7.2 0.0 copy-start
  7.2 0.0 all-gather.6.cloned.1.call-start
  7.2 0.7 all-gather.6.cloned.1.call-update
  7.9 0.0 reduce-scatter.3.cloned.1.call-start
  8.0 1.8 copy.8
  9.8 128.8 %all-gather.6.cloned.1.call-done = bf16[1,4096,1664]{2,1,0:T(8,128)(2,1)} async-done(((bf16[1,128,1664]{2,1,0:T(8,128)(2,1)}), bf16[1,4096,1664]{2,1,0:T(8,128)(2,1)}) %all-gather.6.cloned.1.call-update) | async-done | bytes 13631504 | tf_op jit(solution)/shard_map/all_gather | solution.py:58
  138.6 10.6 %fusion.2 = f32[4096,384]{1,0:T(8,128)S(1)} fusion(bf16[1664,384]{0,1:T(8,128)(2,1)S(1)} %bitcast.52, bf16[1,4096,1664]{2,1,0:T(8,128)(2,1)} %all-gather.6.cloned.1.call-done), kind=kOutput, calls=%fused_computation.8 | convolution fusion | flops 5234491392 | bytes 21200896 | tf_op jit(solution)/shard_map/dot_general | solution.py:57
  149.2 0.0 copy-start.1
  149.3 2.7 copy-done.1
  151.9 0.0 copy-start.2
  151.9 2.4 slice.86
  154.3 0.0 reduce-scatter.3.cloned.1.call-update
  154.3 0.0 reduce-scatter.5.cloned.1.call-start
  154.3 3.0 slice.88
  157.4 0.0 reduce-scatter.5.cloned.1.call-update
  157.4 0.0 all-gather.4.cloned.1.call-start
  157.4 43.9 %reduce-scatter.3.cloned.1.call-done = f32[1024,256]{1,0:T(8,128)} async-done(((f32[4096,256]{1,0:T(8,128)}), f32[1024,256]{1,0:T(8,128)}) %reduce-scatter.3.cloned.1.call-update) | async-done | bytes 1048592 | tf_op jit(solution)/shard_map/reduce_scatter | solution.py:70
  201.4 2.1 convert_element_type.34
  203.4 0.0 all-gather.4.cloned.1.call-update
  203.5 0.0 copy-done.2
  203.5 0.7 fusion.19
  204.2 0.7 fusion.18
  204.9 4.4 %compare_select_fusion.1 = (s32[1024,1]{0,1:T(1,128)S(1)}, s32[1024,1]{0,1:T(1,128)S(1)}) fusion(s32[]{:T(128)} %bitcast.25, s32[]{:T(128)} %bitcast.26, s32[]{:T(128)} %bitcast.27, s32[]{:T(128)} %bitcast.28, s32[]{:T(128)} %bitcast.29, s32[]{:T(128)} %bitcast.31, s32[]{:T(128)} %bitcast.30, s32[]{:T(128)S(6)} %mul.10), kind=kLoop, calls=%fused_computation.46 | loop fusion | flops 33792 | bytes 8224 | tf_op jit(solution)/shard_map/jit(_take)/gather | solution.py:68
  209.3 0.0 copy-done
  209.3 6.2 %gather_fusion.1 = s32[1024]{0:T(1024)S(1)} fusion(s32[4096]{0:T(1024)S(1)} %bitcast.51, s32[1024]{0:T(1024)S(1)} %broadcast_clamp_fusion), kind=kCustom, calls=%fused_computation.1 | custom fusion | bytes 12288 | tf_op jit(solution)/shard_map/jit(_take)/gather | solution.py:35
  215.5 23.0 %gather_fusion = s32[4096]{0:T(1024)S(1)} fusion(s32[4096]{0:T(1024)S(1)} %bitcast.50, s32[4096]{0:T(1024)S(1)} %iota_clamp_fusion), kind=kCustom, calls=%fused_computation | custom fusion | bytes 49152 | tf_op jit(solution)/shard_map/jit(_take)/gather | solution.py:23
  238.5 0.1 compare_reduce_fusion.24
  238.6 0.1 compare_reduce_fusion
  238.6 0.1 compare_reduce_fusion.2
  238.7 0.1 compare_reduce_fusion.4
  238.8 0.1 compare_reduce_fusion.6
  238.8 0.1 compare_reduce_fusion.8
  238.9 0.1 compare_reduce_fusion.10
  238.9 0.1 compare_reduce_fusion.12
  239.0 0.1 compare_reduce_fusion.14
  239.1 0.1 compare_reduce_fusion.16
  239.1 0.1 compare_reduce_fusion.18
  239.2 0.1 compare_reduce_fusion.20
  239.2 0.1 compare_reduce_fusion.22
  239.3 15.7 %fusion.11 = pred[1024]{0:T(1024)(128)(4,1)S(1)} fusion(pred[1024]{0:T(1024)(128)(4,1)S(1)} %get-tuple-element.42, pred[1024]{0:T(1024)(128)(4,1)S(1)} %get-tuple-element.43, pred[1024]{0:T(1024)(128)(4,1)S(1)} %get-tuple-element.44, pred[1024]{0:T(1024)(128)(4,1)S(1)} %get-tuple-element.45, pred[1024]{0:T(1024)(128)(4,1)S(1)} %get-tuple-element.46, ...), kind=kLoop, calls=%fused_computation.65 | loop fusion | flops 50176 | bytes 30824 | tf_op jit(solution)/shard_map/eq | solution.py:68
  255.0 0.0 reduce-scatter.5.cloned.1.call-done
  255.1 15.9 %all-gather.4.cloned.1.call-done = bf16[4096,256]{1,0:T(8,128)(2,1)} async-done(((bf16[1024,256]{1,0:T(8,128)(2,1)}), bf16[4096,256]{1,0:T(8,128)(2,1)}) %all-gather.4.cloned.1.call-update) | async-done | bytes 2097168 | tf_op jit(solution)/shard_map/all_gather | solution.py:73
  271.0 9.6 %fusion.20 = (f32[1024]{0:T(1024)S(1)}, f32[1024,4096]{1,0:T(8,128)}) fusion(bf16[4096,256]{1,0:T(8,128)(2,1)} %all-gather.4.cloned.1.call-done, f32[1024,128]{1,0:T(8,128)} %reduce-scatter.5.cloned.1.call-done, s32[1024]{0:T(1024)S(1)} %fusion.16, s32[4096]{0:T(1024)S(1)} %fusion.9, s32[1024]{0:T(1024)S(1)} %iota_add_fusion.1), kind=kOutput, calls=%fused_computation.78 | convolution fusion | flops 1099037696 | bytes 18378752 | tf_op jit(solution)/shard_map/rhd,shd->hrs/dot_general | solution.py:27
  280.6 0.0 copy-start.3
  280.6 8.2 %fusion.1 = f32[1024]{0:T(1024)S(1)} fusion(f32[1024,4096]{1,0:T(8,128)} %get-tuple-element.39, f32[1024]{0:T(1024)S(1)} %get-tuple-element.38), kind=kLoop, calls=%fused_computation.7 | loop fusion | flops 8387584 | bytes 16785408 | tf_op jit(solution)/shard_map/reduce_sum | solution.py:42
  288.8 0.0 copy-done.3
  288.8 7.7 %bitcast_select_fusion.1 = (bf16[1,1024,128]{1,2,0:T(8,128)(2,1)S(1)}, bf16[128,1024]{1,0:T(8,128)(2,1)S(1)}) fusion(pred[1024]{0:T(1024)(128)(4,1)S(1)} %fusion.11, f32[1024,4096]{1,0:T(8,128)} %get-tuple-element.39, f32[1024]{0:T(1024)S(1)} %fusion.1, f32[1024]{0:T(1024)S(1)} %get-tuple-element.38, bf16[4096,256]{1,0:T(8,128)(2,1)S(1)} %copy-done.3), kind=kOutput, calls=%fused_computation.15 | convolution fusion | flops 1086586880 | bytes 18359296 | tf_op jit(solution)/shard_map/hrs,shd->rhd/dot_general | solution.py:43
  296.5 0.8 collective-permute-start
  297.3 0.8 copy.9
  298.1 0.3 collective-permute-done
  298.5 0.8 copy.10
  (6 shorter events, 0.0 us)
Async XLA Ops:
  7.2 202.1 %copy-start = (s32[1,4096]{1,0:T(1,128)S(1)}, s32[1,4096]{1,0:T(1,128)}, u32[]{:S(2)}) copy-start(s32[1,4096]{1,0:T(1,128)} %param.6) | copy-start | bytes 49156
  7.2 131.4 %all-gather.6.cloned.1.call-start = ((), (), s32[]{:S(2)}) async-start(), calls=%async_computation.5 | async-start | bytes 14057472 | tf_op jit(solution)/shard_map/all_gather | solution.py:58
  7.9 193.5 %reduce-scatter.3.cloned.1.call-start = ((), (), s32[]{:S(2)}) async-start(), calls=%async_computation.2 | async-start | bytes 5242880 | tf_op jit(solution)/shard_map/reduce_scatter | solution.py:70
  149.2 2.7 copy-start.1
  151.9 51.6 %copy-start.2 = (s32[1,32]{1,0:T(1,128)S(1)}, s32[1,32]{1,0:T(1,128)}, u32[]{:S(2)}) copy-start(s32[1,32]{1,0:T(1,128)} %param.7) | copy-start | bytes 388
  154.3 100.7 %reduce-scatter.5.cloned.1.call-start = ((), (), s32[]{:S(2)}) async-start(), calls=%async_computation.4 | async-start | bytes 2621440 | tf_op jit(solution)/shard_map/reduce_scatter | solution.py:69
  157.4 113.6 %all-gather.4.cloned.1.call-start = ((), (), s32[]{:S(2)}) async-start(), calls=%async_computation.3 | async-start | bytes 2621440 | tf_op jit(solution)/shard_map/all_gather | solution.py:73
  280.6 8.2 %copy-start.3 = (bf16[4096,256]{1,0:T(8,128)(2,1)S(1)}, bf16[4096,256]{1,0:T(8,128)(2,1)}, u32[]{:S(2)}) copy-start(bf16[4096,256]{1,0:T(8,128)(2,1)} %all-gather.4.cloned.1.call-done) | copy-start | bytes 6291460
  296.5 1.9 collective-permute-start
Sparse Core Ops, SparseCore 0:
  10.6 127.9 all-gather.5
  154.4 46.9 reduce-scatter.2
  204.1 31.9 reduce-scatter.4
  237.8 33.1 all-gather.3
where the time goes:
time: 306 us
  waiting for transfers between devices  190 us (62%)
  local copies, waits for them, and re-layouts  42.2 us (14%)
  other arithmetic  31.2 us (10%)
  matrix products  27.9 us (9%)
  between operations  13.9 us (5%)
    all_gather x1, waiting for transfers between devices, local(): lax.all_gather(rows_here, 'tok', axis=0, tiled=True)  129 us
    reduce_scatter x1, waiting for transfers between devices, local(): lax.psum_scatter(key_value_part, 'mp', scatter_dimension=0, tiled=True)  43.9 us
    gather x1, local copies, waits for them, and re-layouts, attend(): key_segment = jnp.take(segment, key_pos)  23 us
    all_gather x1, waiting for transfers between devices, local(): key_value = lax.all_gather(mine, 'mp', axis=0, tiled=True)  15.9 us
    eq x1, other arithmetic, local(): alive = jnp.take(flags, my_blocks) == 0  15.7 us
    dot_general x1, matrix products, local(): jnp.dot(lax.all_gather(rows_here, 'tok', axis=0, tiled=True), flat_weight...  10.6 us
    dot_general x1, matrix products, attend(): jnp.einsum('rhd,shd->hrs', query.reshape(block_rows, heads_here, HEAD), k...  9.62 us
    reduce_sum x1, other arithmetic, attend(): probs = (expo / jnp.sum(expo, axis=-1, keepdims=True)).astype(jnp.bfloat16)  8.24 us
  transfers between devices with their start and end apart: 5, of which 4 were waited for; matrix products, arithmetic and copies ran while one was open for 19% of the time, Pallas kernels for 0%

commit v1 on v0

v1 whole, which is shorter than its diff:
```python
import functools
import math

import jax
import jax.numpy as jnp
from jax import lax
from jax.experimental import pallas as pl
from jax.experimental.pallas import tpu as pltpu
from jax.sharding import Mesh
from jax.sharding import PartitionSpec as P

HEAD = 128
BLOCK = 128
CHUNK = 512
VMEM = pl.BlockSpec(memory_space=pltpu.VMEM)
SMEM = pl.BlockSpec(memory_space=pltpu.SMEM)


def send(block, axis, distance):
    n = lax.axis_size(axis)
    return lax.ppermute(block, axis, [(i, (i + distance) % n) for i in range(n)])


def gather_ring4(part):
    half = part.shape[0] // 2
    left = send(part, "x", 1)
    right = send(part, "x", -1)
    top = send(right[:half], "x", -1)
    bottom = send(left[half:], "x", 1)
    return part, right, top, bottom, left


def project_kernel(shift_ref, rows_ref, own, right, top, bottom, left, out0, out1, out2, out3, cat):
    half = top.shape[0]

    @pl.when(pl.program_id(0) == 0)
    def _():
        for k in range(4):
            slot = lax.rem(k + 4 - shift_ref[0], 4)
            columns = slice(k * HEAD, (k + 1) * HEAD)

            @pl.when(slot == 0)
            def _():
                cat[:, columns] = own[...]

            @pl.when(slot == 1)
            def _():
                cat[:, columns] = right[...]

            @pl.when(slot == 2)
            def _():
                cat[:half, columns] = top[...]
                cat[half:, columns] = bottom[...]

            @pl.when(slot == 3)
            def _():
                cat[:, columns] = left[...]

    product = jnp.dot(rows_ref[...], cat[...], preferred_element_type=jnp.float32)
    out0[...] = product[:, :HEAD]
    for k, out in enumerate((out1, out2, out3), 1):
        out[...] = product[:, k * HEAD : (k + 1) * HEAD].astype(jnp.bfloat16)


def project(shift, rows, weights):
    total, width = rows.shape
    step = 256
    whole = lambda i: (0, 0)
    out = pl.BlockSpec((step, HEAD), lambda i: (i, 0))
    return pl.pallas_call(
        project_kernel,
        grid=(total // step,),
        in_specs=[SMEM, pl.BlockSpec((step, width), lambda i: (i, 0))]
        + [pl.BlockSpec(w.shape, whole) for w in weights],
        out_specs=[out] * 4,
        out_shape=[jax.ShapeDtypeStruct((total, HEAD), jnp.float32)]
        + [jax.ShapeDtypeStruct((total, HEAD), jnp.bfloat16)] * 3,
        scratch_shapes=[pltpu.VMEM((width, 4 * HEAD), jnp.bfloat16)],
        cost_estimate=pl.CostEstimate(
            flops=2 * total * width * 4 * HEAD, bytes_accessed=7 * 2**20, transcendentals=0
        ),
        compiler_params=pltpu.CompilerParams(vmem_limit_bytes=32 * 2**20),
    )(shift, rows, *weights)


def sum_over_y(parts):
    own, one, two, three = parts
    total = own
    for k, part in ((1, one), (3, three), (2, two)):
        total = total + send(part, "y", k).astype(jnp.float32)
    return total.astype(jnp.bfloat16)


def gather_x(block):
    return block, send(block, "x", -1), send(block, "x", -2), send(block, "x", -3)


def attend_kernel(scal_ref, flag_ref, q_ref, *refs):
    ks, vs, outs = refs[:4], refs[4:8], refs[8:12]
    kfull, vfull, scores = refs[12:]
    x = scal_ref[0]
    c1, c2, c3 = scal_ref[1], scal_ref[2], scal_ref[3]
    blocks = q_ref.shape[0] // BLOCK
    for r in range(4):
        lane = lax.rem(x + r, 4)
        for z in range(blocks):
            at = pl.ds(pl.multiple_of((4 * z + lane) * BLOCK, BLOCK), BLOCK)
            kfull[at, :] = ks[r][z * BLOCK : (z + 1) * BLOCK, :]
            vfull[at, :] = vs[r][z * BLOCK : (z + 1) * BLOCK, :]

    def first(i):
        return jnp.where(i >= c3, c3, jnp.where(i >= c2, c2, jnp.where(i >= c1, c1, 0)))

    for s in range(4):
        for t in range(2):
            z = 2 * lax.rem(x + s, 4) + t
            block = 4 * z + x
            out = outs[s]
            mine = slice(t * BLOCK, (t + 1) * BLOCK)

            @pl.when(flag_ref[block] != 0)
            def _():
                out[mine, :] = jnp.zeros((BLOCK, HEAD), jnp.bfloat16)

            @pl.when(flag_ref[block] == 0)
            def _():
                base = block * BLOCK
                low = lax.div(first(base), CHUNK)
                high = lax.div(base, CHUNK) + 1
                query = q_ref[pl.ds(pl.multiple_of(z * BLOCK, BLOCK), BLOCK), :]
                row = base + lax.broadcasted_iota(jnp.int32, (BLOCK, CHUNK), 0)
                column = lax.broadcasted_iota(jnp.int32, (BLOCK, CHUNK), 1)
                begin = first(row)

                def score(c, peak):
                    at = pl.multiple_of(c * CHUNK, CHUNK)
                    value = lax.dot_general(
                        query,
                        kfull[pl.ds(at, CHUNK), :],
                        (((1,), (1,)), ((), ())),
                        preferred_element_type=jnp.float32,
                    ) * (1.0 / math.sqrt(HEAD))
                    place = column + at
                    value = jnp.where((place <= row) & (place >= begin), value, -1e30)
                    scores[c - low] = value
                    return jnp.maximum(peak, jnp.max(value, axis=-1, keepdims=True))

                peak = lax.fori_loop(
                    low, high, score, jnp.full((BLOCK, 1), -1e30, jnp.float32)
                )

                def mix(c, carry):
                    norm, mixed = carry
                    at = pl.multiple_of(c * CHUNK, CHUNK)
                    expo = jnp.exp(scores[c - low] - peak)
                    norm = norm + jnp.sum(expo, axis=-1, keepdims=True)
                    mixed = mixed + jnp.dot(
                        expo.astype(jnp.bfloat16),
                        vfull[pl.ds(at, CHUNK), :],
                        preferred_element_type=jnp.float32,
                    )
                    return norm, mixed

                norm, mixed = lax.fori_loop(
                    low,
                    high,
                    mix,
                    (jnp.zeros((BLOCK, 1), jnp.float32), jnp.zeros((BLOCK, HEAD), jnp.float32)),
                )
                out[mine, :] = (mixed / norm).astype(jnp.bfloat16)


def attend(scalars, flags, query, keys, values):
    rows = query.shape[0]
    tokens = 4 * rows
    quarter = jax.ShapeDtypeStruct((rows // 4, HEAD), jnp.bfloat16)
    return pl.pallas_call(
        attend_kernel,
        in_specs=[SMEM, SMEM] + [VMEM] * 9,
        out_specs=[VMEM] * 4,
        out_shape=[quarter] * 4,
        scratch_shapes=[
            pltpu.VMEM((tokens, HEAD), jnp.bfloat16),
            pltpu.VMEM((tokens, HEAD), jnp.bfloat16),
            pltpu.VMEM((tokens // CHUNK, BLOCK, CHUNK), jnp.float32),
        ],
        cost_estimate=pl.CostEstimate(
            flops=2 * rows * 2048 * HEAD, bytes_accessed=3 * 2**20, transcendentals=rows * 1024
        ),
        compiler_params=pltpu.CompilerParams(vmem_limit_bytes=32 * 2**20),
    )(scalars, flags, query, *keys, *values)


def place_kernel(y_ref, *refs):
    parts, out = refs[:4], refs[4]
    for s in range(4):
        x = lax.rem(y_ref[0] + 4 - s, 4)
        for t in range(2):
            at = pl.ds(pl.multiple_of((4 * t + x) * BLOCK, BLOCK), BLOCK)
            out[at, :] = parts[s][t * BLOCK : (t + 1) * BLOCK, :]


def place(y, parts):
    rows = 4 * parts[0].shape[0]
    return pl.pallas_call(
        place_kernel,
        in_specs=[SMEM] + [VMEM] * 4,
        out_specs=VMEM,
        out_shape=jax.ShapeDtypeStruct((rows, HEAD), jnp.bfloat16),
    )(y, *parts)


def local(hidden, w_qkv, segment_ids, exit_flags):
    x, y = lax.axis_index("x"), lax.axis_index("y")
    weights = w_qkv[0]
    segment = segment_ids[0]
    bounds = [jnp.sum((segment < s).astype(jnp.int32)) for s in (1, 2, 3)]
    scalars = jnp.stack([x.astype(jnp.int32)] + bounds)
    shift = lax.rem(x - y + 4, 4).astype(jnp.int32).reshape(1)
    rows = lax.all_gather(hidden[0], "z", axis=0, tiled=True)
    sums = [
        sum_over_y(project(shift, rows, gather_ring4(weights[:, part, :]))) for part in (1, 2, 0)
    ]
    keys, values, query = sums
    mixed = attend(scalars, exit_flags[0], query, gather_x(keys), gather_x(values))
    moved = [
        lax.ppermute(
            mixed[s],
            ("x", "y"),
            [(4 * i + j, 4 * j + (i + s) % 4) for i in range(4) for j in range(4)],
        )
        for s in range(4)
    ]
    result = place(y.astype(jnp.int32).reshape(1), moved)
    handed = send(result, "phase", 1)
    return (result[None], handed[None])


def solution(mesh):
    split = Mesh(mesh.devices.reshape(2, 8, 4, 4), ("phase", "z", "x", "y"))
    tok = ("z", "x")
    in_specs = (
        P("phase", tok, "y"),
        P("phase", "y", None, tok),
        P("phase", None),
        P("phase", None),
    )
    out_specs = (P("phase", "y", tok), P("phase", "y", tok))
    return jax.shard_map(local, mesh=split, in_specs=in_specs, out_specs=out_specs, check_vma=False)
```

time: 306 us -> 170 us (0.56)
  waiting for transfers between devices: 190 us -> 68.2 us
  starting transfers between devices: 0.92 us -> 51.8 us
  local copies, waits for them, and re-layouts: 42.2 us -> 9.79 us
  other arithmetic: 31.2 us -> 2.94 us
  matrix products: 27.9 us -> 0 us
  Pallas kernels: 0 us -> 21.1 us
    all_gather x2 -> x1, waiting for transfers between devices: 145 us -> 13.9 us  [local(): rows = lax.all_gather(hidden[0], 'z', axis=0, tiled=True)]
    ppermute x1 -> x32, waiting for transfers between devices: 0.32 us -> 53.6 us  [the longest x28 47.1 us: send(): lax.ppermute(block, axis, [(i, (i + distance) % n) for i in range(n)])]
    ppermute x1 -> x32, starting transfers between devices: 0.76 us -> 51.7 us  [the longest x28 42.4 us: send(): lax.ppermute(block, axis, [(i, (i + distance) % n) for i in range(n)])]
    reduce_scatter x2 -> x0, waiting for transfers between devices: 43.9 us -> none  [the longest x1 43.9 us: local(): lax.psum_scatter(key_value_part, 'mp', scatter_dimension=0, tiled=True)]
    gather x4 -> x0, local copies, waits for them, and re-layouts: 30.6 us -> none  [the longest x1 23 us: attend(): key_segment = jnp.take(segment, key_pos)]
    dot_general x3 -> x0, matrix products: 27.9 us -> none  [the longest x1 10.6 us: local(): jnp.dot(lax.all_gather(rows_here, 'tok', axis=0, tiled=True), flat_weight...]
    pallas_call x0 -> x5, Pallas kernels: none -> 21.1 us  [the longest x3 12.2 us: project(): pl.pallas_call(project_kernel, grid=(total // step,), in_specs=[SMEM, pl....]
    eq x1 -> x0, other arithmetic: 15.7 us -> none  [local(): alive = jnp.take(flags, my_blocks) == 0]
  transfers between devices with their start and end apart: 5 -> 33, of which waited for: 4 -> 16; matrix products, arithmetic and copies ran while one was open for 19% -> 6% of each run, Pallas kernels for 0% -> 7%
where the time goes in v1:
time: 170 us; the launch traced here: 168 us
  waiting for transfers between devices  68.2 us (40%)
  starting transfers between devices  51.8 us (30%)
  Pallas kernels  21.1 us (12%)
  between operations  14.2 us (8%)
  local copies, waits for them, and re-layouts  9.79 us (6%)
  other arithmetic  2.94 us (2%)
    ppermute x28, waiting for transfers between devices, send(): lax.ppermute(block, axis, [(i, (i + distance) % n) for i in range(n)])  47.1 us
    ppermute x28, starting transfers between devices, send(): lax.ppermute(block, axis, [(i, (i + distance) % n) for i in range(n)])  42.4 us
    all_gather x1, waiting for transfers between devices, local(): rows = lax.all_gather(hidden[0], 'z', axis=0, tiled=True)  13.9 us
    pallas_call x3, Pallas kernels, project(): pl.pallas_call(project_kernel, grid=(total // step,), in_specs=[SMEM, pl....  12.2 us
    ppermute x4, starting transfers between devices, local(): lax.ppermute(mixed[s], ('x', 'y'), [(4 * i + j, 4 * j + (i + s) % 4) for...  9.35 us
    pallas_call x1, Pallas kernels, attend(): pl.pallas_call(attend_kernel, in_specs=[SMEM, SMEM] + [VMEM] * 9, out_spe...  7.22 us
    ppermute x4, waiting for transfers between devices, local(): lax.ppermute(mixed[s], ('x', 'y'), [(4 * i + j, 4 * j + (i + s) % 4) for...  6.57 us
  transfers between devices with their start and end apart: 33, of which 16 were waited for; matrix products, arithmetic and copies ran while one was open for 6% of the time, Pallas kernels for 7%

profile of v1, /device:TPU:1, one launch (start us, length us, event | category | flops | bytes accessed | tf_op | source)
XLA Modules:
  0.0 168.0 jit_solution(2021798229631960625)
XLA Ops:
  7.2 0.7 all-gather.3.cloned.1.call-update
  7.9 1.4 slice_bitcast_fusion
  9.3 3.4 %collective-permute-start.7 = (bf16[1664,128]{1,0:T(8,128)(2,1)S(1)}, bf16[1664,128]{1,0:T(8,128)(2,1)S(1)}, u32[]{:S(2)}, u32[]{:S(2)}) collective-permute-start(bf16[1664,128]{1,0:T(8,128)(2,1)S(1)} %get-tuple-element.38.own), channel_id=1, source_target_pairs={{0,12},{4,0},{8,4},{12,8},{1,13},{5,1},{9,5},{13,9},{2,14},{6,2},{... | collective-permute-start | bytes 1277960 | tf_op jit(solution)/shard_map/ppermute | solution.py:21
  12.7 2.7 %collective-permute-start = (bf16[1664,128]{1,0:T(8,128)(2,1)S(1)}, bf16[1664,128]{1,0:T(8,128)(2,1)S(1)}, u32[]{:S(2)}, u32[]{:S(2)}) collective-permute-start(bf16[1664,128]{1,0:T(8,128)(2,1)S(1)} %get-tuple-element.39.own), channel_id=1, source_target_pairs={{0,12},{4,0},{8,4},{12,8},{1,13},{5,1},{9,5},{13,9},{2,14},{6,2},{... | collective-permute-start | bytes 1277960 | tf_op jit(solution)/shard_map/ppermute | solution.py:21
  15.3 2.7 %collective-permute-start.17 = (bf16[1664,128]{1,0:T(8,128)(2,1)S(1)}, bf16[1664,128]{1,0:T(8,128)(2,1)S(1)}, u32[]{:S(2)}, u32[]{:S(2)}) collective-permute-start(bf16[1664,128]{1,0:T(8,128)(2,1)S(1)} %get-tuple-element.37.own), channel_id=1, source_target_pairs={{0,12},{4,0},{8,4},{12,8},{1,13},{5,1},{9,5},{13,9},{2,14},{6,2},{... | collective-permute-start | bytes 1277960 | tf_op jit(solution)/shard_map/ppermute | solution.py:21
  18.0 3.1 %collective-permute-done.7.right = bf16[1664,128]{1,0:T(8,128)(2,1)S(1)} collective-permute-done((bf16[1664,128]{1,0:T(8,128)(2,1)S(1)}, bf16[1664,128]{1,0:T(8,128)(2,1)S(1)}, u32[]{:S(2)}, u32[]{:S(2)}) %collective-permute-start.7) | collective-permute-done | bytes 426016 | tf_op jit(solution)/shard_map/ppermute | solution.py:21
  21.1 1.0 collective-permute-start.19
  22.2 0.7 slice.40
  22.9 1.5 collective-permute-done.9.left
  24.3 0.9 collective-permute-start.8
  25.2 1.7 slice.41
  26.9 3.4 %collective-permute-done.right = bf16[1664,128]{1,0:T(8,128)(2,1)S(1)} collective-permute-done((bf16[1664,128]{1,0:T(8,128)(2,1)S(1)}, bf16[1664,128]{1,0:T(8,128)(2,1)S(1)}, u32[]{:S(2)}, u32[]{:S(2)}) %collective-permute-start) | collective-permute-done | bytes 426016 | tf_op jit(solution)/shard_map/ppermute | solution.py:21
  30.3 1.0 collective-permute-start.10
  31.3 0.7 fusion
  32.0 0.7 slice.37
  32.7 0.7 collective-permute-done.2.left
  33.5 1.8 %collective-permute-start.1 = (bf16[832,128]{1,0:T(8,128)(2,1)}, bf16[832,128]{1,0:T(8,128)(2,1)}, u32[]{:S(2)}, u32[]{:S(2)}) collective-permute-start(bf16[832,128]{1,0:T(8,128)(2,1)} %slice.37), channel_id=1, source_target_pairs={{0,12},{4,0},{8,4},{12,8},{1,13},{5,1},{9,5},{13,9},{2,14},{6,2},{... | collective-permute-start | bytes 638984 | tf_op jit(solution)/shard_map/ppermute | solution.py:21
  35.2 0.7 slice.38
  35.9 3.5 %collective-permute-done.17.right = bf16[1664,128]{1,0:T(8,128)(2,1)S(1)} collective-permute-done((bf16[1664,128]{1,0:T(8,128)(2,1)S(1)}, bf16[1664,128]{1,0:T(8,128)(2,1)S(1)}, u32[]{:S(2)}, u32[]{:S(2)}) %collective-permute-start.17) | collective-permute-done | bytes 426016 | tf_op jit(solution)/shard_map/ppermute | solution.py:21
  39.4 1.0 collective-permute-start.3
  40.4 1.8 %pad_add_fusion.scal_ref = s32[4]{0:T(128)S(1)} fusion(s32[1]{0:T(128)} %bitcast.4, s32[1]{0:T(128)} %bitcast.3, s32[1]{0:T(128)} %bitcast.2, s32[1]{0:T(128)} %bitcast.1), kind=kLoop, calls=%fused_computation.12 | loop fusion | flops 12 | bytes 32 | tf_op jit(solution)/shard_map/stack | solution.py:218
  42.2 0.7 slice.43
  43.0 2.5 %collective-permute-start.18 = (bf16[832,128]{1,0:T(8,128)(2,1)}, bf16[832,128]{1,0:T(8,128)(2,1)}, u32[]{:S(2)}, u32[]{:S(2)}) collective-permute-start(bf16[832,128]{1,0:T(8,128)(2,1)} %slice.43), channel_id=1, source_target_pairs={{0,12},{4,0},{8,4},{12,8},{1,13},{5,1},{9,5},{13,9},{2,14},{6,2},{... | collective-permute-start | bytes 638984 | tf_op jit(solution)/shard_map/ppermute | solution.py:21
  45.4 0.7 slice.44
  46.1 1.0 collective-permute-done.10.bottom
  47.2 13.9 %all-gather.3.cloned.1.call-done = bf16[1,1024,1664]{2,1,0:T(8,128)(2,1)} async-done(((bf16[1,128,1664]{2,1,0:T(8,128)(2,1)}), bf16[1,1024,1664]{2,1,0:T(8,128)(2,1)}) %all-gather.3.cloned.1.call-update) | async-done | bytes 3407888 | tf_op jit(solution)/shard_map/all_gather | solution.py:220
  61.1 2.0 %copy-done.1 = bf16[1,1024,1664]{2,1,0:T(8,128)(2,1)S(1)} copy-done((bf16[1,1024,1664]{2,1,0:T(8,128)(2,1)S(1)}, bf16[1,1024,1664]{2,1,0:T(8,128)(2,1)}, u32[]{:S(2)}) %copy-start.1) | copy-done | bytes 3407896
  63.0 4.2 %shard_map.60 = (f32[1024,128]{1,0:T(8,128)S(1)}, bf16[1024,128]{1,0:T(8,128)(2,1)S(1)}, bf16[1024,128]{1,0:T(8,128)(2,1)S(1)}, bf16[1024,128]{1,0:T(8,128)(2,1)S(1)}) custom-call(s32[1]{0:T(128)} %bitcast.6.shift_ref, bf16[1024,1664]{1,0:T(8,128)(2,1)S(1)} %bitcast.18, bf16[1664,128]{1,0:T(8,128)(2,1)S(1)} %get-tuple-element.38.own, ...), custom_call_target="tpu_custom_call" | custom-call | flops 1744830464 | bytes 7340032 | tf_op jit(solution)/shard_map/pallas_call | solution.py:70
  67.2 2.8 %collective-permute-start.13 = (bf16[1024,128]{1,0:T(8,128)(2,1)S(1)}, bf16[1024,128]{1,0:T(8,128)(2,1)S(1)}, u32[]{:S(2)}, u32[]{:S(2)}) collective-permute-start(bf16[1024,128]{1,0:T(8,128)(2,1)S(1)} %get-tuple-element.25), channel_id=1, source_target_pairs={{0,2},{1,3},{2,0},{3,1},{4,6},{5,7},{6,4},{7,5},{8,10},{9,11},{10,... | collective-permute-start | bytes 786440 | tf_op jit(solution)/shard_map/ppermute | solution.py:21
  70.1 0.9 collective-permute-start.12
  70.9 0.6 collective-permute-start.11
  71.5 4.0 %shard_map.59 = (f32[1024,128]{1,0:T(8,128)S(1)}, bf16[1024,128]{1,0:T(8,128)(2,1)S(1)}, bf16[1024,128]{1,0:T(8,128)(2,1)S(1)}, bf16[1024,128]{1,0:T(8,128)(2,1)S(1)}) custom-call(s32[1]{0:T(128)} %bitcast.6.shift_ref, bf16[1024,1664]{1,0:T(8,128)(2,1)S(1)} %bitcast.19, bf16[1664,128]{1,0:T(8,128)(2,1)S(1)} %get-tuple-element.39.own, ...), custom_call_target="tpu_custom_call" | custom-call | flops 1744830464 | bytes 7340032 | tf_op jit(solution)/shard_map/pallas_call | solution.py:70
  75.6 0.7 collective-permute-start.6
  76.3 2.0 %collective-permute-start.5 = (bf16[1024,128]{1,0:T(8,128)(2,1)S(1)}, bf16[1024,128]{1,0:T(8,128)(2,1)S(1)}, u32[]{:S(2)}, u32[]{:S(2)}) collective-permute-start(bf16[1024,128]{1,0:T(8,128)(2,1)S(1)} %get-tuple-element.20), channel_id=1, source_target_pairs={{0,3},{1,0},{2,1},{3,2},{4,7},{5,4},{6,5},{7,6},{8,11},{9,8},{10,9... | collective-permute-start | bytes 786440 | tf_op jit(solution)/shard_map/ppermute | solution.py:21
  78.3 4.0 %shard_map.61 = (f32[1024,128]{1,0:T(8,128)S(1)}, bf16[1024,128]{1,0:T(8,128)(2,1)S(1)}, bf16[1024,128]{1,0:T(8,128)(2,1)S(1)}, bf16[1024,128]{1,0:T(8,128)(2,1)S(1)}) custom-call(s32[1]{0:T(128)} %bitcast.6.shift_ref, bf16[1024,1664]{1,0:T(8,128)(2,1)S(1)} %bitcast.20, bf16[1664,128]{1,0:T(8,128)(2,1)S(1)} %get-tuple-element.37.own, ...), custom_call_target="tpu_custom_call" | custom-call | flops 1744830464 | bytes 7340032 | tf_op jit(solution)/shard_map/pallas_call | solution.py:70
  82.4 1.8 %collective-permute-start.23 = (bf16[1024,128]{1,0:T(8,128)(2,1)S(1)}, bf16[1024,128]{1,0:T(8,128)(2,1)S(1)}, u32[]{:S(2)}, u32[]{:S(2)}) collective-permute-start(bf16[1024,128]{1,0:T(8,128)(2,1)S(1)} %get-tuple-element.29), channel_id=1, source_target_pairs={{0,2},{1,3},{2,0},{3,1},{4,6},{5,7},{6,4},{7,5},{8,10},{9,11},{10,... | collective-permute-start | bytes 786440 | tf_op jit(solution)/shard_map/ppermute | solution.py:21
  84.2 1.9 %collective-permute-start.22 = (bf16[1024,128]{1,0:T(8,128)(2,1)S(1)}, bf16[1024,128]{1,0:T(8,128)(2,1)S(1)}, u32[]{:S(2)}, u32[]{:S(2)}) collective-permute-start(bf16[1024,128]{1,0:T(8,128)(2,1)S(1)} %get-tuple-element.28), channel_id=1, source_target_pairs={{0,3},{1,0},{2,1},{3,2},{4,7},{5,4},{6,5},{7,6},{8,11},{9,8},{10,9... | collective-permute-start | bytes 786440 | tf_op jit(solution)/shard_map/ppermute | solution.py:21
  86.1 0.1 add_convert_fusion.1.refs_0_
  86.3 6.6 %collective-permute-done.23 = bf16[1024,128]{1,0:T(8,128)(2,1)S(1)} collective-permute-done((bf16[1024,128]{1,0:T(8,128)(2,1)S(1)}, bf16[1024,128]{1,0:T(8,128)(2,1)S(1)}, u32[]{:S(2)}, u32[]{:S(2)}) %collective-permute-start.23) | collective-permute-done | bytes 262176 | tf_op jit(solution)/shard_map/ppermute | solution.py:21
  92.9 6.9 %collective-permute-start.4 = (bf16[1024,128]{1,0:T(8,128)(2,1)S(1)}, bf16[1024,128]{1,0:T(8,128)(2,1)S(1)}, u32[]{:S(2)}, u32[]{:S(2)}) collective-permute-start(bf16[1024,128]{1,0:T(8,128)(2,1)S(1)} %get-tuple-element.19), channel_id=1, source_target_pairs={{0,1},{1,2},{2,3},{3,0},{4,5},{5,6},{6,7},{7,4},{8,9},{9,10},{10,1... | collective-permute-start | bytes 786440 | tf_op jit(solution)/shard_map/ppermute | solution.py:21
  99.8 4.5 %collective-permute-done.22 = bf16[1024,128]{1,0:T(8,128)(2,1)S(1)} collective-permute-done((bf16[1024,128]{1,0:T(8,128)(2,1)S(1)}, bf16[1024,128]{1,0:T(8,128)(2,1)S(1)}, u32[]{:S(2)}, u32[]{:S(2)}) %collective-permute-start.22) | collective-permute-done | bytes 262176 | tf_op jit(solution)/shard_map/ppermute | solution.py:21
  104.3 2.4 %collective-permute-start.14 = (bf16[1024,128]{1,0:T(8,128)(2,1)S(1)}, bf16[1024,128]{1,0:T(8,128)(2,1)S(1)}, u32[]{:S(2)}, u32[]{:S(2)}) collective-permute-start(bf16[1024,128]{1,0:T(8,128)(2,1)S(1)} %add_convert_fusion.1.refs_0_), channel_id=1, source_target_pairs={{0,12},{4,0},{8,4},{12,8},{1,13},{5,1},{9,5},{13,9},{2,14},{6,2},{... | collective-permute-start | bytes 786440 | tf_op jit(solution)/shard_map/ppermute | solution.py:21
  106.7 0.6 collective-permute-start.15
  107.3 0.1 add_convert_fusion.refs_4_
  107.4 0.7 collective-permute-start.16
  108.1 2.1 %collective-permute-start.24 = (bf16[1024,128]{1,0:T(8,128)(2,1)S(1)}, bf16[1024,128]{1,0:T(8,128)(2,1)S(1)}, u32[]{:S(2)}, u32[]{:S(2)}) collective-permute-start(bf16[1024,128]{1,0:T(8,128)(2,1)S(1)} %add_convert_fusion.refs_4_), channel_id=1, source_target_pairs={{0,12},{4,0},{8,4},{12,8},{1,13},{5,1},{9,5},{13,9},{2,14},{6,2},{... | collective-permute-start | bytes 786440 | tf_op jit(solution)/shard_map/ppermute | solution.py:21
  110.2 1.2 collective-permute-start.25
  111.4 0.1 collective-permute-done.14.refs_1_
  111.5 0.3 collective-permute-start.26
  111.7 0.1 add_convert_fusion.2.q_ref
  111.9 2.4 %collective-permute-done.15.refs_2_ = bf16[1024,128]{1,0:T(8,128)(2,1)S(1)} collective-permute-done((bf16[1024,128]{1,0:T(8,128)(2,1)S(1)}, bf16[1024,128]{1,0:T(8,128)(2,1)S(1)}, u32[]{:S(2)}, u32[]{:S(2)}) %collective-permute-start.15) | collective-permute-done | bytes 262176 | tf_op jit(solution)/shard_map/ppermute | solution.py:21
  114.3 10.0 %collective-permute-done.16.refs_3_ = bf16[1024,128]{1,0:T(8,128)(2,1)S(1)} collective-permute-done((bf16[1024,128]{1,0:T(8,128)(2,1)S(1)}, bf16[1024,128]{1,0:T(8,128)(2,1)S(1)}, u32[]{:S(2)}, u32[]{:S(2)}) %collective-permute-start.16) | collective-permute-done | bytes 262176 | tf_op jit(solution)/shard_map/ppermute | solution.py:21
  124.2 1.3 collective-permute-done.25.refs_6_
  125.5 7.7 %collective-permute-done.26.refs_7_ = bf16[1024,128]{1,0:T(8,128)(2,1)S(1)} collective-permute-done((bf16[1024,128]{1,0:T(8,128)(2,1)S(1)}, bf16[1024,128]{1,0:T(8,128)(2,1)S(1)}, u32[]{:S(2)}, u32[]{:S(2)}) %collective-permute-start.26) | collective-permute-done | bytes 262176 | tf_op jit(solution)/shard_map/ppermute | solution.py:21
  133.1 7.2 %shard_map.62 = (bf16[256,128]{1,0:T(8,128)(2,1)S(1)}, bf16[256,128]{1,0:T(8,128)(2,1)S(1)}, bf16[256,128]{1,0:T(8,128)(2,1)S(1)}, bf16[256,128]{1,0:T(8,128)(2,1)S(1)}) custom-call(s32[4]{0:T(128)S(1)} %pad_add_fusion.scal_ref, s32[32]{0:T(128)S(1)} %bitcast.17, bf16[1024,128]{1,0:T(8,128)(2,1)S(1)} %add_convert_fusion.2.q_ref, ...), custom_call_target="tpu_custom_call" | custom-call | flops 536870912 | bytes 3145728 | tf_op jit(solution)/shard_map/pallas_call | solution.py:177
  140.4 0.7 collective-permute-start.27
  141.1 3.4 %collective-permute-start.28 = (bf16[256,128]{1,0:T(8,128)(2,1)S(1)}, bf16[256,128]{1,0:T(8,128)(2,1)S(1)}, u32[]{:S(2)}, u32[]{:S(2)}) collective-permute-start(bf16[256,128]{1,0:T(8,128)(2,1)S(1)} %get-tuple-element.31), channel_id=1, source_target_pairs={{0,1},{1,5},{2,9},{3,13},{4,2},{5,6},{6,10},{7,14},{8,3},{9,7},{10... | collective-permute-start | bytes 196616 | tf_op jit(solution)/shard_map/ppermute | solution.py:227
  144.5 5.3 %collective-permute-start.30 = (bf16[256,128]{1,0:T(8,128)(2,1)S(1)}, bf16[256,128]{1,0:T(8,128)(2,1)S(1)}, u32[]{:S(2)}, u32[]{:S(2)}) collective-permute-start(bf16[256,128]{1,0:T(8,128)(2,1)S(1)} %get-tuple-element.33), channel_id=1, source_target_pairs={{0,3},{1,7},{2,11},{3,15},{4,0},{5,4},{6,8},{7,12},{8,1},{9,5},{10... | collective-permute-start | bytes 196616 | tf_op jit(solution)/shard_map/ppermute | solution.py:227
  149.7 6.6 %collective-permute-done.28.refs_1_ = bf16[256,128]{1,0:T(8,128)(2,1)S(1)} collective-permute-done((bf16[256,128]{1,0:T(8,128)(2,1)S(1)}, bf16[256,128]{1,0:T(8,128)(2,1)S(1)}, u32[]{:S(2)}, u32[]{:S(2)}) %collective-permute-start.28) | collective-permute-done | bytes 65568 | tf_op jit(solution)/shard_map/ppermute | solution.py:227
  156.3 0.6 copy-done.3
  157.0 1.7 shard_map.63
  158.6 0.4 collective-permute-start.31
  159.1 1.4 collective-permute-done.31
  160.5 0.7 copy.7
  (35 shorter events, 0.2 us)
Async XLA Ops:
  7.2 53.9 %all-gather.3.cloned.1.call-start = ((), (), s32[]{:S(2)}) async-start(), calls=%async_computation | async-start | bytes 3833856 | tf_op jit(solution)/shard_map/all_gather | solution.py:220
  7.9 23.4 %copy-start.6 = (s32[1,4096]{1,0:T(1,128)S(1)}, s32[1,4096]{1,0:T(1,128)}, u32[]{:S(2)}) copy-start(s32[1,4096]{1,0:T(1,128)} %param.6) | copy-start | bytes 49156
  9.3 11.9 %collective-permute-start.7 = (bf16[1664,128]{1,0:T(8,128)(2,1)S(1)}, bf16[1664,128]{1,0:T(8,128)(2,1)S(1)}, u32[]{:S(2)}, u32[]{:S(2)}) collective-permute-start(bf16[1664,128]{1,0:T(8,128)(2,1)S(1)} %get-tuple-element.38.own), channel_id=1, source_target_pairs={{0,12},{4,0},{8,4},{12,8},{1,13},{5,1},{9,5},{13,9},{2,14},{6,2},{... | collective-permute-start | bytes 1277960 | tf_op jit(solution)/shard_map/ppermute | solution.py:21
  12.6 11.7 %collective-permute-start.9 = (bf16[1664,128]{1,0:T(8,128)(2,1)S(1)}, bf16[1664,128]{1,0:T(8,128)(2,1)}, u32[]{:S(2)}, u32[]{:S(2)}) collective-permute-start(bf16[1664,128]{1,0:T(8,128)(2,1)S(1)} %get-tuple-element.38.own), channel_id=1, source_target_pairs={{0,4},{4,8},{8,12},{12,0},{1,5},{5,9},{9,13},{13,1},{2,6},{6,10},{... | collective-permute-start | bytes 1277960 | tf_op jit(solution)/shard_map/ppermute | solution.py:21
  12.7 17.6 %collective-permute-start = (bf16[1664,128]{1,0:T(8,128)(2,1)S(1)}, bf16[1664,128]{1,0:T(8,128)(2,1)S(1)}, u32[]{:S(2)}, u32[]{:S(2)}) collective-permute-start(bf16[1664,128]{1,0:T(8,128)(2,1)S(1)} %get-tuple-element.39.own), channel_id=1, source_target_pairs={{0,12},{4,0},{8,4},{12,8},{1,13},{5,1},{9,5},{13,9},{2,14},{6,2},{... | collective-permute-start | bytes 1277960 | tf_op jit(solution)/shard_map/ppermute | solution.py:21
  15.3 18.1 %collective-permute-start.2 = (bf16[1664,128]{1,0:T(8,128)(2,1)S(1)}, bf16[1664,128]{1,0:T(8,128)(2,1)S(1)}, u32[]{:S(2)}, u32[]{:S(2)}) collective-permute-start(bf16[1664,128]{1,0:T(8,128)(2,1)S(1)} %get-tuple-element.39.own), channel_id=1, source_target_pairs={{0,4},{4,8},{8,12},{12,0},{1,5},{5,9},{9,13},{13,1},{2,6},{6,10},{... | collective-permute-start | bytes 1277960 | tf_op jit(solution)/shard_map/ppermute | solution.py:21
  15.3 24.1 %collective-permute-start.17 = (bf16[1664,128]{1,0:T(8,128)(2,1)S(1)}, bf16[1664,128]{1,0:T(8,128)(2,1)S(1)}, u32[]{:S(2)}, u32[]{:S(2)}) collective-permute-start(bf16[1664,128]{1,0:T(8,128)(2,1)S(1)} %get-tuple-element.37.own), channel_id=1, source_target_pairs={{0,12},{4,0},{8,4},{12,8},{1,13},{5,1},{9,5},{13,9},{2,14},{6,2},{... | collective-permute-start | bytes 1277960 | tf_op jit(solution)/shard_map/ppermute | solution.py:21
  21.1 21.8 %collective-permute-start.19 = (bf16[1664,128]{1,0:T(8,128)(2,1)S(1)}, bf16[1664,128]{1,0:T(8,128)(2,1)S(1)}, u32[]{:S(2)}, u32[]{:S(2)}) collective-permute-start(bf16[1664,128]{1,0:T(8,128)(2,1)S(1)} %get-tuple-element.37.own), channel_id=1, source_target_pairs={{0,4},{4,8},{8,12},{12,0},{1,5},{5,9},{9,13},{13,1},{2,6},{6,10},{... | collective-permute-start | bytes 1277960 | tf_op jit(solution)/shard_map/ppermute | solution.py:21
  24.3 21.8 %collective-permute-start.8 = (bf16[832,128]{1,0:T(8,128)(2,1)}, bf16[832,128]{1,0:T(8,128)(2,1)}, u32[]{:S(2)}, u32[]{:S(2)}) collective-permute-start(bf16[832,128]{1,0:T(8,128)(2,1)} %slice.40), channel_id=1, source_target_pairs={{0,12},{4,0},{8,4},{12,8},{1,13},{5,1},{9,5},{13,9},{2,14},{6,2},{... | collective-permute-start | bytes 638984 | tf_op jit(solution)/shard_map/ppermute | solution.py:21
  30.3 16.9 %collective-permute-start.10 = (bf16[832,128]{1,0:T(8,128)(2,1)}, bf16[832,128]{1,0:T(8,128)(2,1)}, u32[]{:S(2)}, u32[]{:S(2)}) collective-permute-start(bf16[832,128]{1,0:T(8,128)(2,1)} %slice.41), channel_id=1, source_target_pairs={{0,4},{4,8},{8,12},{12,0},{1,5},{5,9},{9,13},{13,1},{2,6},{6,10},{... | collective-permute-start | bytes 638984 | tf_op jit(solution)/shard_map/ppermute | solution.py:21
  33.5 36.6 %collective-permute-start.1 = (bf16[832,128]{1,0:T(8,128)(2,1)}, bf16[832,128]{1,0:T(8,128)(2,1)}, u32[]{:S(2)}, u32[]{:S(2)}) collective-permute-start(bf16[832,128]{1,0:T(8,128)(2,1)} %slice.37), channel_id=1, source_target_pairs={{0,12},{4,0},{8,4},{12,8},{1,13},{5,1},{9,5},{13,9},{2,14},{6,2},{... | collective-permute-start | bytes 638984 | tf_op jit(solution)/shard_map/ppermute | solution.py:21
  39.4 31.5 %collective-permute-start.3 = (bf16[832,128]{1,0:T(8,128)(2,1)}, bf16[832,128]{1,0:T(8,128)(2,1)}, u32[]{:S(2)}, u32[]{:S(2)}) collective-permute-start(bf16[832,128]{1,0:T(8,128)(2,1)} %slice.38), channel_id=1, source_target_pairs={{0,4},{4,8},{8,12},{12,0},{1,5},{5,9},{9,13},{13,1},{2,6},{6,10},{... | collective-permute-start | bytes 638984 | tf_op jit(solution)/shard_map/ppermute | solution.py:21
  43.0 32.6 %collective-permute-start.18 = (bf16[832,128]{1,0:T(8,128)(2,1)}, bf16[832,128]{1,0:T(8,128)(2,1)}, u32[]{:S(2)}, u32[]{:S(2)}) collective-permute-start(bf16[832,128]{1,0:T(8,128)(2,1)} %slice.43), channel_id=1, source_target_pairs={{0,12},{4,0},{8,4},{12,8},{1,13},{5,1},{9,5},{13,9},{2,14},{6,2},{... | collective-permute-start | bytes 638984 | tf_op jit(solution)/shard_map/ppermute | solution.py:21
  46.1 30.2 %collective-permute-start.20 = (bf16[832,128]{1,0:T(8,128)(2,1)}, bf16[832,128]{1,0:T(8,128)(2,1)}, u32[]{:S(2)}, u32[]{:S(2)}) collective-permute-start(bf16[832,128]{1,0:T(8,128)(2,1)} %slice.44), channel_id=1, source_target_pairs={{0,4},{4,8},{8,12},{12,0},{1,5},{5,9},{9,13},{13,1},{2,6},{6,10},{... | collective-permute-start | bytes 638984 | tf_op jit(solution)/shard_map/ppermute | solution.py:21
  61.1 2.0 %copy-start.1 = (bf16[1,1024,1664]{2,1,0:T(8,128)(2,1)S(1)}, bf16[1,1024,1664]{2,1,0:T(8,128)(2,1)}, u32[]{:S(2)}) copy-start(bf16[1,1024,1664]{2,1,0:T(8,128)(2,1)} %all-gather.3.cloned.1.call-done) | copy-start | bytes 10223620
  67.2 15.1 %collective-permute-start.13 = (bf16[1024,128]{1,0:T(8,128)(2,1)S(1)}, bf16[1024,128]{1,0:T(8,128)(2,1)S(1)}, u32[]{:S(2)}, u32[]{:S(2)}) collective-permute-start(bf16[1024,128]{1,0:T(8,128)(2,1)S(1)} %get-tuple-element.25), channel_id=1, source_target_pairs={{0,2},{1,3},{2,0},{3,1},{4,6},{5,7},{6,4},{7,5},{8,10},{9,11},{10,... | collective-permute-start | bytes 786440 | tf_op jit(solution)/shard_map/ppermute | solution.py:21
  70.1 14.1 %collective-permute-start.12 = (bf16[1024,128]{1,0:T(8,128)(2,1)S(1)}, bf16[1024,128]{1,0:T(8,128)(2,1)S(1)}, u32[]{:S(2)}, u32[]{:S(2)}) collective-permute-start(bf16[1024,128]{1,0:T(8,128)(2,1)S(1)} %get-tuple-element.24), channel_id=1, source_target_pairs={{0,3},{1,0},{2,1},{3,2},{4,7},{5,4},{6,5},{7,6},{8,11},{9,8},{10,9... | collective-permute-start | bytes 786440 | tf_op jit(solution)/shard_map/ppermute | solution.py:21
  70.9 15.2 %collective-permute-start.11 = (bf16[1024,128]{1,0:T(8,128)(2,1)S(1)}, bf16[1024,128]{1,0:T(8,128)(2,1)S(1)}, u32[]{:S(2)}, u32[]{:S(2)}) collective-permute-start(bf16[1024,128]{1,0:T(8,128)(2,1)S(1)} %get-tuple-element.23), channel_id=1, source_target_pairs={{0,1},{1,2},{2,3},{3,0},{4,5},{5,6},{6,7},{7,4},{8,9},{9,10},{10,1... | collective-permute-start | bytes 786440 | tf_op jit(solution)/shard_map/ppermute | solution.py:21
  75.6 31.9 %collective-permute-start.6 = (bf16[1024,128]{1,0:T(8,128)(2,1)S(1)}, bf16[1024,128]{1,0:T(8,128)(2,1)S(1)}, u32[]{:S(2)}, u32[]{:S(2)}) collective-permute-start(bf16[1024,128]{1,0:T(8,128)(2,1)S(1)} %get-tuple-element.21), channel_id=1, source_target_pairs={{0,2},{1,3},{2,0},{3,1},{4,6},{5,7},{6,4},{7,5},{8,10},{9,11},{10,... | collective-permute-start | bytes 786440 | tf_op jit(solution)/shard_map/ppermute | solution.py:21
  76.3 31.8 %collective-permute-start.5 = (bf16[1024,128]{1,0:T(8,128)(2,1)S(1)}, bf16[1024,128]{1,0:T(8,128)(2,1)S(1)}, u32[]{:S(2)}, u32[]{:S(2)}) collective-permute-start(bf16[1024,128]{1,0:T(8,128)(2,1)S(1)} %get-tuple-element.20), channel_id=1, source_target_pairs={{0,3},{1,0},{2,1},{3,2},{4,7},{5,4},{6,5},{7,6},{8,11},{9,8},{10,9... | collective-permute-start | bytes 786440 | tf_op jit(solution)/shard_map/ppermute | solution.py:21
  82.4 10.5 %collective-permute-start.23 = (bf16[1024,128]{1,0:T(8,128)(2,1)S(1)}, bf16[1024,128]{1,0:T(8,128)(2,1)S(1)}, u32[]{:S(2)}, u32[]{:S(2)}) collective-permute-start(bf16[1024,128]{1,0:T(8,128)(2,1)S(1)} %get-tuple-element.29), channel_id=1, source_target_pairs={{0,2},{1,3},{2,0},{3,1},{4,6},{5,7},{6,4},{7,5},{8,10},{9,11},{10,... | collective-permute-start | bytes 786440 | tf_op jit(solution)/shard_map/ppermute | solution.py:21
  84.2 20.1 %collective-permute-start.22 = (bf16[1024,128]{1,0:T(8,128)(2,1)S(1)}, bf16[1024,128]{1,0:T(8,128)(2,1)S(1)}, u32[]{:S(2)}, u32[]{:S(2)}) collective-permute-start(bf16[1024,128]{1,0:T(8,128)(2,1)S(1)} %get-tuple-element.28), channel_id=1, source_target_pairs={{0,3},{1,0},{2,1},{3,2},{4,7},{5,4},{6,5},{7,6},{8,11},{9,8},{10,9... | collective-permute-start | bytes 786440 | tf_op jit(solution)/shard_map/ppermute | solution.py:21
  86.1 20.6 %collective-permute-start.21 = (bf16[1024,128]{1,0:T(8,128)(2,1)S(1)}, bf16[1024,128]{1,0:T(8,128)(2,1)S(1)}, u32[]{:S(2)}, u32[]{:S(2)}) collective-permute-start(bf16[1024,128]{1,0:T(8,128)(2,1)S(1)} %get-tuple-element.27), channel_id=1, source_target_pairs={{0,1},{1,2},{2,3},{3,0},{4,5},{5,6},{6,7},{7,4},{8,9},{9,10},{10,1... | collective-permute-start | bytes 786440 | tf_op jit(solution)/shard_map/ppermute | solution.py:21
  92.9 17.3 %collective-permute-start.4 = (bf16[1024,128]{1,0:T(8,128)(2,1)S(1)}, bf16[1024,128]{1,0:T(8,128)(2,1)S(1)}, u32[]{:S(2)}, u32[]{:S(2)}) collective-permute-start(bf16[1024,128]{1,0:T(8,128)(2,1)S(1)} %get-tuple-element.19), channel_id=1, source_target_pairs={{0,1},{1,2},{2,3},{3,0},{4,5},{5,6},{6,7},{7,4},{8,9},{9,10},{10,1... | collective-permute-start | bytes 786440 | tf_op jit(solution)/shard_map/ppermute | solution.py:21
  104.3 7.2 %collective-permute-start.14 = (bf16[1024,128]{1,0:T(8,128)(2,1)S(1)}, bf16[1024,128]{1,0:T(8,128)(2,1)S(1)}, u32[]{:S(2)}, u32[]{:S(2)}) collective-permute-start(bf16[1024,128]{1,0:T(8,128)(2,1)S(1)} %add_convert_fusion.1.refs_0_), channel_id=1, source_target_pairs={{0,12},{4,0},{8,4},{12,8},{1,13},{5,1},{9,5},{13,9},{2,14},{6,2},{... | collective-permute-start | bytes 786440 | tf_op jit(solution)/shard_map/ppermute | solution.py:21
  106.7 7.5 %collective-permute-start.15 = (bf16[1024,128]{1,0:T(8,128)(2,1)S(1)}, bf16[1024,128]{1,0:T(8,128)(2,1)S(1)}, u32[]{:S(2)}, u32[]{:S(2)}) collective-permute-start(bf16[1024,128]{1,0:T(8,128)(2,1)S(1)} %add_convert_fusion.1.refs_0_), channel_id=1, source_target_pairs={{0,8},{4,12},{8,0},{12,4},{1,9},{5,13},{9,1},{13,5},{2,10},{6,14},... | collective-permute-start | bytes 786440 | tf_op jit(solution)/shard_map/ppermute | solution.py:21
  107.3 25.9 %copy-start = (s32[1,32]{1,0:T(1,128)S(1)}, s32[1,32]{1,0:T(1,128)}, u32[]{:S(2)}) copy-start(s32[1,32]{1,0:T(1,128)} %param.7) | copy-start | bytes 388
  107.4 16.8 %collective-permute-start.16 = (bf16[1024,128]{1,0:T(8,128)(2,1)S(1)}, bf16[1024,128]{1,0:T(8,128)(2,1)S(1)}, u32[]{:S(2)}, u32[]{:S(2)}) collective-permute-start(bf16[1024,128]{1,0:T(8,128)(2,1)S(1)} %add_convert_fusion.1.refs_0_), channel_id=1, source_target_pairs={{0,4},{4,8},{8,12},{12,0},{1,5},{5,9},{9,13},{13,1},{2,6},{6,10},{... | collective-permute-start | bytes 786440 | tf_op jit(solution)/shard_map/ppermute | solution.py:21
  108.1 16.1 %collective-permute-start.24 = (bf16[1024,128]{1,0:T(8,128)(2,1)S(1)}, bf16[1024,128]{1,0:T(8,128)(2,1)S(1)}, u32[]{:S(2)}, u32[]{:S(2)}) collective-permute-start(bf16[1024,128]{1,0:T(8,128)(2,1)S(1)} %add_convert_fusion.refs_4_), channel_id=1, source_target_pairs={{0,12},{4,0},{8,4},{12,8},{1,13},{5,1},{9,5},{13,9},{2,14},{6,2},{... | collective-permute-start | bytes 786440 | tf_op jit(solution)/shard_map/ppermute | solution.py:21
  110.2 15.3 %collective-permute-start.25 = (bf16[1024,128]{1,0:T(8,128)(2,1)S(1)}, bf16[1024,128]{1,0:T(8,128)(2,1)S(1)}, u32[]{:S(2)}, u32[]{:S(2)}) collective-permute-start(bf16[1024,128]{1,0:T(8,128)(2,1)S(1)} %add_convert_fusion.refs_4_), channel_id=1, source_target_pairs={{0,8},{4,12},{8,0},{12,4},{1,9},{5,13},{9,1},{13,5},{2,10},{6,14},... | collective-permute-start | bytes 786440 | tf_op jit(solution)/shard_map/ppermute | solution.py:21
  111.5 21.7 %collective-permute-start.26 = (bf16[1024,128]{1,0:T(8,128)(2,1)S(1)}, bf16[1024,128]{1,0:T(8,128)(2,1)S(1)}, u32[]{:S(2)}, u32[]{:S(2)}) collective-permute-start(bf16[1024,128]{1,0:T(8,128)(2,1)S(1)} %add_convert_fusion.refs_4_), channel_id=1, source_target_pairs={{0,4},{4,8},{8,12},{12,0},{1,5},{5,9},{9,13},{13,1},{2,6},{6,10},{... | collective-permute-start | bytes 786440 | tf_op jit(solution)/shard_map/ppermute | solution.py:21
  140.4 9.4 %collective-permute-start.27 = (bf16[256,128]{1,0:T(8,128)(2,1)S(1)}, bf16[256,128]{1,0:T(8,128)(2,1)S(1)}, u32[]{:S(2)}, u32[]{:S(2)}) collective-permute-start(bf16[256,128]{1,0:T(8,128)(2,1)S(1)} %get-tuple-element.30), channel_id=1, source_target_pairs={{0,0},{1,4},{2,8},{3,12},{4,1},{5,5},{6,9},{7,13},{8,2},{9,6},{10,... | collective-permute-start | bytes 196616 | tf_op jit(solution)/shard_map/ppermute | solution.py:227
  141.1 15.3 %collective-permute-start.28 = (bf16[256,128]{1,0:T(8,128)(2,1)S(1)}, bf16[256,128]{1,0:T(8,128)(2,1)S(1)}, u32[]{:S(2)}, u32[]{:S(2)}) collective-permute-start(bf16[256,128]{1,0:T(8,128)(2,1)S(1)} %get-tuple-element.31), channel_id=1, source_target_pairs={{0,1},{1,5},{2,9},{3,13},{4,2},{5,6},{6,10},{7,14},{8,3},{9,7},{10... | collective-permute-start | bytes 196616 | tf_op jit(solution)/shard_map/ppermute | solution.py:227
  144.5 11.8 %collective-permute-start.29 = (bf16[256,128]{1,0:T(8,128)(2,1)S(1)}, bf16[256,128]{1,0:T(8,128)(2,1)S(1)}, u32[]{:S(2)}, u32[]{:S(2)}) collective-permute-start(bf16[256,128]{1,0:T(8,128)(2,1)S(1)} %get-tuple-element.32), channel_id=1, source_target_pairs={{0,2},{1,6},{2,10},{3,14},{4,3},{5,7},{6,11},{7,15},{8,0},{9,4},{1... | collective-permute-start | bytes 196616 | tf_op jit(solution)/shard_map/ppermute | solution.py:227
  144.5 11.8 %collective-permute-start.30 = (bf16[256,128]{1,0:T(8,128)(2,1)S(1)}, bf16[256,128]{1,0:T(8,128)(2,1)S(1)}, u32[]{:S(2)}, u32[]{:S(2)}) collective-permute-start(bf16[256,128]{1,0:T(8,128)(2,1)S(1)} %get-tuple-element.33), channel_id=1, source_target_pairs={{0,3},{1,7},{2,11},{3,15},{4,0},{5,4},{6,8},{7,12},{8,1},{9,5},{10... | collective-permute-start | bytes 196616 | tf_op jit(solution)/shard_map/ppermute | solution.py:227
  149.7 6.6 %copy-start.2 = (bf16[256,128]{1,0:T(8,128)(2,1)}, bf16[256,128]{1,0:T(8,128)(2,1)S(1)}, u32[]{:S(2)}) copy-start(bf16[256,128]{1,0:T(8,128)(2,1)S(1)} %collective-permute-done.27.refs_0_) | copy-start | bytes 196612
  156.3 0.6 copy-start.3
  156.3 0.6 copy-start.4
  156.3 0.7 copy-start.5
  158.6 1.8 %collective-permute-start.31 = (bf16[1024,128]{1,0:T(8,128)(2,1)}, bf16[1024,128]{1,0:T(8,128)(2,1)S(1)}, u32[]{:S(2)}, u32[]{:S(2)}) collective-permute-start(bf16[1024,128]{1,0:T(8,128)(2,1)} %shard_map.63), channel_id=1, source_target_pairs={{0,128},{128,0},{1,129},{129,1},{2,130},{130,2},{3,131},{131,3},{4... | collective-permute-start | bytes 786440 | tf_op jit(solution)/shard_map/ppermute | solution.py:21
Sparse Core Ops, SparseCore 0:
  9.8 51.2 all-gather.2

commit v2 on v0

v2 whole, which is shorter than its diff:
```python
import functools
import math

import jax
import jax.numpy as jnp
from jax import lax
from jax.experimental import pallas as pl
from jax.experimental.pallas import tpu as pltpu
from jax.sharding import Mesh
from jax.sharding import PartitionSpec as P

HEAD = 128
BLOCK = 128
SPAN = 256
LONGEST = 9
EARLY = (0, 1, 2, 6, 7)
LATE = (3, 4, 5)
CUT = 896
BRIEF = pl.CostEstimate(flops=1, bytes_accessed=1, transcendentals=0)
LONG = pl.CostEstimate(flops=3 * 10**10, bytes_accessed=1, transcendentals=0)
VMEM = pl.BlockSpec(memory_space=pltpu.VMEM)
FAR = pl.BlockSpec(memory_space=pltpu.HBM)
SMEM = pl.BlockSpec(memory_space=pltpu.SMEM)
LIMIT = pltpu.CompilerParams(vmem_limit_bytes=32 * 2**20)


def send(block, axis, distance):
    n = lax.axis_size(axis)
    return lax.ppermute(block, axis, [(i, (i + distance) % n) for i in range(n)])


def after(values, *earlier):
    return lax.optimization_barrier((values, earlier))[0]


def gather_x_ring(part, earlier, second):
    left = send(part, "x", 1)
    right = send(part, "x", -1)
    top = send(after(right, earlier)[:CUT], "x", -1)
    bottom = send(after(left, second)[CUT:], "x", 1)
    return {0: (part,), 1: (right,), 3: (left,), 2: (top, bottom)}


def gather_x_by_right(block, *earlier):
    right = send(block, "x", -1)
    return block, right, send(after(right, earlier), "x", -1), send(block, "x", 1)


def gather_z_ring(block):
    found = {0: [block]}
    left = right = block
    for step in (1, 2, 3):
        left, right = send(left, "z", 1), send(right, "z", -1)
        found[8 - step], found[step] = [left], [right]
    found[4] = [send(left, "z", 1)]
    return found


def fill_rows(pieces, rows):
    at = 0
    for piece in pieces:
        rows[at : at + piece.shape[0], :] = piece[...]
        at += piece.shape[0]


def product_of(rows, weights):
    total, at = None, 0
    for weight in weights:
        width = weight.shape[0]
        term = jnp.dot(
            rows[:, at : at + width], weight[...], preferred_element_type=jnp.float32
        )
        total = term if total is None else total + term
        at += width
    return total


def cut_by(counts, refs):
    groups, at = [], 0
    for count in counts:
        groups.append(refs[at : at + count])
        at += count
    return groups


def store_for(outs, shift, slot, product):
    target = lax.rem(slot + shift, 4)
    if len(outs) == 1:
        outs[0][target] = product.astype(outs[0].dtype)
        return
    for k in range(4):

        @pl.when(target == k)
        def _():
            outs[k][...] = product.astype(outs[k].dtype)


def project_kernel(shift_ref, *refs, pieces, slots, counts):
    total = sum(counts)
    weights = cut_by(counts, refs[pieces : pieces + total])
    outs = refs[pieces + total : -1]
    rows = refs[-1]
    fill_rows(refs[:pieces], rows)
    if len(outs) == 2:
        outs[1][...] = jnp.zeros_like(outs[1])
        outs = outs[:1]
    for slot, weight in zip(slots, weights):
        store_for(outs, shift_ref[0], slot, product_of(rows, weight))


def project_rest_kernel(x_ref, *refs, pieces, slot):
    weights = refs[pieces : pieces + 2]
    out = refs[pieces + 3]
    rows, result, sem = refs[pieces + 4 :]
    fill_rows(refs[:pieces], rows)
    result[...] = product_of(rows, weights).astype(result.dtype)
    copy = pltpu.make_async_copy(result, out.at[lax.rem(slot + x_ref[0], 4)], sem)
    copy.start()
    copy.wait()


def project_far_kernel(shift_ref, *refs, pieces, slots, counts, columns):
    total = sum(counts)
    outs = refs[pieces + total : -3]
    rows, wide, sems = refs[-3:]
    loads, at = [], 0
    for i, piece in enumerate(refs[:pieces]):
        place = rows.at[pl.ds(at, piece.shape[0])]
        loads.append(pltpu.make_async_copy(piece, place, sems.at[i]))
        at += piece.shape[0]
    weight_loads, number = [], pieces
    for i, weights in enumerate(cut_by(counts, refs[pieces : pieces + total])):
        begin, at = i * columns, 0
        for weight in weights:
            place = wide.at[
                begin // 256, pl.ds(at, weight.shape[0]), pl.ds(begin % 256, columns)
            ]
            weight_loads.append((i, pltpu.make_async_copy(weight, place, sems.at[number])))
            at += weight.shape[0]
            number += 1
    for copy in loads:
        copy.start()
    for _, copy in weight_loads:
        copy.start()
    for copy in loads:
        copy.wait()
    for tile in range(4 * columns // 256):
        inside = [i for i in range(4) if i * columns // 256 == tile]
        for i, copy in weight_loads:
            if i in inside:
                copy.wait()
        product = jnp.dot(rows[...], wide[tile], preferred_element_type=jnp.float32)
        for i in inside:
            begin = i * columns % 256
            store_for(outs, shift_ref[0], slots[i], product[:, begin : begin + columns])


def project_far(columns, shift, pieces, parts_of, slots, stacked=False):
    weights = [part for slot in slots for part in parts_of[slot]]
    counts = tuple(len(parts_of[slot]) for slot in slots)
    count = sum(piece.shape[0] for piece in pieces)
    width = pieces[0].shape[1]
    return pl.pallas_call(
        functools.partial(
            project_far_kernel, pieces=len(pieces), slots=slots, counts=counts, columns=columns
        ),
        in_specs=[SMEM] + [FAR] * (len(pieces) + len(weights)),
        out_specs=[VMEM] * (1 if stacked else 4),
        out_shape=[jax.ShapeDtypeStruct((4, count, columns), jnp.bfloat16)]
        if stacked
        else [jax.ShapeDtypeStruct((count, columns), jnp.bfloat16)] * 4,
        scratch_shapes=[
            pltpu.VMEM((count, width), jnp.bfloat16),
            pltpu.VMEM((4 * columns // 256, width, 256), jnp.bfloat16),
            pltpu.SemaphoreType.DMA((len(pieces) + len(weights),)),
        ],
        cost_estimate=LONG,
        compiler_params=LIMIT,
    )(shift, *pieces, *weights)


def project(kernel, columns, shift, pieces, parts_of, slots, stacked=False, mark=False):
    weights = [part for slot in slots for part in parts_of[slot]]
    counts = tuple(len(parts_of[slot]) for slot in slots)
    count = sum(piece.shape[0] for piece in pieces)
    width = pieces[0].shape[1]
    scratch = [pltpu.VMEM((count, width), jnp.bfloat16)]
    return pl.pallas_call(
        functools.partial(kernel, pieces=len(pieces), slots=slots, counts=counts),
        in_specs=[SMEM] + [VMEM] * (len(pieces) + len(weights)),
        out_specs=[VMEM] * (1 + mark if stacked else 4),
        out_shape=[
            jax.ShapeDtypeStruct((4, count, columns), jnp.bfloat16),
            jax.ShapeDtypeStruct((8, HEAD), jnp.float32),
        ][: 1 + mark]
        if stacked
        else [jax.ShapeDtypeStruct((count, columns), jnp.bfloat16)] * 4,
        scratch_shapes=scratch,
        cost_estimate=BRIEF if mark else LONG,
        compiler_params=LIMIT,
    )(shift, *pieces, *weights)


def project_rest(x, pieces, halves, slot, stack):
    _, count, columns = stack.shape
    width = pieces[0].shape[1]
    return pl.pallas_call(
        functools.partial(project_rest_kernel, pieces=len(pieces), slot=slot),
        in_specs=[SMEM] + [VMEM] * (len(pieces) + 2) + [FAR],
        out_specs=FAR,
        out_shape=jax.ShapeDtypeStruct(stack.shape, stack.dtype),
        input_output_aliases={3 + len(pieces): 0},
        scratch_shapes=[
            pltpu.VMEM((count, width), jnp.bfloat16),
            pltpu.VMEM((count, columns), jnp.bfloat16),
            pltpu.SemaphoreType.DMA,
        ],
        cost_estimate=LONG,
        compiler_params=LIMIT,
    )(x, *pieces, *halves[slot], stack)


def exchange(stack, axis):
    return lax.all_to_all(stack, axis, 0, 0, tiled=True)


def sum_of(stack):
    return jnp.sum(stack.astype(jnp.float32), axis=0).astype(jnp.bfloat16)


def sum_over_y(parts):
    own, one, two, three = parts
    total = own.astype(jnp.float32)
    for k, part in ((1, one), (3, three), (2, two)):
        total = total + send(part, "y", k).astype(jnp.float32)
    return total.astype(jnp.bfloat16)


def gather_x(block):
    return block, send(block, "x", -1), send(block, "x", -2), send(block, "x", -3)


def attend_kernel(x_ref, z_ref, bound_ref, flag_ref, q_ref, *refs):
    early, late, out = refs[:4], refs[4:8], refs[8]
    kfull, vfull = refs[9:]
    x, z = x_ref[0], z_ref[0]
    c1, c2, c3 = bound_ref[0], bound_ref[1], bound_ref[2]
    for r in range(4):
        lane = lax.rem(x + r, 4)
        for group, offsets in ((early[r], EARLY), (late[r], LATE)):
            for i, offset in enumerate(offsets):
                place = 4 * lax.rem(z + offset, 8) + lane
                at = pl.ds(pl.multiple_of(place * BLOCK, BLOCK), BLOCK)
                kfull[at, :] = group[i * BLOCK : (i + 1) * BLOCK, :HEAD]
                vfull[at, :] = group[i * BLOCK : (i + 1) * BLOCK, HEAD:]

    def first(i):
        return jnp.where(i >= c3, c3, jnp.where(i >= c2, c2, jnp.where(i >= c1, c1, 0)))

    def one_block(index, carry):
        there = 2 * lax.rem(x + lax.div(index, 2), 4) + lax.rem(index, 2)
        base = (4 * there + x) * BLOCK
        mine = pl.ds(pl.multiple_of(index * BLOCK, BLOCK), BLOCK)
        spans = lax.div(base + BLOCK - first(base) + SPAN - 1, SPAN)
        alive = flag_ref[4 * there + x] == 0

        @pl.when(jnp.logical_not(alive))
        def _():
            out[mine, :] = jnp.zeros((BLOCK, HEAD), jnp.bfloat16)

        for n in range(1, LONGEST + 1):

            @pl.when(alive & (spans == n))
            def _():
                keys = n * SPAN
                low = jnp.maximum(base + BLOCK - keys, 0)
                window = pl.ds(pl.multiple_of(low, BLOCK), keys)
                q_at = lax.rem(there - z + 8, 8) * BLOCK
                query = q_ref[pl.ds(pl.multiple_of(q_at, BLOCK), BLOCK), :]
                score = lax.dot_general(
                    query,
                    kfull[window, :],
                    (((1,), (1,)), ((), ())),
                    preferred_element_type=jnp.float32,
                ) * (1.0 / math.sqrt(HEAD))
                row = base + lax.broadcasted_iota(jnp.int32, (BLOCK, 1), 0)
                begin = first(row)
                column = low + lax.broadcasted_iota(jnp.int32, (BLOCK, keys), 1)
                score = jnp.where((column <= row) & (column >= begin), score, -1e30)
                expo = jnp.exp(score - jnp.max(score, axis=-1, keepdims=True))
                norm = jnp.sum(expo, axis=-1, keepdims=True)
                mixed = jnp.dot(
                    expo.astype(jnp.bfloat16), vfull[window, :], preferred_element_type=jnp.float32
                )
                out[mine, :] = (mixed / norm).astype(jnp.bfloat16)

        return carry

    lax.fori_loop(0, 8, one_block, 0)


def attend(x, z, bounds, flags, query, early, late):
    rows = query.shape[0]
    return pl.pallas_call(
        attend_kernel,
        in_specs=[SMEM] * 4 + [VMEM] * 9,
        out_specs=VMEM,
        out_shape=jax.ShapeDtypeStruct((rows, HEAD), jnp.bfloat16),
        scratch_shapes=[pltpu.VMEM((4 * rows, HEAD), jnp.bfloat16)] * 2,
        cost_estimate=BRIEF,
        compiler_params=LIMIT,
    )(x, z, bounds, flags, query, *early, *late)


def place_kernel(y_ref, *refs):
    parts, out = refs[:4], refs[4]
    for s in range(4):
        x = lax.rem(y_ref[0] + 4 - s, 4)
        for t in range(2):
            at = pl.ds(pl.multiple_of((4 * t + x) * BLOCK, BLOCK), BLOCK)
            out[at, :] = parts[s][t * BLOCK : (t + 1) * BLOCK, :]


def place(y, parts):
    rows = 4 * parts[0].shape[0]
    return pl.pallas_call(
        place_kernel,
        in_specs=[SMEM] + [VMEM] * 4,
        out_specs=VMEM,
        out_shape=jax.ShapeDtypeStruct((rows, HEAD), jnp.bfloat16),
    )(y, *parts)


def local(hidden, w_qkv, segment_ids, exit_flags):
    x, y, z = (lax.axis_index(axis).astype(jnp.int32) for axis in ("x", "y", "z"))
    weights = w_qkv[0]
    segment = segment_ids[0]
    steps = jnp.arange(1, 4, dtype=jnp.int32)
    bounds = jnp.sum((segment[None, :] < steps[:, None]).astype(jnp.int32), axis=1)
    x, y, z = (index.reshape(1) for index in (x, y, z))
    shift = lax.rem(x - y + 4, 4)
    blocks = gather_z_ring(hidden[0])
    key_value = jnp.concatenate([weights[:, 1, :], weights[:, 2, :]], axis=1)
    kv_w = gather_x_ring(key_value, (bounds, shift), (blocks[2], blocks[6]))

    def pieces(offsets):
        return [piece for offset in offsets for piece in blocks[offset]]

    near = pieces(EARLY)
    stack, mark = project(project_kernel, 256, x, near, kv_w, (0, 1, 3), True, True)
    near = after(near, blocks[3], blocks[5])
    stack = project_rest(x, near, kv_w, 2, stack)
    own = after(weights[:, 0, :], mark, kv_w[2])
    q_w = [(part,) for part in gather_x_by_right(own, stack)]
    received = exchange(stack, "y")
    late_pieces = after(pieces(LATE), stack)
    late_parts = project_far(256, shift, late_pieces, kv_w, (0, 1, 3, 2))
    late = sum_over_y(late_parts)
    early = sum_of(received)
    q_w = after(q_w, late_parts[0], early)
    early = gather_x_by_right(early)
    (stack,) = project_far(128, x, pieces(range(8)), q_w, (0, 1, 3, 2), True)
    query = sum_of(exchange(after(stack, late, early[1], early[3]), "y"))
    mixed = attend(x, z, bounds, exit_flags[0], query, early, gather_x(late))
    quarter = mixed.shape[0] // 4
    moved = [
        lax.ppermute(
            mixed[s * quarter : (s + 1) * quarter],
            ("x", "y"),
            [(4 * i + j, 4 * j + (i + s) % 4) for i in range(4) for j in range(4)],
        )
        for s in range(4)
    ]
    result = place(y, moved)
    handed = send(result, "phase", 1)
    return (result[None], handed[None])


def solution(mesh):
    split = Mesh(mesh.devices.reshape(2, 8, 4, 4), ("phase", "z", "x", "y"))
    tok = ("z", "x")
    in_specs = (
        P("phase", tok, "y"),
        P("phase", "y", None, tok),
        P("phase", None),
        P("phase", None),
    )
    out_specs = (P("phase", "y", tok), P("phase", "y", tok))
    return jax.shard_map(local, mesh=split, in_specs=in_specs, out_specs=out_specs, check_vma=False)
```

time: 306 us -> 135 us (0.44)
  waiting for transfers between devices: 190 us -> 38.5 us
  starting transfers between devices: 0.92 us -> 58.6 us
  local copies, waits for them, and re-layouts: 42.2 us -> 9.19 us
  matrix products: 27.9 us -> 0 us
  other arithmetic: 31.2 us -> 3.56 us
  Pallas kernels: 0 us -> 23.4 us
  between operations: 13.9 us -> 0.9 us
    all_gather x2 -> x0, waiting for transfers between devices: 145 us -> none  [the longest x1 129 us: local(): lax.all_gather(rows_here, 'tok', axis=0, tiled=True)]
    ppermute x1 -> x28, starting transfers between devices: 0.76 us -> 49.9 us  [the longest x24 36.7 us: send(): lax.ppermute(block, axis, [(i, (i + distance) % n) for i in range(n)])]
    reduce_scatter x2 -> x0, waiting for transfers between devices: 43.9 us -> none  [the longest x1 43.9 us: local(): lax.psum_scatter(key_value_part, 'mp', scatter_dimension=0, tiled=True)]
    ppermute x1 -> x28, waiting for transfers between devices: 0.32 us -> 31.7 us  [the longest x24 27.9 us: send(): lax.ppermute(block, axis, [(i, (i + distance) % n) for i in range(n)])]
    gather x4 -> x0, local copies, waits for them, and re-layouts: 30.6 us -> none  [the longest x1 23 us: attend(): key_segment = jnp.take(segment, key_pos)]
    dot_general x3 -> x0, matrix products: 27.9 us -> none  [the longest x1 10.6 us: local(): jnp.dot(lax.all_gather(rows_here, 'tok', axis=0, tiled=True), flat_weight...]
    pallas_call x0 -> x6, Pallas kernels: none -> 23.4 us  [the longest x2 12.2 us: project_far(): pl.pallas_call(functools.partial(project_far_kernel, pieces=len(pieces),...]
    eq x1 -> x0, other arithmetic: 15.7 us -> none  [local(): alive = jnp.take(flags, my_blocks) == 0]
  transfers between devices with their start and end apart: 5 -> 30, of which waited for: 4 -> 9; matrix products, arithmetic and copies ran while one was open for 19% -> 3% of each run, Pallas kernels for 0% -> 14%
where the time goes in v2:
time: 135 us; the launch traced here: 134 us
  starting transfers between devices  58.6 us (43%)
  waiting for transfers between devices  38.5 us (29%)
  Pallas kernels  23.4 us (17%)
  local copies, waits for them, and re-layouts  9.19 us (7%)
  other arithmetic  3.56 us (3%)
    ppermute x24, starting transfers between devices, send(): lax.ppermute(block, axis, [(i, (i + distance) % n) for i in range(n)])  36.7 us
    ppermute x24, waiting for transfers between devices, send(): lax.ppermute(block, axis, [(i, (i + distance) % n) for i in range(n)])  27.9 us
    ppermute x4, starting transfers between devices, local(): lax.ppermute(mixed[s * quarter:(s + 1) * quarter], ('x', 'y'), [(4 * i +...  13.2 us
    pallas_call x2, Pallas kernels, project_far(): pl.pallas_call(functools.partial(project_far_kernel, pieces=len(pieces),...  12.2 us
    all_to_all x2, starting transfers between devices, exchange(): return lax.all_to_all(stack, axis, 0, 0, tiled=True)  8.75 us
    unnamed x31, local copies, waits for them, and re-layouts  7.76 us
    all_to_all x2, waiting for transfers between devices, exchange(): return lax.all_to_all(stack, axis, 0, 0, tiled=True)  6.85 us
    pallas_call x1, Pallas kernels, project(): pl.pallas_call(functools.partial(kernel, pieces=len(pieces), slots=slots,...  3.86 us
  transfers between devices with their start and end apart: 30, of which 9 were waited for; matrix products, arithmetic and copies ran while one was open for 3% of the time, Pallas kernels for 14%

profile of v2, /device:TPU:1, one launch (start us, length us, event | category | flops | bytes accessed | tf_op | source)
XLA Modules:
  0.0 134.2 jit_solution(10620286622035305398)
XLA Ops:
  0.6 1.3 %slice_bitcast_fusion.1 = (bf16[1664,128]{1,0:T(8,128)(2,1)S(1)}, bf16[1664,128]{1,0:T(8,128)(2,1)S(1)}, bf16[1664,128]{1,0:T(8,128)(2,1)S(1)}) fusion(bf16[1664,3,128]{2,0,1:T(8,128)(2,1)} %bitcast.21), kind=kLoop, calls=%fused_computation.2 | loop fusion | bytes 2555904 | tf_op jit(solution)/shard_map/squeeze | solution.py:343
  2.0 0.0 copy-start.1
  2.0 0.0 copy-start.14
  2.0 0.1 pad_maximum_fusion.refs_5_.refs_3_
  2.1 3.4 %collective-permute-start.7 = (bf16[1664,256]{1,0:T(8,128)(2,1)S(1)}, bf16[1664,256]{1,0:T(8,128)(2,1)S(1)}, u32[]{:S(2)}, u32[]{:S(2)}) collective-permute-start(bf16[1664,256]{1,0:T(8,128)(2,1)S(1)} %pad_maximum_fusion.refs_5_.refs_3_), channel_id=1, source_target_pairs={{0,12},{4,0},{8,4},{12,8},{1,13},{5,1},{9,5},{13,9},{2,14},{6,2},{... | collective-permute-start | bytes 2555912 | tf_op jit(solution)/shard_map/ppermute | solution.py:29
  5.5 1.6 %collective-permute-start.3 = (bf16[128,1664]{1,0:T(8,128)(2,1)S(1)}, bf16[128,1664]{1,0:T(8,128)(2,1)}, u32[]{:S(2)}, u32[]{:S(2)}) collective-permute-start(bf16[128,1664]{1,0:T(8,128)(2,1)S(1)} %bitcast.15), channel_id=1, source_target_pairs={{0,16},{16,32},{32,48},{48,64},{64,80},{80,96},{96,112},{112,0},{1... | collective-permute-start | bytes 1277960 | tf_op jit(solution)/shard_map/ppermute | solution.py:29
  7.1 3.9 %collective-permute-start = (bf16[128,1664]{1,0:T(8,128)(2,1)S(1)}, bf16[128,1664]{1,0:T(8,128)(2,1)}, u32[]{:S(2)}, u32[]{:S(2)}) collective-permute-start(bf16[128,1664]{1,0:T(8,128)(2,1)S(1)} %bitcast.16), channel_id=1, source_target_pairs={{0,112},{16,0},{32,16},{48,32},{64,48},{80,64},{96,80},{112,96},{1... | collective-permute-start | bytes 1277960 | tf_op jit(solution)/shard_map/ppermute | solution.py:29
  11.1 9.3 %collective-permute-done.3.refs_4_.refs_7_ = bf16[128,1664]{1,0:T(8,128)(2,1)} collective-permute-done((bf16[128,1664]{1,0:T(8,128)(2,1)S(1)}, bf16[128,1664]{1,0:T(8,128)(2,1)}, u32[]{:S(2)}, u32[]{:S(2)}) %collective-permute-start.3) | collective-permute-done | bytes 426016 | tf_op jit(solution)/shard_map/ppermute | solution.py:29
  20.4 0.0 collective-permute-start.4
  20.4 0.0 collective-permute-done.refs_1_
  20.4 2.7 %collective-permute-start.1 = (bf16[128,1664]{1,0:T(8,128)(2,1)}, bf16[128,1664]{1,0:T(8,128)(2,1)}, u32[]{:S(2)}, u32[]{:S(2)}) collective-permute-start(bf16[128,1664]{1,0:T(8,128)(2,1)} %collective-permute-done.refs_1_), channel_id=1, source_target_pairs={{0,112},{16,0},{32,16},{48,32},{64,48},{80,64},{96,80},{112,96},{1... | collective-permute-start | bytes 1277960 | tf_op jit(solution)/shard_map/ppermute | solution.py:29
  23.1 0.2 convert_reduce_fusion.bound_ref
  23.3 3.3 %collective-permute-start.8 = (bf16[896,256]{1,0:T(8,128)(2,1)S(1)}, bf16[896,256]{1,0:T(8,128)(2,1)S(1)}, u32[]{:S(2)}, u32[]{:S(2)}) collective-permute-start(bf16[896,256]{1,0:T(8,128)(2,1)S(1)} %slice.30), channel_id=1, source_target_pairs={{0,12},{4,0},{8,4},{12,8},{1,13},{5,1},{9,5},{13,9},{2,14},{6,2},{... | collective-permute-start | bytes 1376264 | tf_op jit(solution)/shard_map/ppermute | solution.py:29
  26.6 5.1 %collective-permute-done.4.refs_3_.refs_6_ = bf16[128,1664]{1,0:T(8,128)(2,1)} collective-permute-done((bf16[128,1664]{1,0:T(8,128)(2,1)}, bf16[128,1664]{1,0:T(8,128)(2,1)}, u32[]{:S(2)}, u32[]{:S(2)}) %collective-permute-start.4) | collective-permute-done | bytes 426016 | tf_op jit(solution)/shard_map/ppermute | solution.py:29
  31.7 2.7 %collective-permute-start.2 = (bf16[128,1664]{1,0:T(8,128)(2,1)}, bf16[128,1664]{1,0:T(8,128)(2,1)S(1)}, u32[]{:S(2)}, u32[]{:S(2)}) collective-permute-start(bf16[128,1664]{1,0:T(8,128)(2,1)} %collective-permute-done.1.refs_2_), channel_id=1, source_target_pairs={{0,112},{16,0},{32,16},{48,32},{64,48},{80,64},{96,80},{112,96},{1... | collective-permute-start | bytes 1277960 | tf_op jit(solution)/shard_map/ppermute | solution.py:29
  34.4 0.0 collective-permute-done.9.refs_7_.refs_5_
  34.4 0.3 collective-permute-start.10
  34.7 3.9 %shard_map.59 = (bf16[4,640,256]{2,1,0:T(8,128)(2,1)S(1)}, f32[8,128]{1,0:T(8,128)}) custom-call(s32[1]{0:T(128)} %bitcast.1.shift_ref.x_ref, bf16[128,1664]{1,0:T(8,128)(2,1)S(1)} %bitcast.17, bf16[128,1664]{1,0:T(8,128)(2,1)} %collective-permute-done.refs_1_, bf16[128,1664]{1,0:T(8,128)(2,1)} %collective-permute-done.1.refs_2_, ...), custom_call_target="tpu_custom_call" | custom-call | flops 1 | bytes 1 | tf_op jit(solution)/shard_map/pallas_call | solution.py:188
  38.5 3.5 %collective-permute-done.5.refs_2_.refs_5_ = bf16[128,1664]{1,0:T(8,128)(2,1)} collective-permute-done((bf16[128,1664]{1,0:T(8,128)(2,1)}, bf16[128,1664]{1,0:T(8,128)(2,1)}, u32[]{:S(2)}, u32[]{:S(2)}) %collective-permute-start.5) | collective-permute-done | bytes 426016 | tf_op jit(solution)/shard_map/ppermute | solution.py:29
  42.1 0.0 collective-permute-done.2.refs_0_.refs_3_
  42.1 0.8 copy-done.5
  42.8 0.0 collective-permute-start.6
  42.8 0.5 collective-permute-done.10.refs_6_.refs_7_
  43.4 1.2 collective-permute-start.11
  44.6 2.3 %shard_map.60 = bf16[4,640,256]{2,1,0:T(8,128)(2,1)S(1)} custom-call(s32[1]{0:T(128)} %bitcast.1.shift_ref.x_ref, bf16[128,1664]{1,0:T(8,128)(2,1)S(1)} %bitcast.18, bf16[128,1664]{1,0:T(8,128)(2,1)} %collective-permute-done.refs_1_, bf16[128,1664]{1,0:T(8,128)(2,1)} %collective-permute-done.1.refs_2_, ...), custom_call_target="tpu_custom_call", output_to_operand_aliasing={{}: (8, {})} | custom-call | flops 30000001024 | bytes 1 | tf_op jit(solution)/shard_map/pallas_call | solution.py:207
  46.9 1.1 copy-done
  48.0 0.8 copy-done.3
  48.8 0.8 copy-done.8
  49.5 4.5 %all-to-all-start = ((bf16[4,640,256]{2,1,0:T(8,128)(2,1)}), bf16[4,640,256]{2,1,0:T(8,128)(2,1)}, u32[]{:S(2)}, u32[]{:S(2)}) async-start(bf16[4,640,256]{2,1,0:T(8,128)(2,1)} %copy-done), calls=%async_computation | async-start | bytes 2621440 | tf_op jit(solution)/shard_map/all_to_all | solution.py:224
  54.0 1.0 copy-done.4
  55.0 1.0 copy-done.6
  56.0 1.0 copy-done.9
  57.0 4.9 %shard_map.61 = (bf16[384,256]{1,0:T(8,128)(2,1)S(1)}, bf16[384,256]{1,0:T(8,128)(2,1)S(1)}, bf16[384,256]{1,0:T(8,128)(2,1)S(1)}, bf16[384,256]{1,0:T(8,128)(2,1)S(1)}) custom-call(s32[1]{0:T(128)S(6)} %rem.18.shift_ref, bf16[128,1664]{1,0:T(8,128)(2,1)S(1)} %copy-done.6, bf16[128,1664]{1,0:T(8,128)(2,1)} %collective-permute-done.6.refs_1_.refs_4_, ...), custom_call_target="tpu_custom_call" | custom-call | flops 30000001024 | bytes 1 | tf_op jit(solution)/shard_map/pallas_call | solution.py:163
  62.0 1.3 %collective-permute-start.14 = (bf16[384,256]{1,0:T(8,128)(2,1)S(1)}, bf16[384,256]{1,0:T(8,128)(2,1)S(1)}, u32[]{:S(2)}, u32[]{:S(2)}) collective-permute-start(bf16[384,256]{1,0:T(8,128)(2,1)S(1)} %get-tuple-element.42), channel_id=1, source_target_pairs={{0,1},{1,2},{2,3},{3,0},{4,5},{5,6},{6,7},{7,4},{8,9},{9,10},{10,1... | collective-permute-start | bytes 589832 | tf_op jit(solution)/shard_map/ppermute | solution.py:29
  63.3 1.6 %collective-permute-start.15 = (bf16[384,256]{1,0:T(8,128)(2,1)S(1)}, bf16[384,256]{1,0:T(8,128)(2,1)S(1)}, u32[]{:S(2)}, u32[]{:S(2)}) collective-permute-start(bf16[384,256]{1,0:T(8,128)(2,1)S(1)} %get-tuple-element.43), channel_id=1, source_target_pairs={{0,3},{1,0},{2,1},{3,2},{4,7},{5,4},{6,5},{7,6},{8,11},{9,8},{10,9... | collective-permute-start | bytes 589832 | tf_op jit(solution)/shard_map/ppermute | solution.py:29
  64.9 1.6 %collective-permute-start.16 = (bf16[384,256]{1,0:T(8,128)(2,1)S(1)}, bf16[384,256]{1,0:T(8,128)(2,1)S(1)}, u32[]{:S(2)}, u32[]{:S(2)}) collective-permute-start(bf16[384,256]{1,0:T(8,128)(2,1)S(1)} %get-tuple-element.44), channel_id=1, source_target_pairs={{0,2},{1,3},{2,0},{3,1},{4,6},{5,7},{6,4},{7,5},{8,10},{9,11},{10,... | collective-permute-start | bytes 589832 | tf_op jit(solution)/shard_map/ppermute | solution.py:29
  66.4 0.3 collective-permute-start.13
  66.7 2.4 %collective-permute-start.12 = (bf16[1664,128]{1,0:T(8,128)(2,1)}, bf16[1664,128]{1,0:T(8,128)(2,1)}, u32[]{:S(2)}, u32[]{:S(2)}) collective-permute-start(bf16[1664,128]{1,0:T(8,128)(2,1)} %collective-permute-done.11.refs_9_), channel_id=1, source_target_pairs={{0,12},{4,0},{8,4},{12,8},{1,13},{5,1},{9,5},{13,9},{2,14},{6,2},{... | collective-permute-start | bytes 1277960 | tf_op jit(solution)/shard_map/ppermute | solution.py:29
  69.1 8.0 %collective-permute-done.14 = bf16[384,256]{1,0:T(8,128)(2,1)S(1)} collective-permute-done((bf16[384,256]{1,0:T(8,128)(2,1)S(1)}, bf16[384,256]{1,0:T(8,128)(2,1)S(1)}, u32[]{:S(2)}, u32[]{:S(2)}) %collective-permute-start.14) | collective-permute-done | bytes 196640 | tf_op jit(solution)/shard_map/ppermute | solution.py:29
  77.1 0.1 add_convert_fusion.refs_4_
  77.2 1.7 %reduce_sum.34.refs_0_ = bf16[640,256]{1,0:T(8,128)(2,1)S(1)} reduce(bf16[4,640,256]{2,1,0:T(8,128)(2,1)} %all-to-all-done, bf16[]{:T(256)} %constant.28.clone.1), dimensions={0}, to_apply=%region_1.0 | reduce | flops 491520 | bytes 1638402 | tf_op jit(solution)/shard_map/reduce_sum | solution.py:228
  78.9 0.7 collective-permute-start.17
  79.6 0.8 collective-permute-start.18
  80.5 7.3 %shard_map.62 = bf16[4,1024,128]{2,1,0:T(8,128)(2,1)} custom-call(s32[1]{0:T(128)} %bitcast.1.shift_ref.x_ref, bf16[128,1664]{1,0:T(8,128)(2,1)S(1)} %bitcast.19, bf16[128,1664]{1,0:T(8,128)(2,1)} %collective-permute-done.refs_1_, bf16[128,1664]{1,0:T(8,128)(2,1)} %collective-permute-done.1.refs_2_, bf16[128,1664]{1,0:T(8,128)(2,1)S(1)} %copy-done.7, ...), custom_call_target="tpu_custom_call" | custom-call | flops 30000001024 | bytes 1 | tf_op jit(solution)/shard_map/pallas_call | solution.py:163
  87.7 0.0 copy-start.2
  87.8 4.3 %all-to-all-start.1 = ((bf16[4,1024,128]{2,1,0:T(8,128)(2,1)}), bf16[4,1024,128]{2,1,0:T(8,128)(2,1)}, u32[]{:S(2)}, u32[]{:S(2)}) async-start(bf16[4,1024,128]{2,1,0:T(8,128)(2,1)} %shard_map.62), calls=%async_computation.1 | async-start | bytes 2097152 | tf_op jit(solution)/shard_map/all_to_all | solution.py:224
  92.0 1.9 %collective-permute-start.19 = (bf16[640,256]{1,0:T(8,128)(2,1)S(1)}, bf16[640,256]{1,0:T(8,128)(2,1)S(1)}, u32[]{:S(2)}, u32[]{:S(2)}) collective-permute-start(bf16[640,256]{1,0:T(8,128)(2,1)S(1)} %collective-permute-done.17.refs_1_), channel_id=1, source_target_pairs={{0,12},{4,0},{8,4},{12,8},{1,13},{5,1},{9,5},{13,9},{2,14},{6,2},{... | collective-permute-start | bytes 983048 | tf_op jit(solution)/shard_map/ppermute | solution.py:29
  94.0 0.1 collective-permute-start.20
  94.1 1.3 collective-permute-start.21
  95.4 0.1 collective-permute-start.22
  95.4 6.8 %all-to-all-done.1 = bf16[4,1024,128]{2,1,0:T(8,128)(2,1)} async-done(((bf16[4,1024,128]{2,1,0:T(8,128)(2,1)}), bf16[4,1024,128]{2,1,0:T(8,128)(2,1)}, u32[]{:S(2)}, u32[]{:S(2)}) %all-to-all-start.1) | async-done | bytes 1048608 | tf_op jit(solution)/shard_map/all_to_all | solution.py:224
  102.3 1.5 %reduce_sum.35.q_ref = bf16[1024,128]{1,0:T(8,128)(2,1)S(1)} reduce(bf16[4,1024,128]{2,1,0:T(8,128)(2,1)} %all-to-all-done.1, bf16[]{:T(256)} %constant.28.clone.1), dimensions={0}, to_apply=%region_2.0 | reduce | flops 393216 | bytes 1310722 | tf_op jit(solution)/shard_map/reduce_sum | solution.py:228
  103.8 3.4 %shard_map.63 = bf16[1024,128]{1,0:T(8,128)(2,1)S(1)} custom-call(s32[1]{0:T(128)} %bitcast.1.shift_ref.x_ref, s32[1]{0:T(128)} %bitcast.2.z_ref, s32[3]{0:T(128)S(1)} %convert_reduce_fusion.bound_ref, s32[32]{0:T(128)S(1)} %bitcast.20, bf16[1024,128]{1,0:T(8,128)(2,1)S(1)} %reduce_sum.35.q_ref, bf16[640,256]{1,0:T(8,128)(2,1)S(1)} %reduce_sum.34.refs_0_, ...), custom_call_target="tpu_custom_call" | custom-call | flops 1 | bytes 1 | tf_op jit(solution)/shard_map/pallas_call | solution.py:304
  107.3 0.7 collective-permute-start.23
  107.9 6.7 %collective-permute-start.24 = (bf16[256,128]{1,0:T(8,128)(2,1)S(1)}, bf16[256,128]{1,0:T(8,128)(2,1)S(1)}, u32[]{:S(2)}, u32[]{:S(2)}) collective-permute-start(bf16[256,128]{1,0:T(8,128)(2,1)S(1)} %get-tuple-element.51), channel_id=1, source_target_pairs={{0,1},{1,5},{2,9},{3,13},{4,2},{5,6},{6,10},{7,14},{8,3},{9,7},{10... | collective-permute-start | bytes 196616 | tf_op jit(solution)/shard_map/ppermute | solution.py:367
  114.7 3.7 %collective-permute-start.25 = (bf16[256,128]{1,0:T(8,128)(2,1)S(1)}, bf16[256,128]{1,0:T(8,128)(2,1)S(1)}, u32[]{:S(2)}, u32[]{:S(2)}) collective-permute-start(bf16[256,128]{1,0:T(8,128)(2,1)S(1)} %get-tuple-element.50), channel_id=1, source_target_pairs={{0,2},{1,6},{2,10},{3,14},{4,3},{5,7},{6,11},{7,15},{8,0},{9,4},{1... | collective-permute-start | bytes 196616 | tf_op jit(solution)/shard_map/ppermute | solution.py:367
  118.4 2.1 %collective-permute-start.26 = (bf16[256,128]{1,0:T(8,128)(2,1)S(1)}, bf16[256,128]{1,0:T(8,128)(2,1)S(1)}, u32[]{:S(2)}, u32[]{:S(2)}) collective-permute-start(bf16[256,128]{1,0:T(8,128)(2,1)S(1)} %get-tuple-element.49), channel_id=1, source_target_pairs={{0,3},{1,7},{2,11},{3,15},{4,0},{5,4},{6,8},{7,12},{8,1},{9,5},{10... | collective-permute-start | bytes 196616 | tf_op jit(solution)/shard_map/ppermute | solution.py:367
  120.5 0.7 collective-permute-done.25.refs_2_
  121.2 3.1 %collective-permute-done.26.refs_3_ = bf16[256,128]{1,0:T(8,128)(2,1)S(1)} collective-permute-done((bf16[256,128]{1,0:T(8,128)(2,1)S(1)}, bf16[256,128]{1,0:T(8,128)(2,1)S(1)}, u32[]{:S(2)}, u32[]{:S(2)}) %collective-permute-start.26) | collective-permute-done | bytes 65568 | tf_op jit(solution)/shard_map/ppermute | solution.py:367
  124.3 0.6 copy-done.13
  124.9 1.7 %shard_map.64 = bf16[1024,128]{1,0:T(8,128)(2,1)} custom-call(s32[1]{0:T(128)} %bitcast.y_ref, bf16[256,128]{1,0:T(8,128)(2,1)} %copy-done.10, bf16[256,128]{1,0:T(8,128)(2,1)} %copy-done.11, bf16[256,128]{1,0:T(8,128)(2,1)} %copy-done.12, bf16[256,128]{1,0:T(8,128)(2,1)} %copy-done.13), custom_call_target="tpu_custom_call" | custom-call | tf_op jit(solution)/shard_map/pallas_call | solution.py:326
  126.6 5.6 %collective-permute-start.27 = (bf16[1024,128]{1,0:T(8,128)(2,1)}, bf16[1024,128]{1,0:T(8,128)(2,1)S(1)}, u32[]{:S(2)}, u32[]{:S(2)}) collective-permute-start(bf16[1024,128]{1,0:T(8,128)(2,1)} %shard_map.64), channel_id=1, source_target_pairs={{0,128},{128,0},{1,129},{129,1},{2,130},{130,2},{3,131},{131,3},{4... | collective-permute-start | bytes 786440 | tf_op jit(solution)/shard_map/ppermute | solution.py:29
  132.2 1.4 %collective-permute-done.27 = bf16[1024,128]{1,0:T(8,128)(2,1)S(1)} collective-permute-done((bf16[1024,128]{1,0:T(8,128)(2,1)}, bf16[1024,128]{1,0:T(8,128)(2,1)S(1)}, u32[]{:S(2)}, u32[]{:S(2)}) %collective-permute-start.27) | collective-permute-done | bytes 262176 | tf_op jit(solution)/shard_map/ppermute | solution.py:29
  133.5 0.7 copy.9
  (43 shorter events, 0.2 us)
Async XLA Ops:
  2.0 3.5 %copy-start.1 = (bf16[1,128,1664]{2,1,0:T(8,128)(2,1)S(1)}, bf16[1,128,1664]{2,1,0:T(8,128)(2,1)}, u32[]{:S(2)}) copy-start(bf16[1,128,1664]{2,1,0:T(8,128)(2,1)} %param.4) | copy-start | bytes 1277956
  2.0 21.1 %copy-start.14 = (s32[1,4096]{1,0:T(1,128)S(1)}, s32[1,4096]{1,0:T(1,128)}, u32[]{:S(2)}) copy-start(s32[1,4096]{1,0:T(1,128)} %param.6) | copy-start | bytes 49156
  2.1 21.2 %collective-permute-start.7 = (bf16[1664,256]{1,0:T(8,128)(2,1)S(1)}, bf16[1664,256]{1,0:T(8,128)(2,1)S(1)}, u32[]{:S(2)}, u32[]{:S(2)}) collective-permute-start(bf16[1664,256]{1,0:T(8,128)(2,1)S(1)} %pad_maximum_fusion.refs_5_.refs_3_), channel_id=1, source_target_pairs={{0,12},{4,0},{8,4},{12,8},{1,13},{5,1},{9,5},{13,9},{2,14},{6,2},{... | collective-permute-start | bytes 2555912 | tf_op jit(solution)/shard_map/ppermute | solution.py:29
  5.5 14.9 %collective-permute-start.3 = (bf16[128,1664]{1,0:T(8,128)(2,1)S(1)}, bf16[128,1664]{1,0:T(8,128)(2,1)}, u32[]{:S(2)}, u32[]{:S(2)}) collective-permute-start(bf16[128,1664]{1,0:T(8,128)(2,1)S(1)} %bitcast.15), channel_id=1, source_target_pairs={{0,16},{16,32},{32,48},{48,64},{64,80},{80,96},{96,112},{112,0},{1... | collective-permute-start | bytes 1277960 | tf_op jit(solution)/shard_map/ppermute | solution.py:29
  7.1 13.3 %collective-permute-start = (bf16[128,1664]{1,0:T(8,128)(2,1)S(1)}, bf16[128,1664]{1,0:T(8,128)(2,1)}, u32[]{:S(2)}, u32[]{:S(2)}) collective-permute-start(bf16[128,1664]{1,0:T(8,128)(2,1)S(1)} %bitcast.16), channel_id=1, source_target_pairs={{0,112},{16,0},{32,16},{48,32},{64,48},{80,64},{96,80},{112,96},{1... | collective-permute-start | bytes 1277960 | tf_op jit(solution)/shard_map/ppermute | solution.py:29
  11.1 23.3 %collective-permute-start.9 = (bf16[1664,256]{1,0:T(8,128)(2,1)S(1)}, bf16[1664,256]{1,0:T(8,128)(2,1)S(1)}, u32[]{:S(2)}, u32[]{:S(2)}) collective-permute-start(bf16[1664,256]{1,0:T(8,128)(2,1)S(1)} %pad_maximum_fusion.refs_5_.refs_3_), channel_id=1, source_target_pairs={{0,4},{4,8},{8,12},{12,0},{1,5},{5,9},{9,13},{13,1},{2,6},{6,10},{... | collective-permute-start | bytes 2555912 | tf_op jit(solution)/shard_map/ppermute | solution.py:29
  20.4 11.3 %collective-permute-start.4 = (bf16[128,1664]{1,0:T(8,128)(2,1)}, bf16[128,1664]{1,0:T(8,128)(2,1)}, u32[]{:S(2)}, u32[]{:S(2)}) collective-permute-start(bf16[128,1664]{1,0:T(8,128)(2,1)} %collective-permute-done.3.refs_4_.refs_7_), channel_id=1, source_target_pairs={{0,16},{16,32},{32,48},{48,64},{64,80},{80,96},{96,112},{112,0},{1... | collective-permute-start | bytes 1277960 | tf_op jit(solution)/shard_map/ppermute | solution.py:29
  20.4 11.3 %collective-permute-start.1 = (bf16[128,1664]{1,0:T(8,128)(2,1)}, bf16[128,1664]{1,0:T(8,128)(2,1)}, u32[]{:S(2)}, u32[]{:S(2)}) collective-permute-start(bf16[128,1664]{1,0:T(8,128)(2,1)} %collective-permute-done.refs_1_), channel_id=1, source_target_pairs={{0,112},{16,0},{32,16},{48,32},{64,48},{80,64},{96,80},{112,96},{1... | collective-permute-start | bytes 1277960 | tf_op jit(solution)/shard_map/ppermute | solution.py:29
  23.3 20.0 %collective-permute-start.8 = (bf16[896,256]{1,0:T(8,128)(2,1)S(1)}, bf16[896,256]{1,0:T(8,128)(2,1)S(1)}, u32[]{:S(2)}, u32[]{:S(2)}) collective-permute-start(bf16[896,256]{1,0:T(8,128)(2,1)S(1)} %slice.30), channel_id=1, source_target_pairs={{0,12},{4,0},{8,4},{12,8},{1,13},{5,1},{9,5},{13,9},{2,14},{6,2},{... | collective-permute-start | bytes 1376264 | tf_op jit(solution)/shard_map/ppermute | solution.py:29
  31.7 10.4 %collective-permute-start.5 = (bf16[128,1664]{1,0:T(8,128)(2,1)}, bf16[128,1664]{1,0:T(8,128)(2,1)}, u32[]{:S(2)}, u32[]{:S(2)}) collective-permute-start(bf16[128,1664]{1,0:T(8,128)(2,1)} %collective-permute-done.4.refs_3_.refs_6_), channel_id=1, source_target_pairs={{0,16},{16,32},{32,48},{48,64},{64,80},{80,96},{96,112},{112,0},{1... | collective-permute-start | bytes 1277960 | tf_op jit(solution)/shard_map/ppermute | solution.py:29
  31.7 10.4 %collective-permute-start.2 = (bf16[128,1664]{1,0:T(8,128)(2,1)}, bf16[128,1664]{1,0:T(8,128)(2,1)S(1)}, u32[]{:S(2)}, u32[]{:S(2)}) collective-permute-start(bf16[128,1664]{1,0:T(8,128)(2,1)} %collective-permute-done.1.refs_2_), channel_id=1, source_target_pairs={{0,112},{16,0},{32,16},{48,32},{64,48},{80,64},{96,80},{112,96},{1... | collective-permute-start | bytes 1277960 | tf_op jit(solution)/shard_map/ppermute | solution.py:29
  34.4 9.0 %collective-permute-start.10 = (bf16[768,256]{1,0:T(8,128)(2,1)S(1)}, bf16[768,256]{1,0:T(8,128)(2,1)S(1)}, u32[]{:S(2)}, u32[]{:S(2)}) collective-permute-start(bf16[768,256]{1,0:T(8,128)(2,1)S(1)} %slice.31), channel_id=1, source_target_pairs={{0,4},{4,8},{8,12},{12,0},{1,5},{5,9},{9,13},{13,1},{2,6},{6,10},{... | collective-permute-start | bytes 1179656 | tf_op jit(solution)/shard_map/ppermute | solution.py:29
  42.1 0.8 copy-start.5
  42.8 11.2 %collective-permute-start.6 = (bf16[128,1664]{1,0:T(8,128)(2,1)}, bf16[128,1664]{1,0:T(8,128)(2,1)}, u32[]{:S(2)}, u32[]{:S(2)}) collective-permute-start(bf16[128,1664]{1,0:T(8,128)(2,1)} %collective-permute-done.5.refs_2_.refs_5_), channel_id=1, source_target_pairs={{0,16},{16,32},{32,48},{48,64},{64,80},{80,96},{96,112},{112,0},{1... | collective-permute-start | bytes 1277960 | tf_op jit(solution)/shard_map/ppermute | solution.py:29
  43.4 23.3 %collective-permute-start.11 = (bf16[1664,128]{1,0:T(8,128)(2,1)S(1)}, bf16[1664,128]{1,0:T(8,128)(2,1)}, u32[]{:S(2)}, u32[]{:S(2)}) collective-permute-start(bf16[1664,128]{1,0:T(8,128)(2,1)S(1)} %get-tuple-element.38.refs_8_), channel_id=1, source_target_pairs={{0,12},{4,0},{8,4},{12,8},{1,13},{5,1},{9,5},{13,9},{2,14},{6,2},{... | collective-permute-start | bytes 1277960 | tf_op jit(solution)/shard_map/ppermute | solution.py:29
  46.9 1.1 copy-start
  48.0 0.8 copy-start.3
  48.8 0.8 copy-start.8
  49.5 27.7 %all-to-all-start = ((bf16[4,640,256]{2,1,0:T(8,128)(2,1)}), bf16[4,640,256]{2,1,0:T(8,128)(2,1)}, u32[]{:S(2)}, u32[]{:S(2)}) async-start(bf16[4,640,256]{2,1,0:T(8,128)(2,1)} %copy-done), calls=%async_computation | async-start | bytes 2621440 | tf_op jit(solution)/shard_map/all_to_all | solution.py:224
  54.0 1.0 copy-start.4
  55.0 1.0 copy-start.6
  56.0 1.0 copy-start.9
  62.0 15.1 %collective-permute-start.14 = (bf16[384,256]{1,0:T(8,128)(2,1)S(1)}, bf16[384,256]{1,0:T(8,128)(2,1)S(1)}, u32[]{:S(2)}, u32[]{:S(2)}) collective-permute-start(bf16[384,256]{1,0:T(8,128)(2,1)S(1)} %get-tuple-element.42), channel_id=1, source_target_pairs={{0,1},{1,2},{2,3},{3,0},{4,5},{5,6},{6,7},{7,4},{8,9},{9,10},{10,1... | collective-permute-start | bytes 589832 | tf_op jit(solution)/shard_map/ppermute | solution.py:29
  63.3 13.8 %collective-permute-start.15 = (bf16[384,256]{1,0:T(8,128)(2,1)S(1)}, bf16[384,256]{1,0:T(8,128)(2,1)S(1)}, u32[]{:S(2)}, u32[]{:S(2)}) collective-permute-start(bf16[384,256]{1,0:T(8,128)(2,1)S(1)} %get-tuple-element.43), channel_id=1, source_target_pairs={{0,3},{1,0},{2,1},{3,2},{4,7},{5,4},{6,5},{7,6},{8,11},{9,8},{10,9... | collective-permute-start | bytes 589832 | tf_op jit(solution)/shard_map/ppermute | solution.py:29
  64.9 12.2 %collective-permute-start.16 = (bf16[384,256]{1,0:T(8,128)(2,1)S(1)}, bf16[384,256]{1,0:T(8,128)(2,1)S(1)}, u32[]{:S(2)}, u32[]{:S(2)}) collective-permute-start(bf16[384,256]{1,0:T(8,128)(2,1)S(1)} %get-tuple-element.44), channel_id=1, source_target_pairs={{0,2},{1,3},{2,0},{3,1},{4,6},{5,7},{6,4},{7,5},{8,10},{9,11},{10,... | collective-permute-start | bytes 589832 | tf_op jit(solution)/shard_map/ppermute | solution.py:29
  66.4 14.0 %collective-permute-start.13 = (bf16[1664,128]{1,0:T(8,128)(2,1)S(1)}, bf16[1664,128]{1,0:T(8,128)(2,1)S(1)}, u32[]{:S(2)}, u32[]{:S(2)}) collective-permute-start(bf16[1664,128]{1,0:T(8,128)(2,1)S(1)} %get-tuple-element.38.refs_8_), channel_id=1, source_target_pairs={{0,4},{4,8},{8,12},{12,0},{1,5},{5,9},{9,13},{13,1},{2,6},{6,10},{... | collective-permute-start | bytes 1277960 | tf_op jit(solution)/shard_map/ppermute | solution.py:29
  66.7 13.8 %collective-permute-start.12 = (bf16[1664,128]{1,0:T(8,128)(2,1)}, bf16[1664,128]{1,0:T(8,128)(2,1)}, u32[]{:S(2)}, u32[]{:S(2)}) collective-permute-start(bf16[1664,128]{1,0:T(8,128)(2,1)} %collective-permute-done.11.refs_9_), channel_id=1, source_target_pairs={{0,12},{4,0},{8,4},{12,8},{1,13},{5,1},{9,5},{13,9},{2,14},{6,2},{... | collective-permute-start | bytes 1277960 | tf_op jit(solution)/shard_map/ppermute | solution.py:29
  77.1 3.4 %copy-start.7 = (bf16[128,1664]{1,0:T(8,128)(2,1)S(1)}, bf16[128,1664]{1,0:T(8,128)(2,1)}, u32[]{:S(2)}) copy-start(bf16[128,1664]{1,0:T(8,128)(2,1)} %copy-done.5) | copy-start | bytes 1277956
  78.9 8.8 %collective-permute-start.17 = (bf16[640,256]{1,0:T(8,128)(2,1)S(1)}, bf16[640,256]{1,0:T(8,128)(2,1)S(1)}, u32[]{:S(2)}, u32[]{:S(2)}) collective-permute-start(bf16[640,256]{1,0:T(8,128)(2,1)S(1)} %reduce_sum.34.refs_0_), channel_id=1, source_target_pairs={{0,12},{4,0},{8,4},{12,8},{1,13},{5,1},{9,5},{13,9},{2,14},{6,2},{... | collective-permute-start | bytes 983048 | tf_op jit(solution)/shard_map/ppermute | solution.py:29
  79.6 8.1 %collective-permute-start.18 = (bf16[640,256]{1,0:T(8,128)(2,1)S(1)}, bf16[640,256]{1,0:T(8,128)(2,1)S(1)}, u32[]{:S(2)}, u32[]{:S(2)}) collective-permute-start(bf16[640,256]{1,0:T(8,128)(2,1)S(1)} %reduce_sum.34.refs_0_), channel_id=1, source_target_pairs={{0,4},{4,8},{8,12},{12,0},{1,5},{5,9},{9,13},{13,1},{2,6},{6,10},{... | collective-permute-start | bytes 983048 | tf_op jit(solution)/shard_map/ppermute | solution.py:29
  87.7 16.1 %copy-start.2 = (s32[1,32]{1,0:T(1,128)S(1)}, s32[1,32]{1,0:T(1,128)}, u32[]{:S(2)}) copy-start(s32[1,32]{1,0:T(1,128)} %param.7) | copy-start | bytes 388
  87.8 14.5 %all-to-all-start.1 = ((bf16[4,1024,128]{2,1,0:T(8,128)(2,1)}), bf16[4,1024,128]{2,1,0:T(8,128)(2,1)}, u32[]{:S(2)}, u32[]{:S(2)}) async-start(bf16[4,1024,128]{2,1,0:T(8,128)(2,1)} %shard_map.62), calls=%async_computation.1 | async-start | bytes 2097152 | tf_op jit(solution)/shard_map/all_to_all | solution.py:224
  92.0 11.8 %collective-permute-start.19 = (bf16[640,256]{1,0:T(8,128)(2,1)S(1)}, bf16[640,256]{1,0:T(8,128)(2,1)S(1)}, u32[]{:S(2)}, u32[]{:S(2)}) collective-permute-start(bf16[640,256]{1,0:T(8,128)(2,1)S(1)} %collective-permute-done.17.refs_1_), channel_id=1, source_target_pairs={{0,12},{4,0},{8,4},{12,8},{1,13},{5,1},{9,5},{13,9},{2,14},{6,2},{... | collective-permute-start | bytes 983048 | tf_op jit(solution)/shard_map/ppermute | solution.py:29
  94.0 9.8 %collective-permute-start.20 = (bf16[384,256]{1,0:T(8,128)(2,1)S(1)}, bf16[384,256]{1,0:T(8,128)(2,1)S(1)}, u32[]{:S(2)}, u32[]{:S(2)}) collective-permute-start(bf16[384,256]{1,0:T(8,128)(2,1)S(1)} %add_convert_fusion.refs_4_), channel_id=1, source_target_pairs={{0,12},{4,0},{8,4},{12,8},{1,13},{5,1},{9,5},{13,9},{2,14},{6,2},{... | collective-permute-start | bytes 589832 | tf_op jit(solution)/shard_map/ppermute | solution.py:29
  94.1 9.7 %collective-permute-start.21 = (bf16[384,256]{1,0:T(8,128)(2,1)S(1)}, bf16[384,256]{1,0:T(8,128)(2,1)S(1)}, u32[]{:S(2)}, u32[]{:S(2)}) collective-permute-start(bf16[384,256]{1,0:T(8,128)(2,1)S(1)} %add_convert_fusion.refs_4_), channel_id=1, source_target_pairs={{0,8},{4,12},{8,0},{12,4},{1,9},{5,13},{9,1},{13,5},{2,10},{6,14},... | collective-permute-start | bytes 589832 | tf_op jit(solution)/shard_map/ppermute | solution.py:29
  95.4 8.4 %collective-permute-start.22 = (bf16[384,256]{1,0:T(8,128)(2,1)S(1)}, bf16[384,256]{1,0:T(8,128)(2,1)S(1)}, u32[]{:S(2)}, u32[]{:S(2)}) collective-permute-start(bf16[384,256]{1,0:T(8,128)(2,1)S(1)} %add_convert_fusion.refs_4_), channel_id=1, source_target_pairs={{0,4},{4,8},{8,12},{12,0},{1,5},{5,9},{9,13},{13,1},{2,6},{6,10},{... | collective-permute-start | bytes 589832 | tf_op jit(solution)/shard_map/ppermute | solution.py:29
  107.3 13.2 %collective-permute-start.23 = (bf16[256,128]{1,0:T(8,128)(2,1)S(1)}, bf16[256,128]{1,0:T(8,128)(2,1)S(1)}, u32[]{:S(2)}, u32[]{:S(2)}) collective-permute-start(bf16[256,128]{1,0:T(8,128)(2,1)S(1)} %get-tuple-element.52), channel_id=1, source_target_pairs={{0,0},{1,4},{2,8},{3,12},{4,1},{5,5},{6,9},{7,13},{8,2},{9,6},{10,... | collective-permute-start | bytes 196616 | tf_op jit(solution)/shard_map/ppermute | solution.py:367
  107.9 12.5 %collective-permute-start.24 = (bf16[256,128]{1,0:T(8,128)(2,1)S(1)}, bf16[256,128]{1,0:T(8,128)(2,1)S(1)}, u32[]{:S(2)}, u32[]{:S(2)}) collective-permute-start(bf16[256,128]{1,0:T(8,128)(2,1)S(1)} %get-tuple-element.51), channel_id=1, source_target_pairs={{0,1},{1,5},{2,9},{3,13},{4,2},{5,6},{6,10},{7,14},{8,3},{9,7},{10... | collective-permute-start | bytes 196616 | tf_op jit(solution)/shard_map/ppermute | solution.py:367
  114.7 6.5 %collective-permute-start.25 = (bf16[256,128]{1,0:T(8,128)(2,1)S(1)}, bf16[256,128]{1,0:T(8,128)(2,1)S(1)}, u32[]{:S(2)}, u32[]{:S(2)}) collective-permute-start(bf16[256,128]{1,0:T(8,128)(2,1)S(1)} %get-tuple-element.50), channel_id=1, source_target_pairs={{0,2},{1,6},{2,10},{3,14},{4,3},{5,7},{6,11},{7,15},{8,0},{9,4},{1... | collective-permute-start | bytes 196616 | tf_op jit(solution)/shard_map/ppermute | solution.py:367
  118.4 6.0 %collective-permute-start.26 = (bf16[256,128]{1,0:T(8,128)(2,1)S(1)}, bf16[256,128]{1,0:T(8,128)(2,1)S(1)}, u32[]{:S(2)}, u32[]{:S(2)}) collective-permute-start(bf16[256,128]{1,0:T(8,128)(2,1)S(1)} %get-tuple-element.49), channel_id=1, source_target_pairs={{0,3},{1,7},{2,11},{3,15},{4,0},{5,4},{6,8},{7,12},{8,1},{9,5},{10... | collective-permute-start | bytes 196616 | tf_op jit(solution)/shard_map/ppermute | solution.py:367
  120.5 3.8 %copy-start.10 = (bf16[256,128]{1,0:T(8,128)(2,1)}, bf16[256,128]{1,0:T(8,128)(2,1)S(1)}, u32[]{:S(2)}) copy-start(bf16[256,128]{1,0:T(8,128)(2,1)S(1)} %collective-permute-done.23.refs_0_) | copy-start | bytes 196612
  120.5 3.8 %copy-start.11 = (bf16[256,128]{1,0:T(8,128)(2,1)}, bf16[256,128]{1,0:T(8,128)(2,1)S(1)}, u32[]{:S(2)}) copy-start(bf16[256,128]{1,0:T(8,128)(2,1)S(1)} %collective-permute-done.24.refs_1_) | copy-start | bytes 196612
  121.2 3.1 %copy-start.12 = (bf16[256,128]{1,0:T(8,128)(2,1)}, bf16[256,128]{1,0:T(8,128)(2,1)S(1)}, u32[]{:S(2)}) copy-start(bf16[256,128]{1,0:T(8,128)(2,1)S(1)} %collective-permute-done.25.refs_2_) | copy-start | bytes 196612
  124.3 0.6 copy-start.13
  126.6 6.9 %collective-permute-start.27 = (bf16[1024,128]{1,0:T(8,128)(2,1)}, bf16[1024,128]{1,0:T(8,128)(2,1)S(1)}, u32[]{:S(2)}, u32[]{:S(2)}) collective-permute-start(bf16[1024,128]{1,0:T(8,128)(2,1)} %shard_map.64), channel_id=1, source_target_pairs={{0,128},{128,0},{1,129},{129,1},{2,130},{130,2},{3,131},{131,3},{4... | collective-permute-start | bytes 786440 | tf_op jit(solution)/shard_map/ppermute | solution.py:29

commit v3 on v2

--- a/solution.py
+++ b/solution.py
@@ -56,23 +56,27 @@
     return found
 
 
-def fill_rows(pieces, rows):
-    at = 0
-    for piece in pieces:
-        rows[at : at + piece.shape[0], :] = piece[...]
+def loads_of(pieces, weights, columns, rows, wide, sems):
+    row_loads, at = [], 0
+    for i, piece in enumerate(pieces):
+        place = rows.at[pl.ds(at, piece.shape[0])]
+        row_loads.append(pltpu.make_async_copy(piece, place, sems.at[i]))
         at += piece.shape[0]
-
-
-def product_of(rows, weights):
-    total, at = None, 0
-    for weight in weights:
-        width = weight.shape[0]
-        term = jnp.dot(
-            rows[:, at : at + width], weight[...], preferred_element_type=jnp.float32
-        )
-        total = term if total is None else total + term
-        at += width
-    return total
+    slot_loads, number = [], len(pieces)
+    for i, parts in enumerate(weights):
+        begin, at, copies = i * columns, 0, []
+        for part in parts:
+            place = wide.at[begin // 256, pl.ds(at, part.shape[0]), pl.ds(begin % 256, columns)]
+            copies.append(pltpu.make_async_copy(part, place, sems.at[number]))
+            at += part.shape[0]
+            number += 1
+        slot_loads.append(copies)
+    for copies in [row_loads] + slot_loads:
+        for copy in copies:
+            copy.start()
+    for copy in row_loads:
+        copy.wait()
+    return slot_loads
 
 
 def cut_by(counts, refs):
@@ -83,141 +87,107 @@
     return groups
 
 
-def store_for(outs, shift, slot, product):
-    target = lax.rem(slot + shift, 4)
-    if len(outs) == 1:
-        outs[0][target] = product.astype(outs[0].dtype)
-        return
-    for k in range(4):
-
-        @pl.when(target == k)
-        def _():
-            outs[k][...] = product.astype(outs[k].dtype)
-
-
-def project_kernel(shift_ref, *refs, pieces, slots, counts):
-    total = sum(counts)
-    weights = cut_by(counts, refs[pieces : pieces + total])
-    outs = refs[pieces + total : -1]
-    rows = refs[-1]
-    fill_rows(refs[:pieces], rows)
-    if len(outs) == 2:
-        outs[1][...] = jnp.zeros_like(outs[1])
-        outs = outs[:1]
-    for slot, weight in zip(slots, weights):
-        store_for(outs, shift_ref[0], slot, product_of(rows, weight))
-
-
-def project_rest_kernel(x_ref, *refs, pieces, slot):
-    weights = refs[pieces : pieces + 2]
-    out = refs[pieces + 3]
-    rows, result, sem = refs[pieces + 4 :]
-    fill_rows(refs[:pieces], rows)
-    result[...] = product_of(rows, weights).astype(result.dtype)
-    copy = pltpu.make_async_copy(result, out.at[lax.rem(slot + x_ref[0], 4)], sem)
-    copy.start()
-    copy.wait()
-
-
-def project_far_kernel(shift_ref, *refs, pieces, slots, counts, columns):
-    total = sum(counts)
-    outs = refs[pieces + total : -3]
-    rows, wide, sems = refs[-3:]
-    loads, at = [], 0
-    for i, piece in enumerate(refs[:pieces]):
-        place = rows.at[pl.ds(at, piece.shape[0])]
-        loads.append(pltpu.make_async_copy(piece, place, sems.at[i]))
-        at += piece.shape[0]
-    weight_loads, number = [], pieces
-    for i, weights in enumerate(cut_by(counts, refs[pieces : pieces + total])):
-        begin, at = i * columns, 0
-        for weight in weights:
-            place = wide.at[
-                begin // 256, pl.ds(at, weight.shape[0]), pl.ds(begin % 256, columns)
-            ]
-            weight_loads.append((i, pltpu.make_async_copy(weight, place, sems.at[number])))
-            at += weight.shape[0]
-            number += 1
-    for copy in loads:
-        copy.start()
-    for _, copy in weight_loads:
-        copy.start()
-    for copy in loads:
-        copy.wait()
-    for tile in range(4 * columns // 256):
-        inside = [i for i in range(4) if i * columns // 256 == tile]
-        for i, copy in weight_loads:
-            if i in inside:
+def products(pieces, weights, columns, rows, wide, sems):
+    slot_loads = loads_of(pieces, weights, columns, rows, wide, sems)
+    per_tile = 256 // columns
+    for tile in range(len(weights) // per_tile):
+        inside = range(tile * per_tile, (tile + 1) * per_tile)
+        for i in inside:
+            for copy in slot_loads[i]:
                 copy.wait()
         product = jnp.dot(rows[...], wide[tile], preferred_element_type=jnp.float32)
         for i in inside:
             begin = i * columns % 256
-            store_for(outs, shift_ref[0], slots[i], product[:, begin : begin + columns])
-
-
-def project_far(columns, shift, pieces, parts_of, slots, stacked=False):
+            yield i, product[:, begin : begin + columns].astype(jnp.bfloat16)
+
+
+def scratch_for(count, width, columns, slots, operands):
+    return [
+        pltpu.VMEM((count, width), jnp.bfloat16),
+        pltpu.VMEM((slots * columns // 256, width, 256), jnp.bfloat16),
+        pltpu.SemaphoreType.DMA((operands,)),
+    ]
+
+
+def project_kernel(shift_ref, *refs, pieces, slots, counts, columns):
+    total = pieces + sum(counts)
+    outs = refs[total : total + 4]
+    weights = cut_by(counts, refs[pieces:total])
+    for i, product in products(refs[:pieces], weights, columns, *refs[total + 4 :]):
+        target = lax.rem(slots[i] + shift_ref[0], 4)
+        for k in range(4):
+
+            @pl.when(target == k)
+            def _():
+                outs[k][...] = product
+
+
+def project_stack_kernel(x_ref, *refs, pieces, slots, counts, columns, added):
+    total = pieces + sum(counts)
+    weights = cut_by(counts, refs[pieces:total])
+    out, mark = refs[total + added : total + added + 2]
+    rows, wide, sems, stage, out_sems = refs[total + added + 2 :]
+    mark[...] = jnp.zeros_like(mark)
+    copies = []
+    for i, product in products(refs[:pieces], weights, columns, rows, wide, sems):
+        stage[i] = product
+        place = out.at[lax.rem(slots[i] + x_ref[0], 4)]
+        copies.append(pltpu.make_async_copy(stage.at[i], place, out_sems.at[i]))
+        copies[-1].start()
+    for copy in copies:
+        copy.wait()
+
+
+def project(columns, shift, pieces, parts_of, slots):
     weights = [part for slot in slots for part in parts_of[slot]]
     counts = tuple(len(parts_of[slot]) for slot in slots)
     count = sum(piece.shape[0] for piece in pieces)
     width = pieces[0].shape[1]
+    operands = len(pieces) + len(weights)
     return pl.pallas_call(
         functools.partial(
-            project_far_kernel, pieces=len(pieces), slots=slots, counts=counts, columns=columns
+            project_kernel, pieces=len(pieces), slots=slots, counts=counts, columns=columns
         ),
-        in_specs=[SMEM] + [FAR] * (len(pieces) + len(weights)),
-        out_specs=[VMEM] * (1 if stacked else 4),
-        out_shape=[jax.ShapeDtypeStruct((4, count, columns), jnp.bfloat16)]
-        if stacked
-        else [jax.ShapeDtypeStruct((count, columns), jnp.bfloat16)] * 4,
-        scratch_shapes=[
-            pltpu.VMEM((count, width), jnp.bfloat16),
-            pltpu.VMEM((4 * columns // 256, width, 256), jnp.bfloat16),
-            pltpu.SemaphoreType.DMA((len(pieces) + len(weights),)),
-        ],
+        in_specs=[SMEM] + [FAR] * operands,
+        out_specs=[VMEM] * 4,
+        out_shape=[jax.ShapeDtypeStruct((count, columns), jnp.bfloat16)] * 4,
+        scratch_shapes=scratch_for(count, width, columns, len(slots), operands),
         cost_estimate=LONG,
         compiler_params=LIMIT,
     )(shift, *pieces, *weights)
 
 
-def project(kernel, columns, shift, pieces, parts_of, slots, stacked=False, mark=False):
+def project_stack(columns, x, pieces, parts_of, slots, stack=None):
     weights = [part for slot in slots for part in parts_of[slot]]
     counts = tuple(len(parts_of[slot]) for slot in slots)
     count = sum(piece.shape[0] for piece in pieces)
     width = pieces[0].shape[1]
-    scratch = [pltpu.VMEM((count, width), jnp.bfloat16)]
+    operands = len(pieces) + len(weights)
+    extra = [] if stack is None else [stack]
     return pl.pallas_call(
-        functools.partial(kernel, pieces=len(pieces), slots=slots, counts=counts),
-        in_specs=[SMEM] + [VMEM] * (len(pieces) + len(weights)),
-        out_specs=[VMEM] * (1 + mark if stacked else 4),
+        functools.partial(
+            project_stack_kernel,
+            pieces=len(pieces),
+            slots=slots,
+            counts=counts,
+            columns=columns,
+            added=len(extra),
+        ),
+        in_specs=[SMEM] + [FAR] * (operands + len(extra)),
+        out_specs=[FAR, VMEM],
         out_shape=[
             jax.ShapeDtypeStruct((4, count, columns), jnp.bfloat16),
             jax.ShapeDtypeStruct((8, HEAD), jnp.float32),
-        ][: 1 + mark]
-        if stacked
-        else [jax.ShapeDtypeStruct((count, columns), jnp.bfloat16)] * 4,
-        scratch_shapes=scratch,
-        cost_estimate=BRIEF if mark else LONG,
+        ],
+        input_output_aliases={1 + operands: 0} if extra else {},
+        scratch_shapes=scratch_for(count, width, columns, len(slots), operands)
+        + [
+            pltpu.VMEM((len(slots), count, columns), jnp.bfloat16),
+            pltpu.SemaphoreType.DMA((len(slots),)),
+        ],
+        cost_estimate=BRIEF if len(slots) == 3 else LONG,
         compiler_params=LIMIT,
-    )(shift, *pieces, *weights)
-
-
-def project_rest(x, pieces, halves, slot, stack):
-    _, count, columns = stack.shape
-    width = pieces[0].shape[1]
-    return pl.pallas_call(
-        functools.partial(project_rest_kernel, pieces=len(pieces), slot=slot),
-        in_specs=[SMEM] + [VMEM] * (len(pieces) + 2) + [FAR],
-        out_specs=FAR,
-        out_shape=jax.ShapeDtypeStruct(stack.shape, stack.dtype),
-        input_output_aliases={3 + len(pieces): 0},
-        scratch_shapes=[
-            pltpu.VMEM((count, width), jnp.bfloat16),
-            pltpu.VMEM((count, columns), jnp.bfloat16),
-            pltpu.SemaphoreType.DMA,
-        ],
-        cost_estimate=LONG,
-        compiler_params=LIMIT,
-    )(x, *pieces, *halves[slot], stack)
+    )(x, *pieces, *weights, *extra)
 
 
 def exchange(stack, axis):
@@ -228,11 +198,11 @@
     return jnp.sum(stack.astype(jnp.float32), axis=0).astype(jnp.bfloat16)
 
 
-def sum_over_y(parts):
-    own, one, two, three = parts
-    total = own.astype(jnp.float32)
-    for k, part in ((1, one), (3, three), (2, two)):
-        total = total + send(part, "y", k).astype(jnp.float32)
+def sum_over_y(parts, *earlier):
+    received = after([send(part, "y", k) for k, part in enumerate(parts) if k], earlier)
+    total = parts[0].astype(jnp.float32)
+    for part in received:
+        total = total + part.astype(jnp.float32)
     return total.astype(jnp.bfloat16)
 
 
@@ -313,12 +283,13 @@
 
 
 def place_kernel(y_ref, *refs):
-    parts, out = refs[:4], refs[4]
+    parts, outs = refs[:4], refs[4:]
     for s in range(4):
         x = lax.rem(y_ref[0] + 4 - s, 4)
         for t in range(2):
             at = pl.ds(pl.multiple_of((4 * t + x) * BLOCK, BLOCK), BLOCK)
-            out[at, :] = parts[s][t * BLOCK : (t + 1) * BLOCK, :]
+            for out in outs:
+                out[at, :] = parts[s][t * BLOCK : (t + 1) * BLOCK, :]
 
 
 def place(y, parts):
@@ -326,8 +297,8 @@
     return pl.pallas_call(
         place_kernel,
         in_specs=[SMEM] + [VMEM] * 4,
-        out_specs=VMEM,
-        out_shape=jax.ShapeDtypeStruct((rows, HEAD), jnp.bfloat16),
+        out_specs=[VMEM] * 2,
+        out_shape=[jax.ShapeDtypeStruct((rows, HEAD), jnp.bfloat16)] * 2,
     )(y, *parts)
 
 
@@ -347,19 +318,18 @@
         return [piece for offset in offsets for piece in blocks[offset]]
 
     near = pieces(EARLY)
-    stack, mark = project(project_kernel, 256, x, near, kv_w, (0, 1, 3), True, True)
+    stack, mark = project_stack(256, x, near, kv_w, (0, 1, 3))
     near = after(near, blocks[3], blocks[5])
-    stack = project_rest(x, near, kv_w, 2, stack)
     own = after(weights[:, 0, :], mark, kv_w[2])
-    q_w = [(part,) for part in gather_x_by_right(own, stack)]
+    stack, mark = project_stack(256, x, near, kv_w, (2,), stack)
+    q_w = [(part,) for part in gather_x_by_right(own)]
     received = exchange(stack, "y")
-    late_pieces = after(pieces(LATE), stack)
-    late_parts = project_far(256, shift, late_pieces, kv_w, (0, 1, 3, 2))
-    late = sum_over_y(late_parts)
+    late_parts = project(256, shift, after(pieces(LATE), mark), kv_w, (0, 1, 3, 2))
     early = sum_of(received)
     q_w = after(q_w, late_parts[0], early)
     early = gather_x_by_right(early)
-    (stack,) = project_far(128, x, pieces(range(8)), q_w, (0, 1, 3, 2), True)
+    stack, mark = project_stack(128, x, pieces(range(8)), q_w, (0, 1, 3, 2))
+    late = sum_over_y(late_parts, stack)
     query = sum_of(exchange(after(stack, late, early[1], early[3]), "y"))
     mixed = attend(x, z, bounds, exit_flags[0], query, early, gather_x(late))
     quarter = mixed.shape[0] // 4
@@ -371,8 +341,8 @@
         )
         for s in range(4)
     ]
-    result = place(y, moved)
-    handed = send(result, "phase", 1)
+    result, given = place(y, moved)
+    handed = send(given, "phase", 1)
     return (result[None], handed[None])
 
 

time: 135 us -> 130 us (0.963)
  waiting for transfers between devices: 38.5 us -> 28.5 us
  Pallas kernels: 23.4 us -> 27.3 us
  starting transfers between devices: 58.6 us -> 61.2 us
  local copies, waits for them, and re-layouts: 9.19 us -> 7.61 us
    ppermute x24, waiting for transfers between devices: 27.9 us -> 18.5 us  [send(): lax.ppermute(block, axis, [(i, (i + distance) % n) for i in range(n)])]
    ppermute x24, starting transfers between devices: 36.7 us -> 43.7 us  [send(): lax.ppermute(block, axis, [(i, (i + distance) % n) for i in range(n)])]
    pallas_call x5, Pallas kernels: 20 us -> 24.4 us  [the longest x3 16.9 us: project_stack(): pl.pallas_call(functools.partial(project_stack_kernel, pieces=len(pieces)...]
    ppermute x4, starting transfers between devices: 13.2 us -> 8.96 us  [local(): lax.ppermute(mixed[s * quarter:(s + 1) * quarter], ('x', 'y'), [(4 * i +...]
    unnamed x31 -> x35, local copies, waits for them, and re-layouts: 7.76 us -> 6.18 us
  transfers between devices with their start and end apart: 30 -> 30, of which waited for: 9 -> 8; matrix products, arithmetic and copies ran while one was open for 3% -> 3% of each run, Pallas kernels for 14% -> 18%
where the time goes in v3:
time: 130 us; the launch traced here: 129 us
  starting transfers between devices  61.2 us (47%)
  waiting for transfers between devices  28.5 us (22%)
  Pallas kernels  27.3 us (21%)
  local copies, waits for them, and re-layouts  7.61 us (6%)
  other arithmetic  3.53 us (3%)
    ppermute x24, starting transfers between devices, send(): lax.ppermute(block, axis, [(i, (i + distance) % n) for i in range(n)])  43.7 us
    ppermute x24, waiting for transfers between devices, send(): lax.ppermute(block, axis, [(i, (i + distance) % n) for i in range(n)])  18.5 us
    pallas_call x3, Pallas kernels, project_stack(): pl.pallas_call(functools.partial(project_stack_kernel, pieces=len(pieces)...  16.9 us
    ppermute x4, starting transfers between devices, local(): lax.ppermute(mixed[s * quarter:(s + 1) * quarter], ('x', 'y'), [(4 * i +...  8.96 us
    all_to_all x2, starting transfers between devices, exchange(): return lax.all_to_all(stack, axis, 0, 0, tiled=True)  8.55 us
    all_to_all x2, waiting for transfers between devices, exchange(): return lax.all_to_all(stack, axis, 0, 0, tiled=True)  6.47 us
    unnamed x35, local copies, waits for them, and re-layouts  6.18 us
    pallas_call x1, Pallas kernels, project(): pl.pallas_call(functools.partial(project_kernel, pieces=len(pieces), slot...  5.75 us
  transfers between devices with their start and end apart: 30, of which 8 were waited for; matrix products, arithmetic and copies ran while one was open for 3% of the time, Pallas kernels for 18%

profile of v3, /device:TPU:1, one launch (start us, length us, event | category | flops | bytes accessed | tf_op | source)
XLA Modules:
  0.0 129.2 jit_solution(7085022199938756955)
XLA Ops:
  0.6 1.3 %slice_bitcast_fusion.1 = (bf16[1664,128]{1,0:T(8,128)(2,1)S(1)}, bf16[1664,128]{1,0:T(8,128)(2,1)S(1)}, bf16[1664,128]{1,0:T(8,128)(2,1)S(1)}) fusion(bf16[1664,3,128]{2,0,1:T(8,128)(2,1)} %bitcast.21), kind=kLoop, calls=%fused_computation.2 | loop fusion | bytes 2555904 | tf_op jit(solution)/shard_map/squeeze | solution.py:314
  2.0 0.0 copy-start.1
  2.0 0.0 copy-start.16
  2.0 0.1 pad_maximum_fusion.refs_3_.refs_5_
  2.1 3.4 %collective-permute-start.7 = (bf16[1664,256]{1,0:T(8,128)(2,1)S(1)}, bf16[1664,256]{1,0:T(8,128)(2,1)S(1)}, u32[]{:S(2)}, u32[]{:S(2)}) collective-permute-start(bf16[1664,256]{1,0:T(8,128)(2,1)S(1)} %pad_maximum_fusion.refs_3_.refs_5_), channel_id=1, source_target_pairs={{0,12},{4,0},{8,4},{12,8},{1,13},{5,1},{9,5},{13,9},{2,14},{6,2},{... | collective-permute-start | bytes 2555912 | tf_op jit(solution)/shard_map/ppermute | solution.py:29
  5.5 1.6 %collective-permute-start.3 = (bf16[128,1664]{1,0:T(8,128)(2,1)S(1)}, bf16[128,1664]{1,0:T(8,128)(2,1)}, u32[]{:S(2)}, u32[]{:S(2)}) collective-permute-start(bf16[128,1664]{1,0:T(8,128)(2,1)S(1)} %bitcast.15), channel_id=1, source_target_pairs={{0,16},{16,32},{32,48},{48,64},{64,80},{80,96},{96,112},{112,0},{1... | collective-permute-start | bytes 1277960 | tf_op jit(solution)/shard_map/ppermute | solution.py:29
  7.1 3.9 %collective-permute-start = (bf16[128,1664]{1,0:T(8,128)(2,1)S(1)}, bf16[128,1664]{1,0:T(8,128)(2,1)}, u32[]{:S(2)}, u32[]{:S(2)}) collective-permute-start(bf16[128,1664]{1,0:T(8,128)(2,1)S(1)} %bitcast.16), channel_id=1, source_target_pairs={{0,112},{16,0},{32,16},{48,32},{64,48},{80,64},{96,80},{112,96},{1... | collective-permute-start | bytes 1277960 | tf_op jit(solution)/shard_map/ppermute | solution.py:29
  11.1 9.3 %collective-permute-done.3.refs_4_.refs_7_ = bf16[128,1664]{1,0:T(8,128)(2,1)} collective-permute-done((bf16[128,1664]{1,0:T(8,128)(2,1)S(1)}, bf16[128,1664]{1,0:T(8,128)(2,1)}, u32[]{:S(2)}, u32[]{:S(2)}) %collective-permute-start.3) | collective-permute-done | bytes 426016 | tf_op jit(solution)/shard_map/ppermute | solution.py:29
  20.4 0.0 collective-permute-start.4
  20.4 0.0 collective-permute-done.refs_1_
  20.4 2.7 %collective-permute-start.1 = (bf16[128,1664]{1,0:T(8,128)(2,1)}, bf16[128,1664]{1,0:T(8,128)(2,1)}, u32[]{:S(2)}, u32[]{:S(2)}) collective-permute-start(bf16[128,1664]{1,0:T(8,128)(2,1)} %collective-permute-done.refs_1_), channel_id=1, source_target_pairs={{0,112},{16,0},{32,16},{48,32},{64,48},{80,64},{96,80},{112,96},{1... | collective-permute-start | bytes 1277960 | tf_op jit(solution)/shard_map/ppermute | solution.py:29
  23.1 0.2 convert_reduce_fusion.bound_ref
  23.3 3.3 %collective-permute-start.8 = (bf16[896,256]{1,0:T(8,128)(2,1)S(1)}, bf16[896,256]{1,0:T(8,128)(2,1)S(1)}, u32[]{:S(2)}, u32[]{:S(2)}) collective-permute-start(bf16[896,256]{1,0:T(8,128)(2,1)S(1)} %slice.30), channel_id=1, source_target_pairs={{0,12},{4,0},{8,4},{12,8},{1,13},{5,1},{9,5},{13,9},{2,14},{6,2},{... | collective-permute-start | bytes 1376264 | tf_op jit(solution)/shard_map/ppermute | solution.py:29
  26.6 5.1 %collective-permute-done.4.refs_3_.refs_6_ = bf16[128,1664]{1,0:T(8,128)(2,1)} collective-permute-done((bf16[128,1664]{1,0:T(8,128)(2,1)}, bf16[128,1664]{1,0:T(8,128)(2,1)}, u32[]{:S(2)}, u32[]{:S(2)}) %collective-permute-start.4) | collective-permute-done | bytes 426016 | tf_op jit(solution)/shard_map/ppermute | solution.py:29
  31.7 2.7 %collective-permute-start.2 = (bf16[128,1664]{1,0:T(8,128)(2,1)}, bf16[128,1664]{1,0:T(8,128)(2,1)S(1)}, u32[]{:S(2)}, u32[]{:S(2)}) collective-permute-start(bf16[128,1664]{1,0:T(8,128)(2,1)} %collective-permute-done.1.refs_2_), channel_id=1, source_target_pairs={{0,112},{16,0},{32,16},{48,32},{64,48},{80,64},{96,80},{112,96},{1... | collective-permute-start | bytes 1277960 | tf_op jit(solution)/shard_map/ppermute | solution.py:29
  34.4 0.0 collective-permute-done.9.refs_5_.refs_7_
  34.4 0.3 collective-permute-start.10
  34.7 6.0 %shard_map.60 = (bf16[4,640,256]{2,1,0:T(8,128)(2,1)S(1)}, f32[8,128]{1,0:T(8,128)}) custom-call(s32[1]{0:T(128)} %bitcast.1.x_ref, bf16[128,1664]{1,0:T(8,128)(2,1)S(1)} %bitcast.17, bf16[128,1664]{1,0:T(8,128)(2,1)} %collective-permute-done.refs_1_, bf16[128,1664]{1,0:T(8,128)(2,1)} %collective-permute-done.1.refs_2_, ...), custom_call_target="tpu_custom_call" | custom-call | flops 1 | bytes 1 | tf_op jit(solution)/shard_map/pallas_call | solution.py:167
  40.7 1.4 %collective-permute-done.5.refs_2_.refs_5_ = bf16[128,1664]{1,0:T(8,128)(2,1)} collective-permute-done((bf16[128,1664]{1,0:T(8,128)(2,1)}, bf16[128,1664]{1,0:T(8,128)(2,1)}, u32[]{:S(2)}, u32[]{:S(2)}) %collective-permute-start.5) | collective-permute-done | bytes 426016 | tf_op jit(solution)/shard_map/ppermute | solution.py:29
  42.1 0.0 collective-permute-done.2.refs_0_.refs_3_
  42.1 0.0 collective-permute-start.6
  42.1 1.3 %collective-permute-done.10.refs_7_.refs_6_ = bf16[768,256]{1,0:T(8,128)(2,1)S(1)} collective-permute-done((bf16[768,256]{1,0:T(8,128)(2,1)S(1)}, bf16[768,256]{1,0:T(8,128)(2,1)S(1)}, u32[]{:S(2)}, u32[]{:S(2)}) %collective-permute-start.10) | collective-permute-done | bytes 393248 | tf_op jit(solution)/shard_map/ppermute | solution.py:29
  43.4 0.0 collective-permute-done.8.refs_6_.refs_5_
  43.4 0.5 collective-permute-start.11
  43.9 1.0 collective-permute-start.13
  44.9 3.1 %shard_map.61 = (bf16[4,640,256]{2,1,0:T(8,128)(2,1)S(1)}, f32[8,128]{1,0:T(8,128)}) custom-call(s32[1]{0:T(128)} %bitcast.1.x_ref, bf16[128,1664]{1,0:T(8,128)(2,1)S(1)} %bitcast.18, bf16[128,1664]{1,0:T(8,128)(2,1)} %collective-permute-done.refs_1_, bf16[128,1664]{1,0:T(8,128)(2,1)} %collective-permute-done.1.refs_2_, ...), custom_call_target="tpu_custom_call", output_to_operand_aliasing={{0}: (8, {})} | custom-call | flops 30000001024 | bytes 1 | tf_op jit(solution)/shard_map/pallas_call | solution.py:167
  48.1 1.0 copy-done
  49.2 4.3 %all-to-all-start = ((bf16[4,640,256]{2,1,0:T(8,128)(2,1)}), bf16[4,640,256]{2,1,0:T(8,128)(2,1)}, u32[]{:S(2)}, u32[]{:S(2)}) async-start(bf16[4,640,256]{2,1,0:T(8,128)(2,1)} %copy-done), calls=%async_computation | async-start | bytes 2621440 | tf_op jit(solution)/shard_map/all_to_all | solution.py:194
  53.5 0.0 collective-permute-done.6.refs_1_.refs_4_
  53.5 1.7 %collective-permute-start.12 = (bf16[1664,128]{1,0:T(8,128)(2,1)}, bf16[1664,128]{1,0:T(8,128)(2,1)}, u32[]{:S(2)}, u32[]{:S(2)}) collective-permute-start(bf16[1664,128]{1,0:T(8,128)(2,1)} %collective-permute-done.11.refs_9_), channel_id=1, source_target_pairs={{0,12},{4,0},{8,4},{12,8},{1,13},{5,1},{9,5},{13,9},{2,14},{6,2},{... | collective-permute-start | bytes 1277960 | tf_op jit(solution)/shard_map/ppermute | solution.py:29
  55.2 1.0 copy-done.6
  56.2 1.0 copy-done.8
  57.2 1.0 copy-done.11
  58.2 5.8 %shard_map.59 = (bf16[384,256]{1,0:T(8,128)(2,1)S(1)}, bf16[384,256]{1,0:T(8,128)(2,1)}, bf16[384,256]{1,0:T(8,128)(2,1)}, bf16[384,256]{1,0:T(8,128)(2,1)}) custom-call(s32[1]{0:T(128)S(6)} %rem.18.shift_ref, bf16[128,1664]{1,0:T(8,128)(2,1)S(1)} %copy-done.8, bf16[128,1664]{1,0:T(8,128)(2,1)} %collective-permute-done.6.refs_1_.refs_4_, ...), custom_call_target="tpu_custom_call" | custom-call | flops 30000001024 | bytes 1 | tf_op jit(solution)/shard_map/pallas_call | solution.py:147
  64.0 0.7 copy-done.2
  64.7 1.4 %collective-permute-start.14 = (bf16[384,256]{1,0:T(8,128)(2,1)}, bf16[384,256]{1,0:T(8,128)(2,1)S(1)}, u32[]{:S(2)}, u32[]{:S(2)}) collective-permute-start(bf16[384,256]{1,0:T(8,128)(2,1)} %get-tuple-element.49), channel_id=1, source_target_pairs={{0,1},{1,2},{2,3},{3,0},{4,5},{5,6},{6,7},{7,4},{8,9},{9,10},{10,1... | collective-permute-start | bytes 589832 | tf_op jit(solution)/shard_map/ppermute | solution.py:29
  66.0 2.6 %collective-permute-start.15 = (bf16[384,256]{1,0:T(8,128)(2,1)}, bf16[384,256]{1,0:T(8,128)(2,1)S(1)}, u32[]{:S(2)}, u32[]{:S(2)}) collective-permute-start(bf16[384,256]{1,0:T(8,128)(2,1)} %get-tuple-element.50), channel_id=1, source_target_pairs={{0,2},{1,3},{2,0},{3,1},{4,6},{5,7},{6,4},{7,5},{8,10},{9,11},{10,... | collective-permute-start | bytes 589832 | tf_op jit(solution)/shard_map/ppermute | solution.py:29
  68.6 1.1 collective-permute-start.16
  69.7 1.6 %reduce_sum.34.refs_0_ = bf16[640,256]{1,0:T(8,128)(2,1)S(1)} reduce(bf16[4,640,256]{2,1,0:T(8,128)(2,1)} %all-to-all-done, bf16[]{:T(256)} %constant.28.clone.1), dimensions={0}, to_apply=%region_1.0 | reduce | flops 491520 | bytes 1638402 | tf_op jit(solution)/shard_map/reduce_sum | solution.py:198
  71.3 0.1 collective-permute-start.17
  71.4 1.4 %collective-permute-start.18 = (bf16[640,256]{1,0:T(8,128)(2,1)S(1)}, bf16[640,256]{1,0:T(8,128)(2,1)S(1)}, u32[]{:S(2)}, u32[]{:S(2)}) collective-permute-start(bf16[640,256]{1,0:T(8,128)(2,1)S(1)} %reduce_sum.34.refs_0_), channel_id=1, source_target_pairs={{0,4},{4,8},{8,12},{12,0},{1,5},{5,9},{9,13},{13,1},{2,6},{6,10},{... | collective-permute-start | bytes 983048 | tf_op jit(solution)/shard_map/ppermute | solution.py:29
  72.9 7.7 %shard_map.62 = (bf16[4,1024,128]{2,1,0:T(8,128)(2,1)}, f32[8,128]{1,0:T(8,128)}) custom-call(s32[1]{0:T(128)} %bitcast.1.x_ref, bf16[128,1664]{1,0:T(8,128)(2,1)S(1)} %bitcast.19, bf16[128,1664]{1,0:T(8,128)(2,1)} %collective-permute-done.refs_1_, bf16[128,1664]{1,0:T(8,128)(2,1)} %collective-permute-done.1.refs_2_, bf16[128,1664]{1,0:T(8,128)(2,1)S(1)} %copy-done.9, ...), custom_call_target="tpu_custom_call" | custom-call | flops 30000001024 | bytes 1 | tf_op jit(solution)/shard_map/pallas_call | solution.py:167
  80.7 0.1 add_convert_fusion.refs_4_
  80.8 0.0 copy-start.4
  80.8 4.3 %all-to-all-start.1 = ((bf16[4,1024,128]{2,1,0:T(8,128)(2,1)}), bf16[4,1024,128]{2,1,0:T(8,128)(2,1)}, u32[]{:S(2)}, u32[]{:S(2)}) async-start(bf16[4,1024,128]{2,1,0:T(8,128)(2,1)} %get-tuple-element.55), calls=%async_computation.1 | async-start | bytes 2097152 | tf_op jit(solution)/shard_map/all_to_all | solution.py:194
  85.1 1.4 %collective-permute-start.19 = (bf16[640,256]{1,0:T(8,128)(2,1)S(1)}, bf16[640,256]{1,0:T(8,128)(2,1)S(1)}, u32[]{:S(2)}, u32[]{:S(2)}) collective-permute-start(bf16[640,256]{1,0:T(8,128)(2,1)S(1)} %collective-permute-done.17.refs_1_), channel_id=1, source_target_pairs={{0,12},{4,0},{8,4},{12,8},{1,13},{5,1},{9,5},{13,9},{2,14},{6,2},{... | collective-permute-start | bytes 983048 | tf_op jit(solution)/shard_map/ppermute | solution.py:29
  86.4 0.1 collective-permute-start.20
  86.5 1.9 %collective-permute-start.21 = (bf16[384,256]{1,0:T(8,128)(2,1)S(1)}, bf16[384,256]{1,0:T(8,128)(2,1)S(1)}, u32[]{:S(2)}, u32[]{:S(2)}) collective-permute-start(bf16[384,256]{1,0:T(8,128)(2,1)S(1)} %add_convert_fusion.refs_4_), channel_id=1, source_target_pairs={{0,8},{4,12},{8,0},{12,4},{1,9},{5,13},{9,1},{13,5},{2,10},{6,14},... | collective-permute-start | bytes 589832 | tf_op jit(solution)/shard_map/ppermute | solution.py:29
  88.4 0.0 collective-permute-start.22
  88.4 6.5 %all-to-all-done.1 = bf16[4,1024,128]{2,1,0:T(8,128)(2,1)} async-done(((bf16[4,1024,128]{2,1,0:T(8,128)(2,1)}), bf16[4,1024,128]{2,1,0:T(8,128)(2,1)}, u32[]{:S(2)}, u32[]{:S(2)}) %all-to-all-start.1) | async-done | bytes 1048608 | tf_op jit(solution)/shard_map/all_to_all | solution.py:194
  94.9 1.5 %reduce_sum.35.q_ref = bf16[1024,128]{1,0:T(8,128)(2,1)S(1)} reduce(bf16[4,1024,128]{2,1,0:T(8,128)(2,1)} %all-to-all-done.1, bf16[]{:T(256)} %constant.28.clone.1), dimensions={0}, to_apply=%region_2.0 | reduce | flops 393216 | bytes 1310722 | tf_op jit(solution)/shard_map/reduce_sum | solution.py:198
  96.4 2.9 %shard_map.63 = bf16[1024,128]{1,0:T(8,128)(2,1)S(1)} custom-call(s32[1]{0:T(128)} %bitcast.1.x_ref, s32[1]{0:T(128)} %bitcast.2.z_ref, s32[3]{0:T(128)S(1)} %convert_reduce_fusion.bound_ref, s32[32]{0:T(128)S(1)} %bitcast.20, bf16[1024,128]{1,0:T(8,128)(2,1)S(1)} %reduce_sum.35.q_ref, bf16[640,256]{1,0:T(8,128)(2,1)S(1)} %reduce_sum.34.refs_0_, ...), custom_call_target="tpu_custom_call" | custom-call | flops 1 | bytes 1 | tf_op jit(solution)/shard_map/pallas_call | solution.py:274
  99.3 0.7 collective-permute-start.23
  100.0 2.4 %collective-permute-start.24 = (bf16[256,128]{1,0:T(8,128)(2,1)S(1)}, bf16[256,128]{1,0:T(8,128)(2,1)S(1)}, u32[]{:S(2)}, u32[]{:S(2)}) collective-permute-start(bf16[256,128]{1,0:T(8,128)(2,1)S(1)} %get-tuple-element.63), channel_id=1, source_target_pairs={{0,1},{1,5},{2,9},{3,13},{4,2},{5,6},{6,10},{7,14},{8,3},{9,7},{10... | collective-permute-start | bytes 196616 | tf_op jit(solution)/shard_map/ppermute | solution.py:337
  102.4 4.0 %collective-permute-start.25 = (bf16[256,128]{1,0:T(8,128)(2,1)S(1)}, bf16[256,128]{1,0:T(8,128)(2,1)S(1)}, u32[]{:S(2)}, u32[]{:S(2)}) collective-permute-start(bf16[256,128]{1,0:T(8,128)(2,1)S(1)} %get-tuple-element.62), channel_id=1, source_target_pairs={{0,2},{1,6},{2,10},{3,14},{4,3},{5,7},{6,11},{7,15},{8,0},{9,4},{1... | collective-permute-start | bytes 196616 | tf_op jit(solution)/shard_map/ppermute | solution.py:337
  106.5 1.8 %collective-permute-start.26 = (bf16[256,128]{1,0:T(8,128)(2,1)S(1)}, bf16[256,128]{1,0:T(8,128)(2,1)S(1)}, u32[]{:S(2)}, u32[]{:S(2)}) collective-permute-start(bf16[256,128]{1,0:T(8,128)(2,1)S(1)} %get-tuple-element.61), channel_id=1, source_target_pairs={{0,3},{1,7},{2,11},{3,15},{4,0},{5,4},{6,8},{7,12},{8,1},{9,5},{10... | collective-permute-start | bytes 196616 | tf_op jit(solution)/shard_map/ppermute | solution.py:337
  108.3 3.0 %collective-permute-done.25.refs_2_ = bf16[256,128]{1,0:T(8,128)(2,1)S(1)} collective-permute-done((bf16[256,128]{1,0:T(8,128)(2,1)S(1)}, bf16[256,128]{1,0:T(8,128)(2,1)S(1)}, u32[]{:S(2)}, u32[]{:S(2)}) %collective-permute-start.25) | collective-permute-done | bytes 65568 | tf_op jit(solution)/shard_map/ppermute | solution.py:337
  111.3 0.5 collective-permute-done.26.refs_3_
  111.8 0.1 copy-done.14
  111.9 0.6 copy-done.15
  112.6 1.8 %shard_map.64 = (bf16[1024,128]{1,0:T(8,128)(2,1)}, bf16[1024,128]{1,0:T(8,128)(2,1)}) custom-call(s32[1]{0:T(128)} %bitcast.y_ref, bf16[256,128]{1,0:T(8,128)(2,1)} %copy-done.12, bf16[256,128]{1,0:T(8,128)(2,1)} %copy-done.13, bf16[256,128]{1,0:T(8,128)(2,1)} %copy-done.14, bf16[256,128]{1,0:T(8,128)(2,1)} %copy-done.15), custom_call_target="tpu_custom_call" | custom-call | tf_op jit(solution)/shard_map/pallas_call | solution.py:297
  114.4 12.7 %collective-permute-start.27 = (bf16[1024,128]{1,0:T(8,128)(2,1)}, bf16[1024,128]{1,0:T(8,128)(2,1)S(1)}, u32[]{:S(2)}, u32[]{:S(2)}) collective-permute-start(bf16[1024,128]{1,0:T(8,128)(2,1)} %get-tuple-element.57), channel_id=1, source_target_pairs={{0,128},{128,0},{1,129},{129,1},{2,130},{130,2},{3,131},{131,3},{4... | collective-permute-start | bytes 786440 | tf_op jit(solution)/shard_map/ppermute | solution.py:29
  127.1 1.4 %collective-permute-done.27 = bf16[1024,128]{1,0:T(8,128)(2,1)S(1)} collective-permute-done((bf16[1024,128]{1,0:T(8,128)(2,1)}, bf16[1024,128]{1,0:T(8,128)(2,1)S(1)}, u32[]{:S(2)}, u32[]{:S(2)}) %collective-permute-start.27) | collective-permute-done | bytes 262176 | tf_op jit(solution)/shard_map/ppermute | solution.py:29
  128.4 0.7 copy.9
  (47 shorter events, 0.2 us)
Async XLA Ops:
  2.0 3.5 %copy-start.1 = (bf16[1,128,1664]{2,1,0:T(8,128)(2,1)S(1)}, bf16[1,128,1664]{2,1,0:T(8,128)(2,1)}, u32[]{:S(2)}) copy-start(bf16[1,128,1664]{2,1,0:T(8,128)(2,1)} %param.4) | copy-start | bytes 1277956
  2.0 21.1 %copy-start.16 = (s32[1,4096]{1,0:T(1,128)S(1)}, s32[1,4096]{1,0:T(1,128)}, u32[]{:S(2)}) copy-start(s32[1,4096]{1,0:T(1,128)} %param.6) | copy-start | bytes 49156
  2.1 21.2 %collective-permute-start.7 = (bf16[1664,256]{1,0:T(8,128)(2,1)S(1)}, bf16[1664,256]{1,0:T(8,128)(2,1)S(1)}, u32[]{:S(2)}, u32[]{:S(2)}) collective-permute-start(bf16[1664,256]{1,0:T(8,128)(2,1)S(1)} %pad_maximum_fusion.refs_3_.refs_5_), channel_id=1, source_target_pairs={{0,12},{4,0},{8,4},{12,8},{1,13},{5,1},{9,5},{13,9},{2,14},{6,2},{... | collective-permute-start | bytes 2555912 | tf_op jit(solution)/shard_map/ppermute | solution.py:29
  5.5 14.9 %collective-permute-start.3 = (bf16[128,1664]{1,0:T(8,128)(2,1)S(1)}, bf16[128,1664]{1,0:T(8,128)(2,1)}, u32[]{:S(2)}, u32[]{:S(2)}) collective-permute-start(bf16[128,1664]{1,0:T(8,128)(2,1)S(1)} %bitcast.15), channel_id=1, source_target_pairs={{0,16},{16,32},{32,48},{48,64},{64,80},{80,96},{96,112},{112,0},{1... | collective-permute-start | bytes 1277960 | tf_op jit(solution)/shard_map/ppermute | solution.py:29
  7.1 13.3 %collective-permute-start = (bf16[128,1664]{1,0:T(8,128)(2,1)S(1)}, bf16[128,1664]{1,0:T(8,128)(2,1)}, u32[]{:S(2)}, u32[]{:S(2)}) collective-permute-start(bf16[128,1664]{1,0:T(8,128)(2,1)S(1)} %bitcast.16), channel_id=1, source_target_pairs={{0,112},{16,0},{32,16},{48,32},{64,48},{80,64},{96,80},{112,96},{1... | collective-permute-start | bytes 1277960 | tf_op jit(solution)/shard_map/ppermute | solution.py:29
  11.1 23.3 %collective-permute-start.9 = (bf16[1664,256]{1,0:T(8,128)(2,1)S(1)}, bf16[1664,256]{1,0:T(8,128)(2,1)S(1)}, u32[]{:S(2)}, u32[]{:S(2)}) collective-permute-start(bf16[1664,256]{1,0:T(8,128)(2,1)S(1)} %pad_maximum_fusion.refs_3_.refs_5_), channel_id=1, source_target_pairs={{0,4},{4,8},{8,12},{12,0},{1,5},{5,9},{9,13},{13,1},{2,6},{6,10},{... | collective-permute-start | bytes 2555912 | tf_op jit(solution)/shard_map/ppermute | solution.py:29
  20.4 11.3 %collective-permute-start.4 = (bf16[128,1664]{1,0:T(8,128)(2,1)}, bf16[128,1664]{1,0:T(8,128)(2,1)}, u32[]{:S(2)}, u32[]{:S(2)}) collective-permute-start(bf16[128,1664]{1,0:T(8,128)(2,1)} %collective-permute-done.3.refs_4_.refs_7_), channel_id=1, source_target_pairs={{0,16},{16,32},{32,48},{48,64},{64,80},{80,96},{96,112},{112,0},{1... | collective-permute-start | bytes 1277960 | tf_op jit(solution)/shard_map/ppermute | solution.py:29
  20.4 11.3 %collective-permute-start.1 = (bf16[128,1664]{1,0:T(8,128)(2,1)}, bf16[128,1664]{1,0:T(8,128)(2,1)}, u32[]{:S(2)}, u32[]{:S(2)}) collective-permute-start(bf16[128,1664]{1,0:T(8,128)(2,1)} %collective-permute-done.refs_1_), channel_id=1, source_target_pairs={{0,112},{16,0},{32,16},{48,32},{64,48},{80,64},{96,80},{112,96},{1... | collective-permute-start | bytes 1277960 | tf_op jit(solution)/shard_map/ppermute | solution.py:29
  23.3 20.0 %collective-permute-start.8 = (bf16[896,256]{1,0:T(8,128)(2,1)S(1)}, bf16[896,256]{1,0:T(8,128)(2,1)S(1)}, u32[]{:S(2)}, u32[]{:S(2)}) collective-permute-start(bf16[896,256]{1,0:T(8,128)(2,1)S(1)} %slice.30), channel_id=1, source_target_pairs={{0,12},{4,0},{8,4},{12,8},{1,13},{5,1},{9,5},{13,9},{2,14},{6,2},{... | collective-permute-start | bytes 1376264 | tf_op jit(solution)/shard_map/ppermute | solution.py:29
  31.7 10.4 %collective-permute-start.5 = (bf16[128,1664]{1,0:T(8,128)(2,1)}, bf16[128,1664]{1,0:T(8,128)(2,1)}, u32[]{:S(2)}, u32[]{:S(2)}) collective-permute-start(bf16[128,1664]{1,0:T(8,128)(2,1)} %collective-permute-done.4.refs_3_.refs_6_), channel_id=1, source_target_pairs={{0,16},{16,32},{32,48},{48,64},{64,80},{80,96},{96,112},{112,0},{1... | collective-permute-start | bytes 1277960 | tf_op jit(solution)/shard_map/ppermute | solution.py:29
  31.7 10.4 %collective-permute-start.2 = (bf16[128,1664]{1,0:T(8,128)(2,1)}, bf16[128,1664]{1,0:T(8,128)(2,1)S(1)}, u32[]{:S(2)}, u32[]{:S(2)}) collective-permute-start(bf16[128,1664]{1,0:T(8,128)(2,1)} %collective-permute-done.1.refs_2_), channel_id=1, source_target_pairs={{0,112},{16,0},{32,16},{48,32},{64,48},{80,64},{96,80},{112,96},{1... | collective-permute-start | bytes 1277960 | tf_op jit(solution)/shard_map/ppermute | solution.py:29
  34.4 9.0 %collective-permute-start.10 = (bf16[768,256]{1,0:T(8,128)(2,1)S(1)}, bf16[768,256]{1,0:T(8,128)(2,1)S(1)}, u32[]{:S(2)}, u32[]{:S(2)}) collective-permute-start(bf16[768,256]{1,0:T(8,128)(2,1)S(1)} %slice.31), channel_id=1, source_target_pairs={{0,4},{4,8},{8,12},{12,0},{1,5},{5,9},{9,13},{13,1},{2,6},{6,10},{... | collective-permute-start | bytes 1179656 | tf_op jit(solution)/shard_map/ppermute | solution.py:29
  42.1 6.0 %copy-start.7 = (bf16[128,1664]{1,0:T(8,128)(2,1)}, bf16[128,1664]{1,0:T(8,128)(2,1)S(1)}, u32[]{:S(2)}) copy-start(bf16[128,1664]{1,0:T(8,128)(2,1)S(1)} %collective-permute-done.2.refs_0_.refs_3_) | copy-start | bytes 1277956
  42.1 11.4 %collective-permute-start.6 = (bf16[128,1664]{1,0:T(8,128)(2,1)}, bf16[128,1664]{1,0:T(8,128)(2,1)}, u32[]{:S(2)}, u32[]{:S(2)}) collective-permute-start(bf16[128,1664]{1,0:T(8,128)(2,1)} %collective-permute-done.5.refs_2_.refs_5_), channel_id=1, source_target_pairs={{0,16},{16,32},{32,48},{48,64},{64,80},{80,96},{96,112},{112,0},{1... | collective-permute-start | bytes 1277960 | tf_op jit(solution)/shard_map/ppermute | solution.py:29
  43.4 4.7 %copy-start.10 = (bf16[768,256]{1,0:T(8,128)(2,1)}, bf16[768,256]{1,0:T(8,128)(2,1)S(1)}, u32[]{:S(2)}) copy-start(bf16[768,256]{1,0:T(8,128)(2,1)S(1)} %collective-permute-done.10.refs_7_.refs_6_) | copy-start | bytes 1179652
  43.4 4.7 %copy-start.5 = (bf16[896,256]{1,0:T(8,128)(2,1)}, bf16[896,256]{1,0:T(8,128)(2,1)S(1)}, u32[]{:S(2)}) copy-start(bf16[896,256]{1,0:T(8,128)(2,1)S(1)} %collective-permute-done.8.refs_6_.refs_5_) | copy-start | bytes 1376260
  43.4 10.1 %collective-permute-start.11 = (bf16[1664,128]{1,0:T(8,128)(2,1)S(1)}, bf16[1664,128]{1,0:T(8,128)(2,1)}, u32[]{:S(2)}, u32[]{:S(2)}) collective-permute-start(bf16[1664,128]{1,0:T(8,128)(2,1)S(1)} %get-tuple-element.44.refs_8_), channel_id=1, source_target_pairs={{0,12},{4,0},{8,4},{12,8},{1,13},{5,1},{9,5},{13,9},{2,14},{6,2},{... | collective-permute-start | bytes 1277960 | tf_op jit(solution)/shard_map/ppermute | solution.py:29
  43.9 27.4 %collective-permute-start.13 = (bf16[1664,128]{1,0:T(8,128)(2,1)S(1)}, bf16[1664,128]{1,0:T(8,128)(2,1)}, u32[]{:S(2)}, u32[]{:S(2)}) collective-permute-start(bf16[1664,128]{1,0:T(8,128)(2,1)S(1)} %get-tuple-element.44.refs_8_), channel_id=1, source_target_pairs={{0,4},{4,8},{8,12},{12,0},{1,5},{5,9},{9,13},{13,1},{2,6},{6,10},{... | collective-permute-start | bytes 1277960 | tf_op jit(solution)/shard_map/ppermute | solution.py:29
  48.1 1.1 copy-start
  49.2 20.5 %all-to-all-start = ((bf16[4,640,256]{2,1,0:T(8,128)(2,1)}), bf16[4,640,256]{2,1,0:T(8,128)(2,1)}, u32[]{:S(2)}, u32[]{:S(2)}) async-start(bf16[4,640,256]{2,1,0:T(8,128)(2,1)} %copy-done), calls=%async_computation | async-start | bytes 2621440 | tf_op jit(solution)/shard_map/all_to_all | solution.py:194
  53.5 18.0 %collective-permute-start.12 = (bf16[1664,128]{1,0:T(8,128)(2,1)}, bf16[1664,128]{1,0:T(8,128)(2,1)}, u32[]{:S(2)}, u32[]{:S(2)}) collective-permute-start(bf16[1664,128]{1,0:T(8,128)(2,1)} %collective-permute-done.11.refs_9_), channel_id=1, source_target_pairs={{0,12},{4,0},{8,4},{12,8},{1,13},{5,1},{9,5},{13,9},{2,14},{6,2},{... | collective-permute-start | bytes 1277960 | tf_op jit(solution)/shard_map/ppermute | solution.py:29
  55.2 1.0 copy-start.6
  56.2 1.0 copy-start.8
  57.2 1.0 copy-start.11
  64.0 0.7 copy-start.2
  64.7 8.2 %copy-start.9 = (bf16[128,1664]{1,0:T(8,128)(2,1)S(1)}, bf16[128,1664]{1,0:T(8,128)(2,1)}, u32[]{:S(2)}) copy-start(bf16[128,1664]{1,0:T(8,128)(2,1)} %copy-done.7) | copy-start | bytes 1277956
  64.7 16.0 %collective-permute-start.14 = (bf16[384,256]{1,0:T(8,128)(2,1)}, bf16[384,256]{1,0:T(8,128)(2,1)S(1)}, u32[]{:S(2)}, u32[]{:S(2)}) collective-permute-start(bf16[384,256]{1,0:T(8,128)(2,1)} %get-tuple-element.49), channel_id=1, source_target_pairs={{0,1},{1,2},{2,3},{3,0},{4,5},{5,6},{6,7},{7,4},{8,9},{9,10},{10,1... | collective-permute-start | bytes 589832 | tf_op jit(solution)/shard_map/ppermute | solution.py:29
  66.0 14.6 %collective-permute-start.15 = (bf16[384,256]{1,0:T(8,128)(2,1)}, bf16[384,256]{1,0:T(8,128)(2,1)S(1)}, u32[]{:S(2)}, u32[]{:S(2)}) collective-permute-start(bf16[384,256]{1,0:T(8,128)(2,1)} %get-tuple-element.50), channel_id=1, source_target_pairs={{0,2},{1,3},{2,0},{3,1},{4,6},{5,7},{6,4},{7,5},{8,10},{9,11},{10,... | collective-permute-start | bytes 589832 | tf_op jit(solution)/shard_map/ppermute | solution.py:29
  68.6 12.0 %collective-permute-start.16 = (bf16[384,256]{1,0:T(8,128)(2,1)}, bf16[384,256]{1,0:T(8,128)(2,1)S(1)}, u32[]{:S(2)}, u32[]{:S(2)}) collective-permute-start(bf16[384,256]{1,0:T(8,128)(2,1)} %get-tuple-element.51), channel_id=1, source_target_pairs={{0,3},{1,0},{2,1},{3,2},{4,7},{5,4},{6,5},{7,6},{8,11},{9,8},{10,9... | collective-permute-start | bytes 589832 | tf_op jit(solution)/shard_map/ppermute | solution.py:29
  71.3 9.4 %collective-permute-start.17 = (bf16[640,256]{1,0:T(8,128)(2,1)S(1)}, bf16[640,256]{1,0:T(8,128)(2,1)S(1)}, u32[]{:S(2)}, u32[]{:S(2)}) collective-permute-start(bf16[640,256]{1,0:T(8,128)(2,1)S(1)} %reduce_sum.34.refs_0_), channel_id=1, source_target_pairs={{0,12},{4,0},{8,4},{12,8},{1,13},{5,1},{9,5},{13,9},{2,14},{6,2},{... | collective-permute-start | bytes 983048 | tf_op jit(solution)/shard_map/ppermute | solution.py:29
  71.4 9.4 %collective-permute-start.18 = (bf16[640,256]{1,0:T(8,128)(2,1)S(1)}, bf16[640,256]{1,0:T(8,128)(2,1)S(1)}, u32[]{:S(2)}, u32[]{:S(2)}) collective-permute-start(bf16[640,256]{1,0:T(8,128)(2,1)S(1)} %reduce_sum.34.refs_0_), channel_id=1, source_target_pairs={{0,4},{4,8},{8,12},{12,0},{1,5},{5,9},{9,13},{13,1},{2,6},{6,10},{... | collective-permute-start | bytes 983048 | tf_op jit(solution)/shard_map/ppermute | solution.py:29
  72.9 7.8 %copy-start.3 = (bf16[384,256]{1,0:T(8,128)(2,1)S(1)}, bf16[384,256]{1,0:T(8,128)(2,1)}, u32[]{:S(2)}) copy-start(bf16[384,256]{1,0:T(8,128)(2,1)} %copy-done.2) | copy-start | bytes 589828
  80.8 15.6 %copy-start.4 = (s32[1,32]{1,0:T(1,128)S(1)}, s32[1,32]{1,0:T(1,128)}, u32[]{:S(2)}) copy-start(s32[1,32]{1,0:T(1,128)} %param.7) | copy-start | bytes 388
  80.8 14.1 %all-to-all-start.1 = ((bf16[4,1024,128]{2,1,0:T(8,128)(2,1)}), bf16[4,1024,128]{2,1,0:T(8,128)(2,1)}, u32[]{:S(2)}, u32[]{:S(2)}) async-start(bf16[4,1024,128]{2,1,0:T(8,128)(2,1)} %get-tuple-element.55), calls=%async_computation.1 | async-start | bytes 2097152 | tf_op jit(solution)/shard_map/all_to_all | solution.py:194
  85.1 11.3 %collective-permute-start.19 = (bf16[640,256]{1,0:T(8,128)(2,1)S(1)}, bf16[640,256]{1,0:T(8,128)(2,1)S(1)}, u32[]{:S(2)}, u32[]{:S(2)}) collective-permute-start(bf16[640,256]{1,0:T(8,128)(2,1)S(1)} %collective-permute-done.17.refs_1_), channel_id=1, source_target_pairs={{0,12},{4,0},{8,4},{12,8},{1,13},{5,1},{9,5},{13,9},{2,14},{6,2},{... | collective-permute-start | bytes 983048 | tf_op jit(solution)/shard_map/ppermute | solution.py:29
  86.4 9.9 %collective-permute-start.20 = (bf16[384,256]{1,0:T(8,128)(2,1)S(1)}, bf16[384,256]{1,0:T(8,128)(2,1)S(1)}, u32[]{:S(2)}, u32[]{:S(2)}) collective-permute-start(bf16[384,256]{1,0:T(8,128)(2,1)S(1)} %add_convert_fusion.refs_4_), channel_id=1, source_target_pairs={{0,12},{4,0},{8,4},{12,8},{1,13},{5,1},{9,5},{13,9},{2,14},{6,2},{... | collective-permute-start | bytes 589832 | tf_op jit(solution)/shard_map/ppermute | solution.py:29
  86.5 9.8 %collective-permute-start.21 = (bf16[384,256]{1,0:T(8,128)(2,1)S(1)}, bf16[384,256]{1,0:T(8,128)(2,1)S(1)}, u32[]{:S(2)}, u32[]{:S(2)}) collective-permute-start(bf16[384,256]{1,0:T(8,128)(2,1)S(1)} %add_convert_fusion.refs_4_), channel_id=1, source_target_pairs={{0,8},{4,12},{8,0},{12,4},{1,9},{5,13},{9,1},{13,5},{2,10},{6,14},... | collective-permute-start | bytes 589832 | tf_op jit(solution)/shard_map/ppermute | solution.py:29
  88.4 8.0 %collective-permute-start.22 = (bf16[384,256]{1,0:T(8,128)(2,1)S(1)}, bf16[384,256]{1,0:T(8,128)(2,1)S(1)}, u32[]{:S(2)}, u32[]{:S(2)}) collective-permute-start(bf16[384,256]{1,0:T(8,128)(2,1)S(1)} %add_convert_fusion.refs_4_), channel_id=1, source_target_pairs={{0,4},{4,8},{8,12},{12,0},{1,5},{5,9},{9,13},{13,1},{2,6},{6,10},{... | collective-permute-start | bytes 589832 | tf_op jit(solution)/shard_map/ppermute | solution.py:29
  99.3 9.0 %collective-permute-start.23 = (bf16[256,128]{1,0:T(8,128)(2,1)S(1)}, bf16[256,128]{1,0:T(8,128)(2,1)S(1)}, u32[]{:S(2)}, u32[]{:S(2)}) collective-permute-start(bf16[256,128]{1,0:T(8,128)(2,1)S(1)} %get-tuple-element.64), channel_id=1, source_target_pairs={{0,0},{1,4},{2,8},{3,12},{4,1},{5,5},{6,9},{7,13},{8,2},{9,6},{10,... | collective-permute-start | bytes 196616 | tf_op jit(solution)/shard_map/ppermute | solution.py:337
  100.0 8.3 %collective-permute-start.24 = (bf16[256,128]{1,0:T(8,128)(2,1)S(1)}, bf16[256,128]{1,0:T(8,128)(2,1)S(1)}, u32[]{:S(2)}, u32[]{:S(2)}) collective-permute-start(bf16[256,128]{1,0:T(8,128)(2,1)S(1)} %get-tuple-element.63), channel_id=1, source_target_pairs={{0,1},{1,5},{2,9},{3,13},{4,2},{5,6},{6,10},{7,14},{8,3},{9,7},{10... | collective-permute-start | bytes 196616 | tf_op jit(solution)/shard_map/ppermute | solution.py:337
  102.4 8.9 %collective-permute-start.25 = (bf16[256,128]{1,0:T(8,128)(2,1)S(1)}, bf16[256,128]{1,0:T(8,128)(2,1)S(1)}, u32[]{:S(2)}, u32[]{:S(2)}) collective-permute-start(bf16[256,128]{1,0:T(8,128)(2,1)S(1)} %get-tuple-element.62), channel_id=1, source_target_pairs={{0,2},{1,6},{2,10},{3,14},{4,3},{5,7},{6,11},{7,15},{8,0},{9,4},{1... | collective-permute-start | bytes 196616 | tf_op jit(solution)/shard_map/ppermute | solution.py:337
  106.5 5.4 %collective-permute-start.26 = (bf16[256,128]{1,0:T(8,128)(2,1)S(1)}, bf16[256,128]{1,0:T(8,128)(2,1)S(1)}, u32[]{:S(2)}, u32[]{:S(2)}) collective-permute-start(bf16[256,128]{1,0:T(8,128)(2,1)S(1)} %get-tuple-element.61), channel_id=1, source_target_pairs={{0,3},{1,7},{2,11},{3,15},{4,0},{5,4},{6,8},{7,12},{8,1},{9,5},{10... | collective-permute-start | bytes 196616 | tf_op jit(solution)/shard_map/ppermute | solution.py:337
  108.3 3.5 %copy-start.12 = (bf16[256,128]{1,0:T(8,128)(2,1)}, bf16[256,128]{1,0:T(8,128)(2,1)S(1)}, u32[]{:S(2)}) copy-start(bf16[256,128]{1,0:T(8,128)(2,1)S(1)} %collective-permute-done.23.refs_0_) | copy-start | bytes 196612
  108.3 3.5 %copy-start.13 = (bf16[256,128]{1,0:T(8,128)(2,1)}, bf16[256,128]{1,0:T(8,128)(2,1)S(1)}, u32[]{:S(2)}) copy-start(bf16[256,128]{1,0:T(8,128)(2,1)S(1)} %collective-permute-done.24.refs_1_) | copy-start | bytes 196612
  111.3 0.6 copy-start.14
  111.9 0.6 copy-start.15
  114.4 14.1 %collective-permute-start.27 = (bf16[1024,128]{1,0:T(8,128)(2,1)}, bf16[1024,128]{1,0:T(8,128)(2,1)S(1)}, u32[]{:S(2)}, u32[]{:S(2)}) collective-permute-start(bf16[1024,128]{1,0:T(8,128)(2,1)} %get-tuple-element.57), channel_id=1, source_target_pairs={{0,128},{128,0},{1,129},{129,1},{2,130},{130,2},{3,131},{131,3},{4... | collective-permute-start | bytes 786440 | tf_op jit(solution)/shard_map/ppermute | solution.py:29

commit v4 on v3

--- a/solution.py
+++ b/solution.py
@@ -19,7 +19,7 @@
 BRIEF = pl.CostEstimate(flops=1, bytes_accessed=1, transcendentals=0)
 LONG = pl.CostEstimate(flops=3 * 10**10, bytes_accessed=1, transcendentals=0)
 VMEM = pl.BlockSpec(memory_space=pltpu.VMEM)
-FAR = pl.BlockSpec(memory_space=pltpu.HBM)
+FAR = pl.BlockSpec(memory_space=pl.ANY)
 SMEM = pl.BlockSpec(memory_space=pltpu.SMEM)
 LIMIT = pltpu.CompilerParams(vmem_limit_bytes=32 * 2**20)
 
@@ -74,9 +74,7 @@
     for copies in [row_loads] + slot_loads:
         for copy in copies:
             copy.start()
-    for copy in row_loads:
-        copy.wait()
-    return slot_loads
+    return row_loads, slot_loads
 
 
 def cut_by(counts, refs):
@@ -88,17 +86,28 @@
 
 
 def products(pieces, weights, columns, rows, wide, sems):
-    slot_loads = loads_of(pieces, weights, columns, rows, wide, sems)
+    row_loads, slot_loads = loads_of(pieces, weights, columns, rows, wide, sems)
     per_tile = 256 // columns
+    cut = 4 if len(pieces) == 8 else len(pieces)
+    middle = sum(piece.shape[0] for piece in pieces[:cut])
+    parts = [(slice(0, middle), row_loads[:cut])]
+    if middle < rows.shape[0]:
+        parts.append((slice(middle, rows.shape[0]), row_loads[cut:]))
     for tile in range(len(weights) // per_tile):
         inside = range(tile * per_tile, (tile + 1) * per_tile)
         for i in inside:
             for copy in slot_loads[i]:
                 copy.wait()
-        product = jnp.dot(rows[...], wide[tile], preferred_element_type=jnp.float32)
-        for i in inside:
-            begin = i * columns % 256
-            yield i, product[:, begin : begin + columns].astype(jnp.bfloat16)
+        for part, copies in parts:
+            if tile == 0:
+                for copy in copies:
+                    copy.wait()
+            product = jnp.dot(rows[part, :], wide[tile], preferred_element_type=jnp.float32)
+            last = part.stop == rows.shape[0]
+            for i in inside:
+                begin = i * columns % 256
+                value = product[:, begin : begin + columns].astype(jnp.bfloat16)
+                yield i, part, last, value
 
 
 def scratch_for(count, width, columns, slots, operands):
@@ -113,13 +122,22 @@
     total = pieces + sum(counts)
     outs = refs[total : total + 4]
     weights = cut_by(counts, refs[pieces:total])
-    for i, product in products(refs[:pieces], weights, columns, *refs[total + 4 :]):
+    rows, wide, sems, stage, out_sems = refs[total + 4 :]
+
+    def for_target(i, act):
         target = lax.rem(slots[i] + shift_ref[0], 4)
         for k in range(4):
 
             @pl.when(target == k)
             def _():
-                outs[k][...] = product
+                act(pltpu.make_async_copy(stage.at[i], outs[k], out_sems.at[i]))
+
+    for i, part, last, value in products(refs[:pieces], weights, columns, rows, wide, sems):
+        stage[i, part, :] = value
+        if last:
+            for_target(i, lambda copy: copy.start())
+    for i in range(4):
+        for_target(i, lambda copy: copy.wait())
 
 
 def project_stack_kernel(x_ref, *refs, pieces, slots, counts, columns, added):
@@ -129,8 +147,10 @@
     rows, wide, sems, stage, out_sems = refs[total + added + 2 :]
     mark[...] = jnp.zeros_like(mark)
     copies = []
-    for i, product in products(refs[:pieces], weights, columns, rows, wide, sems):
-        stage[i] = product
+    for i, part, last, value in products(refs[:pieces], weights, columns, rows, wide, sems):
+        stage[i, part, :] = value
+        if not last:
+            continue
         place = out.at[lax.rem(slots[i] + x_ref[0], 4)]
         copies.append(pltpu.make_async_copy(stage.at[i], place, out_sems.at[i]))
         copies[-1].start()
@@ -149,9 +169,13 @@
             project_kernel, pieces=len(pieces), slots=slots, counts=counts, columns=columns
         ),
         in_specs=[SMEM] + [FAR] * operands,
-        out_specs=[VMEM] * 4,
+        out_specs=[FAR] * 4,
         out_shape=[jax.ShapeDtypeStruct((count, columns), jnp.bfloat16)] * 4,
-        scratch_shapes=scratch_for(count, width, columns, len(slots), operands),
+        scratch_shapes=scratch_for(count, width, columns, len(slots), operands)
+        + [
+            pltpu.VMEM((len(slots), count, columns), jnp.bfloat16),
+            pltpu.SemaphoreType.DMA((len(slots),)),
+        ],
         cost_estimate=LONG,
         compiler_params=LIMIT,
     )(shift, *pieces, *weights)
@@ -278,27 +302,42 @@
         out_shape=jax.ShapeDtypeStruct((rows, HEAD), jnp.bfloat16),
         scratch_shapes=[pltpu.VMEM((4 * rows, HEAD), jnp.bfloat16)] * 2,
         cost_estimate=BRIEF,
-        compiler_params=LIMIT,
+        compiler_params=pltpu.CompilerParams(vmem_limit_bytes=24 * 2**20),
     )(x, z, bounds, flags, query, *early, *late)
 
 
 def place_kernel(y_ref, *refs):
-    parts, outs = refs[:4], refs[4:]
+    parts, outs, whole, sems = refs[:4], refs[4:6], refs[6], refs[7]
+    loads = []
     for s in range(4):
         x = lax.rem(y_ref[0] + 4 - s, 4)
         for t in range(2):
             at = pl.ds(pl.multiple_of((4 * t + x) * BLOCK, BLOCK), BLOCK)
-            for out in outs:
-                out[at, :] = parts[s][t * BLOCK : (t + 1) * BLOCK, :]
+            source = parts[s].at[pl.ds(t * BLOCK, BLOCK)]
+            loads.append(pltpu.make_async_copy(source, whole.at[at], sems.at[2 + len(loads)]))
+    for copy in loads:
+        copy.start()
+    for copy in loads:
+        copy.wait()
+    copies = [pltpu.make_async_copy(whole, out, sems.at[i]) for i, out in enumerate(outs)]
+    for copy in copies:
+        copy.start()
+    for copy in copies:
+        copy.wait()
 
 
 def place(y, parts):
     rows = 4 * parts[0].shape[0]
     return pl.pallas_call(
         place_kernel,
-        in_specs=[SMEM] + [VMEM] * 4,
-        out_specs=[VMEM] * 2,
+        in_specs=[SMEM] + [FAR] * 4,
+        out_specs=[FAR] * 2,
         out_shape=[jax.ShapeDtypeStruct((rows, HEAD), jnp.bfloat16)] * 2,
+        scratch_shapes=[
+            pltpu.VMEM((rows, HEAD), jnp.bfloat16),
+            pltpu.SemaphoreType.DMA((10,)),
+        ],
+        compiler_params=pltpu.CompilerParams(vmem_limit_bytes=58 * 2**20),
     )(y, *parts)
 
 
@@ -342,8 +381,8 @@
         for s in range(4)
     ]
     result, given = place(y, moved)
-    handed = send(given, "phase", 1)
-    return (result[None], handed[None])
+    handed = send(given[None], "phase", 1)
+    return (result[None], handed)
 
 
 def solution(mesh):

time: 130 us -> 128 us (0.985)
  starting transfers between devices: 61.2 us -> 58.9 us
    ppermute x24, starting transfers between devices: 43.7 us -> 41.1 us  [send(): lax.ppermute(block, axis, [(i, (i + distance) % n) for i in range(n)])]
    pallas_call x1, Pallas kernels: 2.9 us -> 4.38 us  [attend(): pl.pallas_call(attend_kernel, in_specs=[SMEM] * 4 + [VMEM] * 9, out_specs...]
  transfers between devices with their start and end apart: 30 -> 30, of which waited for: 8 -> 8; matrix products, arithmetic and copies ran while one was open for 3% -> 3% of each run, Pallas kernels for 18% -> 17%
where the time goes in v4:
time: 128 us; the launch traced here: 127 us
  starting transfers between devices  58.9 us (46%)
  waiting for transfers between devices  28.1 us (22%)
  Pallas kernels  28.1 us (22%)
  local copies, waits for them, and re-layouts  7.53 us (6%)
  other arithmetic  3.53 us (3%)
    ppermute x24, starting transfers between devices, send(): lax.ppermute(block, axis, [(i, (i + distance) % n) for i in range(n)])  41.1 us
    ppermute x24, waiting for transfers between devices, send(): lax.ppermute(block, axis, [(i, (i + distance) % n) for i in range(n)])  18.5 us
    pallas_call x3, Pallas kernels, project_stack(): pl.pallas_call(functools.partial(project_stack_kernel, pieces=len(pieces)...  16.1 us
    ppermute x4, starting transfers between devices, local(): lax.ppermute(mixed[s * quarter:(s + 1) * quarter], ('x', 'y'), [(4 * i +...  9.35 us
    all_to_all x2, starting transfers between devices, exchange(): return lax.all_to_all(stack, axis, 0, 0, tiled=True)  8.55 us
    all_to_all x2, waiting for transfers between devices, exchange(): return lax.all_to_all(stack, axis, 0, 0, tiled=True)  6.4 us
    unnamed x35, local copies, waits for them, and re-layouts  6.11 us
    pallas_call x1, Pallas kernels, project(): pl.pallas_call(functools.partial(project_kernel, pieces=len(pieces), slot...  5.82 us
  transfers between devices with their start and end apart: 30, of which 8 were waited for; matrix products, arithmetic and copies ran while one was open for 3% of the time, Pallas kernels for 17%

profile of v4, /device:TPU:1, one launch (start us, length us, event | category | flops | bytes accessed | tf_op | source)
XLA Modules:
  0.0 127.2 jit_solution(15904954278761759882)
XLA Ops:
  0.6 1.3 %slice_bitcast_fusion.1 = (bf16[1664,128]{1,0:T(8,128)(2,1)S(1)}, bf16[1664,128]{1,0:T(8,128)(2,1)S(1)}, bf16[1664,128]{1,0:T(8,128)(2,1)S(1)}) fusion(bf16[1664,3,128]{2,0,1:T(8,128)(2,1)} %bitcast.21), kind=kLoop, calls=%fused_computation.2 | loop fusion | bytes 2555904 | tf_op jit(solution)/shard_map/squeeze | solution.py:353
  2.0 0.0 copy-start.1
  2.0 0.0 copy-start.16
  2.0 0.1 pad_maximum_fusion.refs_3_.refs_5_
  2.1 3.4 %collective-permute-start.7 = (bf16[1664,256]{1,0:T(8,128)(2,1)S(1)}, bf16[1664,256]{1,0:T(8,128)(2,1)S(1)}, u32[]{:S(2)}, u32[]{:S(2)}) collective-permute-start(bf16[1664,256]{1,0:T(8,128)(2,1)S(1)} %pad_maximum_fusion.refs_3_.refs_5_), channel_id=1, source_target_pairs={{0,12},{4,0},{8,4},{12,8},{1,13},{5,1},{9,5},{13,9},{2,14},{6,2},{... | collective-permute-start | bytes 2555912 | tf_op jit(solution)/shard_map/ppermute | solution.py:29
  5.5 1.6 %collective-permute-start.3 = (bf16[128,1664]{1,0:T(8,128)(2,1)S(1)}, bf16[128,1664]{1,0:T(8,128)(2,1)}, u32[]{:S(2)}, u32[]{:S(2)}) collective-permute-start(bf16[128,1664]{1,0:T(8,128)(2,1)S(1)} %bitcast.15), channel_id=1, source_target_pairs={{0,16},{16,32},{32,48},{48,64},{64,80},{80,96},{96,112},{112,0},{1... | collective-permute-start | bytes 1277960 | tf_op jit(solution)/shard_map/ppermute | solution.py:29
  7.1 3.9 %collective-permute-start = (bf16[128,1664]{1,0:T(8,128)(2,1)S(1)}, bf16[128,1664]{1,0:T(8,128)(2,1)}, u32[]{:S(2)}, u32[]{:S(2)}) collective-permute-start(bf16[128,1664]{1,0:T(8,128)(2,1)S(1)} %bitcast.16), channel_id=1, source_target_pairs={{0,112},{16,0},{32,16},{48,32},{64,48},{80,64},{96,80},{112,96},{1... | collective-permute-start | bytes 1277960 | tf_op jit(solution)/shard_map/ppermute | solution.py:29
  11.1 9.3 %collective-permute-done.3.refs_4_.refs_7_ = bf16[128,1664]{1,0:T(8,128)(2,1)} collective-permute-done((bf16[128,1664]{1,0:T(8,128)(2,1)S(1)}, bf16[128,1664]{1,0:T(8,128)(2,1)}, u32[]{:S(2)}, u32[]{:S(2)}) %collective-permute-start.3) | collective-permute-done | bytes 426016 | tf_op jit(solution)/shard_map/ppermute | solution.py:29
  20.4 0.0 collective-permute-start.4
  20.4 0.0 collective-permute-done.refs_1_
  20.4 2.7 %collective-permute-start.1 = (bf16[128,1664]{1,0:T(8,128)(2,1)}, bf16[128,1664]{1,0:T(8,128)(2,1)}, u32[]{:S(2)}, u32[]{:S(2)}) collective-permute-start(bf16[128,1664]{1,0:T(8,128)(2,1)} %collective-permute-done.refs_1_), channel_id=1, source_target_pairs={{0,112},{16,0},{32,16},{48,32},{64,48},{80,64},{96,80},{112,96},{1... | collective-permute-start | bytes 1277960 | tf_op jit(solution)/shard_map/ppermute | solution.py:29
  23.1 0.2 convert_reduce_fusion.bound_ref
  23.3 0.0 collective-permute-done.7.refs_4_.refs_6_
  23.3 3.3 %collective-permute-start.8 = (bf16[896,256]{1,0:T(8,128)(2,1)S(1)}, bf16[896,256]{1,0:T(8,128)(2,1)S(1)}, u32[]{:S(2)}, u32[]{:S(2)}) collective-permute-start(bf16[896,256]{1,0:T(8,128)(2,1)S(1)} %slice.30), channel_id=1, source_target_pairs={{0,12},{4,0},{8,4},{12,8},{1,13},{5,1},{9,5},{13,9},{2,14},{6,2},{... | collective-permute-start | bytes 1376264 | tf_op jit(solution)/shard_map/ppermute | solution.py:29
  26.6 5.1 %collective-permute-done.4.refs_3_.refs_6_ = bf16[128,1664]{1,0:T(8,128)(2,1)} collective-permute-done((bf16[128,1664]{1,0:T(8,128)(2,1)}, bf16[128,1664]{1,0:T(8,128)(2,1)}, u32[]{:S(2)}, u32[]{:S(2)}) %collective-permute-start.4) | collective-permute-done | bytes 426016 | tf_op jit(solution)/shard_map/ppermute | solution.py:29
  31.7 0.0 collective-permute-done.1.refs_2_
  31.7 2.7 %collective-permute-start.2 = (bf16[128,1664]{1,0:T(8,128)(2,1)}, bf16[128,1664]{1,0:T(8,128)(2,1)S(1)}, u32[]{:S(2)}, u32[]{:S(2)}) collective-permute-start(bf16[128,1664]{1,0:T(8,128)(2,1)} %collective-permute-done.1.refs_2_), channel_id=1, source_target_pairs={{0,112},{16,0},{32,16},{48,32},{64,48},{80,64},{96,80},{112,96},{1... | collective-permute-start | bytes 1277960 | tf_op jit(solution)/shard_map/ppermute | solution.py:29
  34.4 0.0 collective-permute-done.9.refs_5_.refs_7_
  34.4 0.3 collective-permute-start.10
  34.7 6.0 %shard_map.60 = (bf16[4,640,256]{2,1,0:T(8,128)(2,1)S(1)}, f32[8,128]{1,0:T(8,128)}) custom-call(s32[1]{0:T(128)} %bitcast.1.x_ref, bf16[128,1664]{1,0:T(8,128)(2,1)S(1)} %bitcast.17, bf16[128,1664]{1,0:T(8,128)(2,1)} %collective-permute-done.refs_1_, bf16[128,1664]{1,0:T(8,128)(2,1)} %collective-permute-done.1.refs_2_, ...), custom_call_target="tpu_custom_call" | custom-call | flops 1 | bytes 1 | tf_op jit(solution)/shard_map/pallas_call | solution.py:191
  40.7 1.4 %collective-permute-done.5.refs_2_.refs_5_ = bf16[128,1664]{1,0:T(8,128)(2,1)} collective-permute-done((bf16[128,1664]{1,0:T(8,128)(2,1)}, bf16[128,1664]{1,0:T(8,128)(2,1)}, u32[]{:S(2)}, u32[]{:S(2)}) %collective-permute-start.5) | collective-permute-done | bytes 426016 | tf_op jit(solution)/shard_map/ppermute | solution.py:29
  42.1 0.0 collective-permute-start.6
  42.1 1.3 %collective-permute-done.10.refs_7_.refs_6_ = bf16[768,256]{1,0:T(8,128)(2,1)S(1)} collective-permute-done((bf16[768,256]{1,0:T(8,128)(2,1)S(1)}, bf16[768,256]{1,0:T(8,128)(2,1)S(1)}, u32[]{:S(2)}, u32[]{:S(2)}) %collective-permute-start.10) | collective-permute-done | bytes 393248 | tf_op jit(solution)/shard_map/ppermute | solution.py:29
  43.4 0.0 collective-permute-done.8.refs_6_.refs_5_
  43.4 0.5 collective-permute-start.11
  43.9 1.0 collective-permute-start.13
  44.9 3.1 %shard_map.61 = (bf16[4,640,256]{2,1,0:T(8,128)(2,1)S(1)}, f32[8,128]{1,0:T(8,128)}) custom-call(s32[1]{0:T(128)} %bitcast.1.x_ref, bf16[128,1664]{1,0:T(8,128)(2,1)S(1)} %bitcast.18, bf16[128,1664]{1,0:T(8,128)(2,1)} %collective-permute-done.refs_1_, bf16[128,1664]{1,0:T(8,128)(2,1)} %collective-permute-done.1.refs_2_, ...), custom_call_target="tpu_custom_call", output_to_operand_aliasing={{0}: (8, {})} | custom-call | flops 30000001024 | bytes 1 | tf_op jit(solution)/shard_map/pallas_call | solution.py:191
  48.1 1.0 copy-done
  49.2 4.3 %all-to-all-start = ((bf16[4,640,256]{2,1,0:T(8,128)(2,1)}), bf16[4,640,256]{2,1,0:T(8,128)(2,1)}, u32[]{:S(2)}, u32[]{:S(2)}) async-start(bf16[4,640,256]{2,1,0:T(8,128)(2,1)} %copy-done), calls=%async_computation | async-start | bytes 2621440 | tf_op jit(solution)/shard_map/all_to_all | solution.py:218
  53.5 0.0 collective-permute-done.6.refs_1_.refs_4_
  53.5 1.7 %collective-permute-start.12 = (bf16[1664,128]{1,0:T(8,128)(2,1)}, bf16[1664,128]{1,0:T(8,128)(2,1)}, u32[]{:S(2)}, u32[]{:S(2)}) collective-permute-start(bf16[1664,128]{1,0:T(8,128)(2,1)} %collective-permute-done.11.refs_9_), channel_id=1, source_target_pairs={{0,12},{4,0},{8,4},{12,8},{1,13},{5,1},{9,5},{13,9},{2,14},{6,2},{... | collective-permute-start | bytes 1277960 | tf_op jit(solution)/shard_map/ppermute | solution.py:29
  55.2 1.0 copy-done.6
  56.2 1.0 copy-done.8
  57.2 1.0 copy-done.11
  58.2 5.8 %shard_map.59 = (bf16[384,256]{1,0:T(8,128)(2,1)S(1)}, bf16[384,256]{1,0:T(8,128)(2,1)}, bf16[384,256]{1,0:T(8,128)(2,1)}, bf16[384,256]{1,0:T(8,128)(2,1)}) custom-call(s32[1]{0:T(128)S(6)} %rem.18.shift_ref, bf16[128,1664]{1,0:T(8,128)(2,1)S(1)} %copy-done.8, bf16[128,1664]{1,0:T(8,128)(2,1)} %collective-permute-done.6.refs_1_.refs_4_, ...), custom_call_target="tpu_custom_call" | custom-call | flops 30000001024 | bytes 1 | tf_op jit(solution)/shard_map/pallas_call | solution.py:167
  64.1 0.7 copy-done.2
  64.7 1.4 %collective-permute-start.14 = (bf16[384,256]{1,0:T(8,128)(2,1)}, bf16[384,256]{1,0:T(8,128)(2,1)S(1)}, u32[]{:S(2)}, u32[]{:S(2)}) collective-permute-start(bf16[384,256]{1,0:T(8,128)(2,1)} %get-tuple-element.49), channel_id=1, source_target_pairs={{0,1},{1,2},{2,3},{3,0},{4,5},{5,6},{6,7},{7,4},{8,9},{9,10},{10,1... | collective-permute-start | bytes 589832 | tf_op jit(solution)/shard_map/ppermute | solution.py:29
  66.1 2.6 %collective-permute-start.15 = (bf16[384,256]{1,0:T(8,128)(2,1)}, bf16[384,256]{1,0:T(8,128)(2,1)S(1)}, u32[]{:S(2)}, u32[]{:S(2)}) collective-permute-start(bf16[384,256]{1,0:T(8,128)(2,1)} %get-tuple-element.50), channel_id=1, source_target_pairs={{0,2},{1,3},{2,0},{3,1},{4,6},{5,7},{6,4},{7,5},{8,10},{9,11},{10,... | collective-permute-start | bytes 589832 | tf_op jit(solution)/shard_map/ppermute | solution.py:29
  68.7 0.4 collective-permute-start.16
  69.1 1.6 %reduce_sum.34.refs_0_ = bf16[640,256]{1,0:T(8,128)(2,1)S(1)} reduce(bf16[4,640,256]{2,1,0:T(8,128)(2,1)} %all-to-all-done, bf16[]{:T(256)} %constant.28.clone.1), dimensions={0}, to_apply=%region_1.0 | reduce | flops 491520 | bytes 1638402 | tf_op jit(solution)/shard_map/reduce_sum | solution.py:222
  70.8 0.7 collective-permute-start.17
  71.5 0.8 collective-permute-start.18
  72.3 6.9 %shard_map.62 = (bf16[4,1024,128]{2,1,0:T(8,128)(2,1)}, f32[8,128]{1,0:T(8,128)}) custom-call(s32[1]{0:T(128)} %bitcast.1.x_ref, bf16[128,1664]{1,0:T(8,128)(2,1)S(1)} %bitcast.19, bf16[128,1664]{1,0:T(8,128)(2,1)} %collective-permute-done.refs_1_, bf16[128,1664]{1,0:T(8,128)(2,1)} %collective-permute-done.1.refs_2_, bf16[128,1664]{1,0:T(8,128)(2,1)S(1)} %copy-done.9, ...), custom_call_target="tpu_custom_call" | custom-call | flops 30000001024 | bytes 1 | tf_op jit(solution)/shard_map/pallas_call | solution.py:191
  79.3 0.1 add_convert_fusion.refs_4_
  79.4 0.0 copy-start.4
  79.5 4.3 %all-to-all-start.1 = ((bf16[4,1024,128]{2,1,0:T(8,128)(2,1)}), bf16[4,1024,128]{2,1,0:T(8,128)(2,1)}, u32[]{:S(2)}, u32[]{:S(2)}) async-start(bf16[4,1024,128]{2,1,0:T(8,128)(2,1)} %get-tuple-element.55), calls=%async_computation.1 | async-start | bytes 2097152 | tf_op jit(solution)/shard_map/all_to_all | solution.py:218
  83.7 1.9 %collective-permute-start.19 = (bf16[640,256]{1,0:T(8,128)(2,1)S(1)}, bf16[640,256]{1,0:T(8,128)(2,1)S(1)}, u32[]{:S(2)}, u32[]{:S(2)}) collective-permute-start(bf16[640,256]{1,0:T(8,128)(2,1)S(1)} %collective-permute-done.17.refs_1_), channel_id=1, source_target_pairs={{0,12},{4,0},{8,4},{12,8},{1,13},{5,1},{9,5},{13,9},{2,14},{6,2},{... | collective-permute-start | bytes 983048 | tf_op jit(solution)/shard_map/ppermute | solution.py:29
  85.7 0.1 collective-permute-start.20
  85.8 1.3 %collective-permute-start.21 = (bf16[384,256]{1,0:T(8,128)(2,1)S(1)}, bf16[384,256]{1,0:T(8,128)(2,1)S(1)}, u32[]{:S(2)}, u32[]{:S(2)}) collective-permute-start(bf16[384,256]{1,0:T(8,128)(2,1)S(1)} %add_convert_fusion.refs_4_), channel_id=1, source_target_pairs={{0,8},{4,12},{8,0},{12,4},{1,9},{5,13},{9,1},{13,5},{2,10},{6,14},... | collective-permute-start | bytes 589832 | tf_op jit(solution)/shard_map/ppermute | solution.py:29
  87.1 0.1 collective-permute-start.22
  87.1 6.4 %all-to-all-done.1 = bf16[4,1024,128]{2,1,0:T(8,128)(2,1)} async-done(((bf16[4,1024,128]{2,1,0:T(8,128)(2,1)}), bf16[4,1024,128]{2,1,0:T(8,128)(2,1)}, u32[]{:S(2)}, u32[]{:S(2)}) %all-to-all-start.1) | async-done | bytes 1048608 | tf_op jit(solution)/shard_map/all_to_all | solution.py:218
  93.5 1.5 %reduce_sum.35.q_ref = bf16[1024,128]{1,0:T(8,128)(2,1)S(1)} reduce(bf16[4,1024,128]{2,1,0:T(8,128)(2,1)} %all-to-all-done.1, bf16[]{:T(256)} %constant.28.clone.1), dimensions={0}, to_apply=%region_2.0 | reduce | flops 393216 | bytes 1310722 | tf_op jit(solution)/shard_map/reduce_sum | solution.py:222
  95.1 4.4 %shard_map.63 = bf16[1024,128]{1,0:T(8,128)(2,1)S(1)} custom-call(s32[1]{0:T(128)} %bitcast.1.x_ref, s32[1]{0:T(128)} %bitcast.2.z_ref, s32[3]{0:T(128)S(1)} %convert_reduce_fusion.bound_ref, s32[32]{0:T(128)S(1)} %bitcast.20, bf16[1024,128]{1,0:T(8,128)(2,1)S(1)} %reduce_sum.35.q_ref, bf16[640,256]{1,0:T(8,128)(2,1)S(1)} %reduce_sum.34.refs_0_, ...), custom_call_target="tpu_custom_call" | custom-call | flops 1 | bytes 1 | tf_op jit(solution)/shard_map/pallas_call | solution.py:298
  99.5 0.7 collective-permute-start.23
  100.2 2.4 %collective-permute-start.24 = (bf16[256,128]{1,0:T(8,128)(2,1)S(1)}, bf16[256,128]{1,0:T(8,128)(2,1)S(1)}, u32[]{:S(2)}, u32[]{:S(2)}) collective-permute-start(bf16[256,128]{1,0:T(8,128)(2,1)S(1)} %get-tuple-element.63), channel_id=1, source_target_pairs={{0,1},{1,5},{2,9},{3,13},{4,2},{5,6},{6,10},{7,14},{8,3},{9,7},{10... | collective-permute-start | bytes 196616 | tf_op jit(solution)/shard_map/ppermute | solution.py:376
  102.5 4.2 %collective-permute-start.25 = (bf16[256,128]{1,0:T(8,128)(2,1)S(1)}, bf16[256,128]{1,0:T(8,128)(2,1)S(1)}, u32[]{:S(2)}, u32[]{:S(2)}) collective-permute-start(bf16[256,128]{1,0:T(8,128)(2,1)S(1)} %get-tuple-element.62), channel_id=1, source_target_pairs={{0,2},{1,6},{2,10},{3,14},{4,3},{5,7},{6,11},{7,15},{8,0},{9,4},{1... | collective-permute-start | bytes 196616 | tf_op jit(solution)/shard_map/ppermute | solution.py:376
  106.7 2.1 %collective-permute-start.26 = (bf16[256,128]{1,0:T(8,128)(2,1)S(1)}, bf16[256,128]{1,0:T(8,128)(2,1)S(1)}, u32[]{:S(2)}, u32[]{:S(2)}) collective-permute-start(bf16[256,128]{1,0:T(8,128)(2,1)S(1)} %get-tuple-element.61), channel_id=1, source_target_pairs={{0,3},{1,7},{2,11},{3,15},{4,0},{5,4},{6,8},{7,12},{8,1},{9,5},{10... | collective-permute-start | bytes 196616 | tf_op jit(solution)/shard_map/ppermute | solution.py:376
  108.8 1.8 %collective-permute-done.24.refs_1_ = bf16[256,128]{1,0:T(8,128)(2,1)S(1)} collective-permute-done((bf16[256,128]{1,0:T(8,128)(2,1)S(1)}, bf16[256,128]{1,0:T(8,128)(2,1)S(1)}, u32[]{:S(2)}, u32[]{:S(2)}) %collective-permute-start.24) | collective-permute-done | bytes 65568 | tf_op jit(solution)/shard_map/ppermute | solution.py:376
  110.7 1.4 %collective-permute-done.26.refs_3_ = bf16[256,128]{1,0:T(8,128)(2,1)S(1)} collective-permute-done((bf16[256,128]{1,0:T(8,128)(2,1)S(1)}, bf16[256,128]{1,0:T(8,128)(2,1)S(1)}, u32[]{:S(2)}, u32[]{:S(2)}) %collective-permute-start.26) | collective-permute-done | bytes 65568 | tf_op jit(solution)/shard_map/ppermute | solution.py:376
  112.1 0.6 copy-done.15
  112.7 1.7 %shard_map.64 = (bf16[1024,128]{1,0:T(8,128)(2,1)}, bf16[1024,128]{1,0:T(8,128)(2,1)}) custom-call(s32[1]{0:T(128)} %bitcast.y_ref, bf16[256,128]{1,0:T(8,128)(2,1)} %copy-done.12, bf16[256,128]{1,0:T(8,128)(2,1)} %copy-done.13, bf16[256,128]{1,0:T(8,128)(2,1)} %copy-done.14, bf16[256,128]{1,0:T(8,128)(2,1)} %copy-done.15), custom_call_target="tpu_custom_call" | custom-call | tf_op jit(solution)/shard_map/pallas_call | solution.py:331
  114.5 10.6 %collective-permute-start.27 = (bf16[1,1024,128]{2,1,0:T(8,128)(2,1)}, bf16[1,1024,128]{2,1,0:T(8,128)(2,1)S(1)}, u32[]{:S(2)}, u32[]{:S(2)}) collective-permute-start(bf16[1,1024,128]{2,1,0:T(8,128)(2,1)} %bitcast.24), channel_id=1, source_target_pairs={{0,128},{128,0},{1,129},{129,1},{2,130},{130,2},{3,131},{131,3},{4... | collective-permute-start | bytes 786440 | tf_op jit(solution)/shard_map/ppermute | solution.py:29
  125.1 1.4 %collective-permute-done.27 = bf16[1,1024,128]{2,1,0:T(8,128)(2,1)S(1)} collective-permute-done((bf16[1,1024,128]{2,1,0:T(8,128)(2,1)}, bf16[1,1024,128]{2,1,0:T(8,128)(2,1)S(1)}, u32[]{:S(2)}, u32[]{:S(2)}) %collective-permute-start.27) | collective-permute-done | bytes 262176 | tf_op jit(solution)/shard_map/ppermute | solution.py:29
  126.5 0.7 copy.9
  (47 shorter events, 0.2 us)
Async XLA Ops:
  2.0 3.5 %copy-start.1 = (bf16[1,128,1664]{2,1,0:T(8,128)(2,1)S(1)}, bf16[1,128,1664]{2,1,0:T(8,128)(2,1)}, u32[]{:S(2)}) copy-start(bf16[1,128,1664]{2,1,0:T(8,128)(2,1)} %param.4) | copy-start | bytes 1277956
  2.0 21.1 %copy-start.16 = (s32[1,4096]{1,0:T(1,128)S(1)}, s32[1,4096]{1,0:T(1,128)}, u32[]{:S(2)}) copy-start(s32[1,4096]{1,0:T(1,128)} %param.6) | copy-start | bytes 49156
  2.1 21.2 %collective-permute-start.7 = (bf16[1664,256]{1,0:T(8,128)(2,1)S(1)}, bf16[1664,256]{1,0:T(8,128)(2,1)S(1)}, u32[]{:S(2)}, u32[]{:S(2)}) collective-permute-start(bf16[1664,256]{1,0:T(8,128)(2,1)S(1)} %pad_maximum_fusion.refs_3_.refs_5_), channel_id=1, source_target_pairs={{0,12},{4,0},{8,4},{12,8},{1,13},{5,1},{9,5},{13,9},{2,14},{6,2},{... | collective-permute-start | bytes 2555912 | tf_op jit(solution)/shard_map/ppermute | solution.py:29
  5.5 14.9 %collective-permute-start.3 = (bf16[128,1664]{1,0:T(8,128)(2,1)S(1)}, bf16[128,1664]{1,0:T(8,128)(2,1)}, u32[]{:S(2)}, u32[]{:S(2)}) collective-permute-start(bf16[128,1664]{1,0:T(8,128)(2,1)S(1)} %bitcast.15), channel_id=1, source_target_pairs={{0,16},{16,32},{32,48},{48,64},{64,80},{80,96},{96,112},{112,0},{1... | collective-permute-start | bytes 1277960 | tf_op jit(solution)/shard_map/ppermute | solution.py:29
  7.1 13.3 %collective-permute-start = (bf16[128,1664]{1,0:T(8,128)(2,1)S(1)}, bf16[128,1664]{1,0:T(8,128)(2,1)}, u32[]{:S(2)}, u32[]{:S(2)}) collective-permute-start(bf16[128,1664]{1,0:T(8,128)(2,1)S(1)} %bitcast.16), channel_id=1, source_target_pairs={{0,112},{16,0},{32,16},{48,32},{64,48},{80,64},{96,80},{112,96},{1... | collective-permute-start | bytes 1277960 | tf_op jit(solution)/shard_map/ppermute | solution.py:29
  11.1 23.3 %collective-permute-start.9 = (bf16[1664,256]{1,0:T(8,128)(2,1)S(1)}, bf16[1664,256]{1,0:T(8,128)(2,1)S(1)}, u32[]{:S(2)}, u32[]{:S(2)}) collective-permute-start(bf16[1664,256]{1,0:T(8,128)(2,1)S(1)} %pad_maximum_fusion.refs_3_.refs_5_), channel_id=1, source_target_pairs={{0,4},{4,8},{8,12},{12,0},{1,5},{5,9},{9,13},{13,1},{2,6},{6,10},{... | collective-permute-start | bytes 2555912 | tf_op jit(solution)/shard_map/ppermute | solution.py:29
  20.4 11.3 %collective-permute-start.4 = (bf16[128,1664]{1,0:T(8,128)(2,1)}, bf16[128,1664]{1,0:T(8,128)(2,1)}, u32[]{:S(2)}, u32[]{:S(2)}) collective-permute-start(bf16[128,1664]{1,0:T(8,128)(2,1)} %collective-permute-done.3.refs_4_.refs_7_), channel_id=1, source_target_pairs={{0,16},{16,32},{32,48},{48,64},{64,80},{80,96},{96,112},{112,0},{1... | collective-permute-start | bytes 1277960 | tf_op jit(solution)/shard_map/ppermute | solution.py:29
  20.4 11.3 %collective-permute-start.1 = (bf16[128,1664]{1,0:T(8,128)(2,1)}, bf16[128,1664]{1,0:T(8,128)(2,1)}, u32[]{:S(2)}, u32[]{:S(2)}) collective-permute-start(bf16[128,1664]{1,0:T(8,128)(2,1)} %collective-permute-done.refs_1_), channel_id=1, source_target_pairs={{0,112},{16,0},{32,16},{48,32},{64,48},{80,64},{96,80},{112,96},{1... | collective-permute-start | bytes 1277960 | tf_op jit(solution)/shard_map/ppermute | solution.py:29
  23.3 20.0 %collective-permute-start.8 = (bf16[896,256]{1,0:T(8,128)(2,1)S(1)}, bf16[896,256]{1,0:T(8,128)(2,1)S(1)}, u32[]{:S(2)}, u32[]{:S(2)}) collective-permute-start(bf16[896,256]{1,0:T(8,128)(2,1)S(1)} %slice.30), channel_id=1, source_target_pairs={{0,12},{4,0},{8,4},{12,8},{1,13},{5,1},{9,5},{13,9},{2,14},{6,2},{... | collective-permute-start | bytes 1376264 | tf_op jit(solution)/shard_map/ppermute | solution.py:29
  31.7 10.4 %collective-permute-start.5 = (bf16[128,1664]{1,0:T(8,128)(2,1)}, bf16[128,1664]{1,0:T(8,128)(2,1)}, u32[]{:S(2)}, u32[]{:S(2)}) collective-permute-start(bf16[128,1664]{1,0:T(8,128)(2,1)} %collective-permute-done.4.refs_3_.refs_6_), channel_id=1, source_target_pairs={{0,16},{16,32},{32,48},{48,64},{64,80},{80,96},{96,112},{112,0},{1... | collective-permute-start | bytes 1277960 | tf_op jit(solution)/shard_map/ppermute | solution.py:29
  31.7 10.4 %collective-permute-start.2 = (bf16[128,1664]{1,0:T(8,128)(2,1)}, bf16[128,1664]{1,0:T(8,128)(2,1)S(1)}, u32[]{:S(2)}, u32[]{:S(2)}) collective-permute-start(bf16[128,1664]{1,0:T(8,128)(2,1)} %collective-permute-done.1.refs_2_), channel_id=1, source_target_pairs={{0,112},{16,0},{32,16},{48,32},{64,48},{80,64},{96,80},{112,96},{1... | collective-permute-start | bytes 1277960 | tf_op jit(solution)/shard_map/ppermute | solution.py:29
  34.4 9.0 %collective-permute-start.10 = (bf16[768,256]{1,0:T(8,128)(2,1)S(1)}, bf16[768,256]{1,0:T(8,128)(2,1)S(1)}, u32[]{:S(2)}, u32[]{:S(2)}) collective-permute-start(bf16[768,256]{1,0:T(8,128)(2,1)S(1)} %slice.31), channel_id=1, source_target_pairs={{0,4},{4,8},{8,12},{12,0},{1,5},{5,9},{9,13},{13,1},{2,6},{6,10},{... | collective-permute-start | bytes 1179656 | tf_op jit(solution)/shard_map/ppermute | solution.py:29
  42.1 6.0 %copy-start.7 = (bf16[128,1664]{1,0:T(8,128)(2,1)}, bf16[128,1664]{1,0:T(8,128)(2,1)S(1)}, u32[]{:S(2)}) copy-start(bf16[128,1664]{1,0:T(8,128)(2,1)S(1)} %collective-permute-done.2.refs_0_.refs_3_) | copy-start | bytes 1277956
  42.1 11.4 %collective-permute-start.6 = (bf16[128,1664]{1,0:T(8,128)(2,1)}, bf16[128,1664]{1,0:T(8,128)(2,1)}, u32[]{:S(2)}, u32[]{:S(2)}) collective-permute-start(bf16[128,1664]{1,0:T(8,128)(2,1)} %collective-permute-done.5.refs_2_.refs_5_), channel_id=1, source_target_pairs={{0,16},{16,32},{32,48},{48,64},{64,80},{80,96},{96,112},{112,0},{1... | collective-permute-start | bytes 1277960 | tf_op jit(solution)/shard_map/ppermute | solution.py:29
  43.4 4.7 %copy-start.10 = (bf16[768,256]{1,0:T(8,128)(2,1)}, bf16[768,256]{1,0:T(8,128)(2,1)S(1)}, u32[]{:S(2)}) copy-start(bf16[768,256]{1,0:T(8,128)(2,1)S(1)} %collective-permute-done.10.refs_7_.refs_6_) | copy-start | bytes 1179652
  43.4 4.7 %copy-start.5 = (bf16[896,256]{1,0:T(8,128)(2,1)}, bf16[896,256]{1,0:T(8,128)(2,1)S(1)}, u32[]{:S(2)}) copy-start(bf16[896,256]{1,0:T(8,128)(2,1)S(1)} %collective-permute-done.8.refs_6_.refs_5_) | copy-start | bytes 1376260
  43.4 10.1 %collective-permute-start.11 = (bf16[1664,128]{1,0:T(8,128)(2,1)S(1)}, bf16[1664,128]{1,0:T(8,128)(2,1)}, u32[]{:S(2)}, u32[]{:S(2)}) collective-permute-start(bf16[1664,128]{1,0:T(8,128)(2,1)S(1)} %get-tuple-element.44.refs_8_), channel_id=1, source_target_pairs={{0,12},{4,0},{8,4},{12,8},{1,13},{5,1},{9,5},{13,9},{2,14},{6,2},{... | collective-permute-start | bytes 1277960 | tf_op jit(solution)/shard_map/ppermute | solution.py:29
  43.9 26.9 %collective-permute-start.13 = (bf16[1664,128]{1,0:T(8,128)(2,1)S(1)}, bf16[1664,128]{1,0:T(8,128)(2,1)}, u32[]{:S(2)}, u32[]{:S(2)}) collective-permute-start(bf16[1664,128]{1,0:T(8,128)(2,1)S(1)} %get-tuple-element.44.refs_8_), channel_id=1, source_target_pairs={{0,4},{4,8},{8,12},{12,0},{1,5},{5,9},{9,13},{13,1},{2,6},{6,10},{... | collective-permute-start | bytes 1277960 | tf_op jit(solution)/shard_map/ppermute | solution.py:29
  48.1 1.1 copy-start
  49.2 19.9 %all-to-all-start = ((bf16[4,640,256]{2,1,0:T(8,128)(2,1)}), bf16[4,640,256]{2,1,0:T(8,128)(2,1)}, u32[]{:S(2)}, u32[]{:S(2)}) async-start(bf16[4,640,256]{2,1,0:T(8,128)(2,1)} %copy-done), calls=%async_computation | async-start | bytes 2621440 | tf_op jit(solution)/shard_map/all_to_all | solution.py:218
  53.5 18.0 %collective-permute-start.12 = (bf16[1664,128]{1,0:T(8,128)(2,1)}, bf16[1664,128]{1,0:T(8,128)(2,1)}, u32[]{:S(2)}, u32[]{:S(2)}) collective-permute-start(bf16[1664,128]{1,0:T(8,128)(2,1)} %collective-permute-done.11.refs_9_), channel_id=1, source_target_pairs={{0,12},{4,0},{8,4},{12,8},{1,13},{5,1},{9,5},{13,9},{2,14},{6,2},{... | collective-permute-start | bytes 1277960 | tf_op jit(solution)/shard_map/ppermute | solution.py:29
  55.2 1.0 copy-start.6
  56.2 1.0 copy-start.8
  57.2 1.0 copy-start.11
  64.1 0.7 copy-start.2
  64.7 7.6 %copy-start.9 = (bf16[128,1664]{1,0:T(8,128)(2,1)S(1)}, bf16[128,1664]{1,0:T(8,128)(2,1)}, u32[]{:S(2)}) copy-start(bf16[128,1664]{1,0:T(8,128)(2,1)} %copy-done.7) | copy-start | bytes 1277956
  64.7 14.5 %collective-permute-start.14 = (bf16[384,256]{1,0:T(8,128)(2,1)}, bf16[384,256]{1,0:T(8,128)(2,1)S(1)}, u32[]{:S(2)}, u32[]{:S(2)}) collective-permute-start(bf16[384,256]{1,0:T(8,128)(2,1)} %get-tuple-element.49), channel_id=1, source_target_pairs={{0,1},{1,2},{2,3},{3,0},{4,5},{5,6},{6,7},{7,4},{8,9},{9,10},{10,1... | collective-permute-start | bytes 589832 | tf_op jit(solution)/shard_map/ppermute | solution.py:29
  66.1 13.2 %collective-permute-start.15 = (bf16[384,256]{1,0:T(8,128)(2,1)}, bf16[384,256]{1,0:T(8,128)(2,1)S(1)}, u32[]{:S(2)}, u32[]{:S(2)}) collective-permute-start(bf16[384,256]{1,0:T(8,128)(2,1)} %get-tuple-element.50), channel_id=1, source_target_pairs={{0,2},{1,3},{2,0},{3,1},{4,6},{5,7},{6,4},{7,5},{8,10},{9,11},{10,... | collective-permute-start | bytes 589832 | tf_op jit(solution)/shard_map/ppermute | solution.py:29
  68.7 10.6 %collective-permute-start.16 = (bf16[384,256]{1,0:T(8,128)(2,1)}, bf16[384,256]{1,0:T(8,128)(2,1)S(1)}, u32[]{:S(2)}, u32[]{:S(2)}) collective-permute-start(bf16[384,256]{1,0:T(8,128)(2,1)} %get-tuple-element.51), channel_id=1, source_target_pairs={{0,3},{1,0},{2,1},{3,2},{4,7},{5,4},{6,5},{7,6},{8,11},{9,8},{10,9... | collective-permute-start | bytes 589832 | tf_op jit(solution)/shard_map/ppermute | solution.py:29
  70.8 8.7 %collective-permute-start.17 = (bf16[640,256]{1,0:T(8,128)(2,1)S(1)}, bf16[640,256]{1,0:T(8,128)(2,1)S(1)}, u32[]{:S(2)}, u32[]{:S(2)}) collective-permute-start(bf16[640,256]{1,0:T(8,128)(2,1)S(1)} %reduce_sum.34.refs_0_), channel_id=1, source_target_pairs={{0,12},{4,0},{8,4},{12,8},{1,13},{5,1},{9,5},{13,9},{2,14},{6,2},{... | collective-permute-start | bytes 983048 | tf_op jit(solution)/shard_map/ppermute | solution.py:29
  71.5 7.9 %collective-permute-start.18 = (bf16[640,256]{1,0:T(8,128)(2,1)S(1)}, bf16[640,256]{1,0:T(8,128)(2,1)S(1)}, u32[]{:S(2)}, u32[]{:S(2)}) collective-permute-start(bf16[640,256]{1,0:T(8,128)(2,1)S(1)} %reduce_sum.34.refs_0_), channel_id=1, source_target_pairs={{0,4},{4,8},{8,12},{12,0},{1,5},{5,9},{9,13},{13,1},{2,6},{6,10},{... | collective-permute-start | bytes 983048 | tf_op jit(solution)/shard_map/ppermute | solution.py:29
  72.3 7.0 %copy-start.3 = (bf16[384,256]{1,0:T(8,128)(2,1)S(1)}, bf16[384,256]{1,0:T(8,128)(2,1)}, u32[]{:S(2)}) copy-start(bf16[384,256]{1,0:T(8,128)(2,1)} %copy-done.2) | copy-start | bytes 589828
  79.4 15.6 %copy-start.4 = (s32[1,32]{1,0:T(1,128)S(1)}, s32[1,32]{1,0:T(1,128)}, u32[]{:S(2)}) copy-start(s32[1,32]{1,0:T(1,128)} %param.7) | copy-start | bytes 388
  79.5 14.1 %all-to-all-start.1 = ((bf16[4,1024,128]{2,1,0:T(8,128)(2,1)}), bf16[4,1024,128]{2,1,0:T(8,128)(2,1)}, u32[]{:S(2)}, u32[]{:S(2)}) async-start(bf16[4,1024,128]{2,1,0:T(8,128)(2,1)} %get-tuple-element.55), calls=%async_computation.1 | async-start | bytes 2097152 | tf_op jit(solution)/shard_map/all_to_all | solution.py:218
  83.7 11.3 %collective-permute-start.19 = (bf16[640,256]{1,0:T(8,128)(2,1)S(1)}, bf16[640,256]{1,0:T(8,128)(2,1)S(1)}, u32[]{:S(2)}, u32[]{:S(2)}) collective-permute-start(bf16[640,256]{1,0:T(8,128)(2,1)S(1)} %collective-permute-done.17.refs_1_), channel_id=1, source_target_pairs={{0,12},{4,0},{8,4},{12,8},{1,13},{5,1},{9,5},{13,9},{2,14},{6,2},{... | collective-permute-start | bytes 983048 | tf_op jit(solution)/shard_map/ppermute | solution.py:29
  85.7 9.3 %collective-permute-start.20 = (bf16[384,256]{1,0:T(8,128)(2,1)S(1)}, bf16[384,256]{1,0:T(8,128)(2,1)S(1)}, u32[]{:S(2)}, u32[]{:S(2)}) collective-permute-start(bf16[384,256]{1,0:T(8,128)(2,1)S(1)} %add_convert_fusion.refs_4_), channel_id=1, source_target_pairs={{0,12},{4,0},{8,4},{12,8},{1,13},{5,1},{9,5},{13,9},{2,14},{6,2},{... | collective-permute-start | bytes 589832 | tf_op jit(solution)/shard_map/ppermute | solution.py:29
  85.8 9.3 %collective-permute-start.21 = (bf16[384,256]{1,0:T(8,128)(2,1)S(1)}, bf16[384,256]{1,0:T(8,128)(2,1)S(1)}, u32[]{:S(2)}, u32[]{:S(2)}) collective-permute-start(bf16[384,256]{1,0:T(8,128)(2,1)S(1)} %add_convert_fusion.refs_4_), channel_id=1, source_target_pairs={{0,8},{4,12},{8,0},{12,4},{1,9},{5,13},{9,1},{13,5},{2,10},{6,14},... | collective-permute-start | bytes 589832 | tf_op jit(solution)/shard_map/ppermute | solution.py:29
  87.1 8.0 %collective-permute-start.22 = (bf16[384,256]{1,0:T(8,128)(2,1)S(1)}, bf16[384,256]{1,0:T(8,128)(2,1)S(1)}, u32[]{:S(2)}, u32[]{:S(2)}) collective-permute-start(bf16[384,256]{1,0:T(8,128)(2,1)S(1)} %add_convert_fusion.refs_4_), channel_id=1, source_target_pairs={{0,4},{4,8},{8,12},{12,0},{1,5},{5,9},{9,13},{13,1},{2,6},{6,10},{... | collective-permute-start | bytes 589832 | tf_op jit(solution)/shard_map/ppermute | solution.py:29
  99.5 9.4 %collective-permute-start.23 = (bf16[256,128]{1,0:T(8,128)(2,1)S(1)}, bf16[256,128]{1,0:T(8,128)(2,1)S(1)}, u32[]{:S(2)}, u32[]{:S(2)}) collective-permute-start(bf16[256,128]{1,0:T(8,128)(2,1)S(1)} %get-tuple-element.64), channel_id=1, source_target_pairs={{0,0},{1,4},{2,8},{3,12},{4,1},{5,5},{6,9},{7,13},{8,2},{9,6},{10,... | collective-permute-start | bytes 196616 | tf_op jit(solution)/shard_map/ppermute | solution.py:376
  100.2 10.5 %collective-permute-start.24 = (bf16[256,128]{1,0:T(8,128)(2,1)S(1)}, bf16[256,128]{1,0:T(8,128)(2,1)S(1)}, u32[]{:S(2)}, u32[]{:S(2)}) collective-permute-start(bf16[256,128]{1,0:T(8,128)(2,1)S(1)} %get-tuple-element.63), channel_id=1, source_target_pairs={{0,1},{1,5},{2,9},{3,13},{4,2},{5,6},{6,10},{7,14},{8,3},{9,7},{10... | collective-permute-start | bytes 196616 | tf_op jit(solution)/shard_map/ppermute | solution.py:376
  102.5 8.1 %collective-permute-start.25 = (bf16[256,128]{1,0:T(8,128)(2,1)S(1)}, bf16[256,128]{1,0:T(8,128)(2,1)S(1)}, u32[]{:S(2)}, u32[]{:S(2)}) collective-permute-start(bf16[256,128]{1,0:T(8,128)(2,1)S(1)} %get-tuple-element.62), channel_id=1, source_target_pairs={{0,2},{1,6},{2,10},{3,14},{4,3},{5,7},{6,11},{7,15},{8,0},{9,4},{1... | collective-permute-start | bytes 196616 | tf_op jit(solution)/shard_map/ppermute | solution.py:376
  106.7 5.4 %collective-permute-start.26 = (bf16[256,128]{1,0:T(8,128)(2,1)S(1)}, bf16[256,128]{1,0:T(8,128)(2,1)S(1)}, u32[]{:S(2)}, u32[]{:S(2)}) collective-permute-start(bf16[256,128]{1,0:T(8,128)(2,1)S(1)} %get-tuple-element.61), channel_id=1, source_target_pairs={{0,3},{1,7},{2,11},{3,15},{4,0},{5,4},{6,8},{7,12},{8,1},{9,5},{10... | collective-permute-start | bytes 196616 | tf_op jit(solution)/shard_map/ppermute | solution.py:376
  108.8 3.3 %copy-start.12 = (bf16[256,128]{1,0:T(8,128)(2,1)}, bf16[256,128]{1,0:T(8,128)(2,1)S(1)}, u32[]{:S(2)}) copy-start(bf16[256,128]{1,0:T(8,128)(2,1)S(1)} %collective-permute-done.23.refs_0_) | copy-start | bytes 196612
  110.6 1.5 %copy-start.13 = (bf16[256,128]{1,0:T(8,128)(2,1)}, bf16[256,128]{1,0:T(8,128)(2,1)S(1)}, u32[]{:S(2)}) copy-start(bf16[256,128]{1,0:T(8,128)(2,1)S(1)} %collective-permute-done.24.refs_1_) | copy-start | bytes 196612
  110.6 1.5 %copy-start.14 = (bf16[256,128]{1,0:T(8,128)(2,1)}, bf16[256,128]{1,0:T(8,128)(2,1)S(1)}, u32[]{:S(2)}) copy-start(bf16[256,128]{1,0:T(8,128)(2,1)S(1)} %collective-permute-done.25.refs_2_) | copy-start | bytes 196612
  112.1 0.6 copy-start.15
  114.5 12.0 %collective-permute-start.27 = (bf16[1,1024,128]{2,1,0:T(8,128)(2,1)}, bf16[1,1024,128]{2,1,0:T(8,128)(2,1)S(1)}, u32[]{:S(2)}, u32[]{:S(2)}) collective-permute-start(bf16[1,1024,128]{2,1,0:T(8,128)(2,1)} %bitcast.24), channel_id=1, source_target_pairs={{0,128},{128,0},{1,129},{129,1},{2,130},{130,2},{3,131},{131,3},{4... | collective-permute-start | bytes 786440 | tf_op jit(solution)/shard_map/ppermute | solution.py:29

commit v5 on v4

--- a/solution.py
+++ b/solution.py
@@ -21,7 +21,7 @@
 VMEM = pl.BlockSpec(memory_space=pltpu.VMEM)
 FAR = pl.BlockSpec(memory_space=pl.ANY)
 SMEM = pl.BlockSpec(memory_space=pltpu.SMEM)
-LIMIT = pltpu.CompilerParams(vmem_limit_bytes=32 * 2**20)
+LIMIT = pltpu.CompilerParams(vmem_limit_bytes=58 * 2**20)
 
 
 def send(block, axis, distance):

time: 128 us -> 129 us (level); the launches traced: 127 us -> 130 us
  starting transfers between devices: 58.9 us -> 68.8 us
  local copies, waits for them, and re-layouts: 7.53 us -> 3.12 us
  other arithmetic: 3.53 us -> 1.03 us
    ppermute x24, starting transfers between devices: 41.1 us -> 47.6 us  [send(): lax.ppermute(block, axis, [(i, (i + distance) % n) for i in range(n)])]
    unnamed x35, local copies, waits for them, and re-layouts: 6.11 us -> 1.7 us
    ppermute x4, starting transfers between devices: 9.35 us -> 12.6 us  [local(): lax.ppermute(mixed[s * quarter:(s + 1) * quarter], ('x', 'y'), [(4 * i +...]
    reduce_sum x2, other arithmetic: 3.12 us -> 0.62 us  [sum_of(): return jnp.sum(stack.astype(jnp.float32), axis=0).astype(jnp.bfloat16)]
    pallas_call x3, Pallas kernels: 16.1 us -> 17.7 us  [project_stack(): pl.pallas_call(functools.partial(project_stack_kernel, pieces=len(pieces)...]
    pallas_call x1, Pallas kernels: 4.38 us -> 3.07 us  [attend(): pl.pallas_call(attend_kernel, in_specs=[SMEM] * 4 + [VMEM] * 9, out_specs...]
  transfers between devices with their start and end apart: 30 -> 30, of which waited for: 8 -> 10; matrix products, arithmetic and copies ran while one was open for 3% -> 1% of each run, Pallas kernels for 17% -> 18%
where the time goes in v5:
time: 129 us; the launch traced here: 130 us
  starting transfers between devices  68.8 us (53%)
  Pallas kernels  28.3 us (22%)
  waiting for transfers between devices  27.6 us (21%)
  local copies, waits for them, and re-layouts  3.12 us (2%)
    ppermute x24, starting transfers between devices, send(): lax.ppermute(block, axis, [(i, (i + distance) % n) for i in range(n)])  47.6 us
    pallas_call x3, Pallas kernels, project_stack(): pl.pallas_call(functools.partial(project_stack_kernel, pieces=len(pieces)...  17.7 us
    ppermute x24, waiting for transfers between devices, send(): lax.ppermute(block, axis, [(i, (i + distance) % n) for i in range(n)])  17.6 us
    ppermute x4, starting transfers between devices, local(): lax.ppermute(mixed[s * quarter:(s + 1) * quarter], ('x', 'y'), [(4 * i +...  12.6 us
    all_to_all x2, starting transfers between devices, exchange(): return lax.all_to_all(stack, axis, 0, 0, tiled=True)  8.66 us
    all_to_all x2, waiting for transfers between devices, exchange(): return lax.all_to_all(stack, axis, 0, 0, tiled=True)  6.47 us
    pallas_call x1, Pallas kernels, project(): pl.pallas_call(functools.partial(project_kernel, pieces=len(pieces), slot...  5.76 us
    ppermute x4, waiting for transfers between devices, local(): lax.ppermute(mixed[s * quarter:(s + 1) * quarter], ('x', 'y'), [(4 * i +...  3.52 us
  transfers between devices with their start and end apart: 30, of which 10 were waited for; matrix products, arithmetic and copies ran while one was open for 1% of the time, Pallas kernels for 18%

profile of v5, /device:TPU:1, one launch (start us, length us, event | category | flops | bytes accessed | tf_op | source)
XLA Modules:
  0.0 129.7 jit_solution(10680138560695393918)
XLA Ops:
  0.6 1.3 %slice_bitcast_fusion.1 = (bf16[1664,128]{1,0:T(8,128)(2,1)S(1)}, bf16[1664,128]{1,0:T(8,128)(2,1)S(1)}, bf16[1664,128]{1,0:T(8,128)(2,1)S(1)}) fusion(bf16[1664,3,128]{2,0,1:T(8,128)(2,1)} %bitcast.16), kind=kLoop, calls=%fused_computation.2 | loop fusion | bytes 2555904 | tf_op jit(solution)/shard_map/squeeze | solution.py:353
  2.0 0.0 copy-start.4
  2.0 0.0 copy-start.12
  2.0 0.1 pad_maximum_fusion.refs_3_.refs_5_
  2.1 3.4 %collective-permute-start.7 = (bf16[1664,256]{1,0:T(8,128)(2,1)S(1)}, bf16[1664,256]{1,0:T(8,128)(2,1)S(1)}, u32[]{:S(2)}, u32[]{:S(2)}) collective-permute-start(bf16[1664,256]{1,0:T(8,128)(2,1)S(1)} %pad_maximum_fusion.refs_3_.refs_5_), channel_id=1, source_target_pairs={{0,12},{4,0},{8,4},{12,8},{1,13},{5,1},{9,5},{13,9},{2,14},{6,2},{... | collective-permute-start | bytes 2555912 | tf_op jit(solution)/shard_map/ppermute | solution.py:29
  5.5 1.6 %collective-permute-start.3 = (bf16[128,1664]{1,0:T(8,128)(2,1)S(1)}, bf16[128,1664]{1,0:T(8,128)(2,1)}, u32[]{:S(2)}, u32[]{:S(2)}) collective-permute-start(bf16[128,1664]{1,0:T(8,128)(2,1)S(1)} %bitcast.20), channel_id=1, source_target_pairs={{0,16},{16,32},{32,48},{48,64},{64,80},{80,96},{96,112},{112,0},{1... | collective-permute-start | bytes 1277960 | tf_op jit(solution)/shard_map/ppermute | solution.py:29
  7.2 3.9 %collective-permute-start = (bf16[128,1664]{1,0:T(8,128)(2,1)S(1)}, bf16[128,1664]{1,0:T(8,128)(2,1)}, u32[]{:S(2)}, u32[]{:S(2)}) collective-permute-start(bf16[128,1664]{1,0:T(8,128)(2,1)S(1)} %bitcast.21), channel_id=1, source_target_pairs={{0,112},{16,0},{32,16},{48,32},{64,48},{80,64},{96,80},{112,96},{1... | collective-permute-start | bytes 1277960 | tf_op jit(solution)/shard_map/ppermute | solution.py:29
  11.1 9.3 %collective-permute-done.3.refs_4_.refs_7_ = bf16[128,1664]{1,0:T(8,128)(2,1)} collective-permute-done((bf16[128,1664]{1,0:T(8,128)(2,1)S(1)}, bf16[128,1664]{1,0:T(8,128)(2,1)}, u32[]{:S(2)}, u32[]{:S(2)}) %collective-permute-start.3) | collective-permute-done | bytes 426016 | tf_op jit(solution)/shard_map/ppermute | solution.py:29
  20.4 0.0 collective-permute-start.4
  20.4 0.0 collective-permute-done.refs_1_
  20.4 2.7 %collective-permute-start.1 = (bf16[128,1664]{1,0:T(8,128)(2,1)}, bf16[128,1664]{1,0:T(8,128)(2,1)S(1)}, u32[]{:S(2)}, u32[]{:S(2)}) collective-permute-start(bf16[128,1664]{1,0:T(8,128)(2,1)} %collective-permute-done.refs_1_), channel_id=1, source_target_pairs={{0,112},{16,0},{32,16},{48,32},{64,48},{80,64},{96,80},{112,96},{1... | collective-permute-start | bytes 1277960 | tf_op jit(solution)/shard_map/ppermute | solution.py:29
  23.1 0.2 convert_reduce_fusion.bound_ref
  23.3 0.0 collective-permute-done.7.refs_4_.refs_6_
  23.4 3.3 %collective-permute-start.8 = (bf16[896,256]{1,0:T(8,128)(2,1)S(1)}, bf16[896,256]{1,0:T(8,128)(2,1)S(1)}, u32[]{:S(2)}, u32[]{:S(2)}) collective-permute-start(bf16[896,256]{1,0:T(8,128)(2,1)S(1)} %slice.30), channel_id=1, source_target_pairs={{0,12},{4,0},{8,4},{12,8},{1,13},{5,1},{9,5},{13,9},{2,14},{6,2},{... | collective-permute-start | bytes 1376264 | tf_op jit(solution)/shard_map/ppermute | solution.py:29
  26.7 5.1 %collective-permute-done.4.refs_3_.refs_6_ = bf16[128,1664]{1,0:T(8,128)(2,1)} collective-permute-done((bf16[128,1664]{1,0:T(8,128)(2,1)}, bf16[128,1664]{1,0:T(8,128)(2,1)}, u32[]{:S(2)}, u32[]{:S(2)}) %collective-permute-start.4) | collective-permute-done | bytes 426016 | tf_op jit(solution)/shard_map/ppermute | solution.py:29
  31.7 0.0 collective-permute-start.5
  31.7 0.0 collective-permute-done.1.refs_2_
  31.7 2.7 %collective-permute-start.2 = (bf16[128,1664]{1,0:T(8,128)(2,1)S(1)}, bf16[128,1664]{1,0:T(8,128)(2,1)S(1)}, u32[]{:S(2)}, u32[]{:S(2)}) collective-permute-start(bf16[128,1664]{1,0:T(8,128)(2,1)S(1)} %collective-permute-done.1.refs_2_), channel_id=1, source_target_pairs={{0,112},{16,0},{32,16},{48,32},{64,48},{80,64},{96,80},{112,96},{1... | collective-permute-start | bytes 1277960 | tf_op jit(solution)/shard_map/ppermute | solution.py:29
  34.4 0.0 collective-permute-done.9.refs_5_.refs_7_
  34.4 0.5 collective-permute-start.10
  35.0 0.3 copy-done.3
  35.3 6.7 %shard_map.60 = (bf16[4,640,256]{2,1,0:T(8,128)(2,1)}, f32[8,128]{1,0:T(8,128)}) custom-call(s32[1]{0:T(128)} %bitcast.1.x_ref, bf16[128,1664]{1,0:T(8,128)(2,1)} %bitcast.17, bf16[128,1664]{1,0:T(8,128)(2,1)} %collective-permute-done.refs_1_, bf16[128,1664]{1,0:T(8,128)(2,1)} %copy-done.6, bf16[128,1664]{1,0:T(8,128)(2,1)} %collective-permute-done.4.refs_3_.refs_6_, ...), custom_call_target="tpu_custom_call" | custom-call | flops 1 | bytes 1 | tf_op jit(solution)/shard_map/pallas_call | solution.py:191
  42.0 0.1 collective-permute-done.5.refs_2_.refs_5_
  42.1 1.3 %collective-permute-done.10.refs_7_.refs_6_ = bf16[768,256]{1,0:T(8,128)(2,1)S(1)} collective-permute-done((bf16[768,256]{1,0:T(8,128)(2,1)S(1)}, bf16[768,256]{1,0:T(8,128)(2,1)S(1)}, u32[]{:S(2)}, u32[]{:S(2)}) %collective-permute-start.10) | collective-permute-done | bytes 393248 | tf_op jit(solution)/shard_map/ppermute | solution.py:29
  43.4 0.9 collective-permute-start.11
  44.3 0.6 collective-permute-start.13
  45.0 3.9 %shard_map.61 = (bf16[4,640,256]{2,1,0:T(8,128)(2,1)}, f32[8,128]{1,0:T(8,128)}) custom-call(s32[1]{0:T(128)} %bitcast.1.x_ref, bf16[128,1664]{1,0:T(8,128)(2,1)} %bitcast.18, bf16[128,1664]{1,0:T(8,128)(2,1)} %collective-permute-done.refs_1_, bf16[128,1664]{1,0:T(8,128)(2,1)} %copy-done.6, ...), custom_call_target="tpu_custom_call", output_to_operand_aliasing={{0}: (8, {})} | custom-call | flops 30000001024 | bytes 1 | tf_op jit(solution)/shard_map/pallas_call | solution.py:191
  48.9 4.2 %all-to-all-start = ((bf16[4,640,256]{2,1,0:T(8,128)(2,1)}), bf16[4,640,256]{2,1,0:T(8,128)(2,1)S(1)}, u32[]{:S(2)}, u32[]{:S(2)}) async-start(bf16[4,640,256]{2,1,0:T(8,128)(2,1)} %get-tuple-element.43), calls=%async_computation | async-start | bytes 2621440 | tf_op jit(solution)/shard_map/all_to_all | solution.py:218
  53.1 2.1 %collective-permute-start.12 = (bf16[1664,128]{1,0:T(8,128)(2,1)}, bf16[1664,128]{1,0:T(8,128)(2,1)}, u32[]{:S(2)}, u32[]{:S(2)}) collective-permute-start(bf16[1664,128]{1,0:T(8,128)(2,1)} %collective-permute-done.11.refs_9_), channel_id=1, source_target_pairs={{0,12},{4,0},{8,4},{12,8},{1,13},{5,1},{9,5},{13,9},{2,14},{6,2},{... | collective-permute-start | bytes 1277960 | tf_op jit(solution)/shard_map/ppermute | solution.py:29
  55.2 5.8 %shard_map.59 = (bf16[384,256]{1,0:T(8,128)(2,1)}, bf16[384,256]{1,0:T(8,128)(2,1)}, bf16[384,256]{1,0:T(8,128)(2,1)}, bf16[384,256]{1,0:T(8,128)(2,1)}) custom-call(s32[1]{0:T(128)S(6)} %rem.18.shift_ref, bf16[128,1664]{1,0:T(8,128)(2,1)} %copy-done.14, bf16[128,1664]{1,0:T(8,128)(2,1)} %copy-done.15, ...), custom_call_target="tpu_custom_call" | custom-call | flops 30000001024 | bytes 1 | tf_op jit(solution)/shard_map/pallas_call | solution.py:167
  61.0 1.5 %collective-permute-start.14 = (bf16[384,256]{1,0:T(8,128)(2,1)}, bf16[384,256]{1,0:T(8,128)(2,1)S(1)}, u32[]{:S(2)}, u32[]{:S(2)}) collective-permute-start(bf16[384,256]{1,0:T(8,128)(2,1)} %get-tuple-element.49), channel_id=1, source_target_pairs={{0,1},{1,2},{2,3},{3,0},{4,5},{5,6},{6,7},{7,4},{8,9},{9,10},{10,1... | collective-permute-start | bytes 589832 | tf_op jit(solution)/shard_map/ppermute | solution.py:29
  62.6 2.4 %collective-permute-start.15 = (bf16[384,256]{1,0:T(8,128)(2,1)}, bf16[384,256]{1,0:T(8,128)(2,1)S(1)}, u32[]{:S(2)}, u32[]{:S(2)}) collective-permute-start(bf16[384,256]{1,0:T(8,128)(2,1)} %get-tuple-element.50), channel_id=1, source_target_pairs={{0,2},{1,3},{2,0},{3,1},{4,6},{5,7},{6,4},{7,5},{8,10},{9,11},{10,... | collective-permute-start | bytes 589832 | tf_op jit(solution)/shard_map/ppermute | solution.py:29
  64.9 1.2 collective-permute-start.16
  66.1 0.4 reduce_sum.34.refs_0_
  66.5 2.4 %collective-permute-start.17 = (bf16[640,256]{1,0:T(8,128)(2,1)S(1)}, bf16[640,256]{1,0:T(8,128)(2,1)S(1)}, u32[]{:S(2)}, u32[]{:S(2)}) collective-permute-start(bf16[640,256]{1,0:T(8,128)(2,1)S(1)} %reduce_sum.34.refs_0_), channel_id=1, source_target_pairs={{0,12},{4,0},{8,4},{12,8},{1,13},{5,1},{9,5},{13,9},{2,14},{6,2},{... | collective-permute-start | bytes 983048 | tf_op jit(solution)/shard_map/ppermute | solution.py:29
  68.9 0.0 collective-permute-start.18
  68.9 7.1 %shard_map.62 = (bf16[4,1024,128]{2,1,0:T(8,128)(2,1)}, f32[8,128]{1,0:T(8,128)}) custom-call(s32[1]{0:T(128)} %bitcast.1.x_ref, bf16[128,1664]{1,0:T(8,128)(2,1)} %bitcast.19, bf16[128,1664]{1,0:T(8,128)(2,1)} %collective-permute-done.refs_1_, bf16[128,1664]{1,0:T(8,128)(2,1)} %copy-done.6, bf16[128,1664]{1,0:T(8,128)(2,1)} %copy-done.14, ...), custom_call_target="tpu_custom_call" | custom-call | flops 30000001024 | bytes 1 | tf_op jit(solution)/shard_map/pallas_call | solution.py:191
  76.0 0.0 collective-permute-done.14
  76.0 0.0 collective-permute-done.15
  76.0 0.1 add_convert_fusion.refs_4_
  76.1 0.0 copy-start
  76.1 0.0 collective-permute-done.17.refs_1_
  76.2 0.2 collective-permute-done.18.refs_3_
  76.3 4.5 %all-to-all-start.1 = ((bf16[4,1024,128]{2,1,0:T(8,128)(2,1)}), bf16[4,1024,128]{2,1,0:T(8,128)(2,1)S(1)}, u32[]{:S(2)}, u32[]{:S(2)}) async-start(bf16[4,1024,128]{2,1,0:T(8,128)(2,1)} %get-tuple-element.55), calls=%async_computation.1 | async-start | bytes 2097152 | tf_op jit(solution)/shard_map/all_to_all | solution.py:218
  80.8 1.8 %collective-permute-start.19 = (bf16[640,256]{1,0:T(8,128)(2,1)S(1)}, bf16[640,256]{1,0:T(8,128)(2,1)S(1)}, u32[]{:S(2)}, u32[]{:S(2)}) collective-permute-start(bf16[640,256]{1,0:T(8,128)(2,1)S(1)} %collective-permute-done.17.refs_1_), channel_id=1, source_target_pairs={{0,12},{4,0},{8,4},{12,8},{1,13},{5,1},{9,5},{13,9},{2,14},{6,2},{... | collective-permute-start | bytes 983048 | tf_op jit(solution)/shard_map/ppermute | solution.py:29
  82.6 0.0 collective-permute-start.20
  82.6 1.4 %collective-permute-start.21 = (bf16[384,256]{1,0:T(8,128)(2,1)S(1)}, bf16[384,256]{1,0:T(8,128)(2,1)S(1)}, u32[]{:S(2)}, u32[]{:S(2)}) collective-permute-start(bf16[384,256]{1,0:T(8,128)(2,1)S(1)} %add_convert_fusion.refs_4_), channel_id=1, source_target_pairs={{0,8},{4,12},{8,0},{12,4},{1,9},{5,13},{9,1},{13,5},{2,10},{6,14},... | collective-permute-start | bytes 589832 | tf_op jit(solution)/shard_map/ppermute | solution.py:29
  84.0 0.0 collective-permute-start.22
  84.1 6.5 %all-to-all-done.1 = bf16[4,1024,128]{2,1,0:T(8,128)(2,1)S(1)} async-done(((bf16[4,1024,128]{2,1,0:T(8,128)(2,1)}), bf16[4,1024,128]{2,1,0:T(8,128)(2,1)S(1)}, u32[]{:S(2)}, u32[]{:S(2)}) %all-to-all-start.1) | async-done | bytes 1048608 | tf_op jit(solution)/shard_map/all_to_all | solution.py:218
  90.5 0.3 reduce_sum.35.q_ref
  90.8 0.2 collective-permute-done.20.refs_5_
  91.0 0.0 collective-permute-done.21.refs_6_
  91.0 3.1 %shard_map.63 = bf16[1024,128]{1,0:T(8,128)(2,1)S(1)} custom-call(s32[1]{0:T(128)} %bitcast.1.x_ref, s32[1]{0:T(128)} %bitcast.2.z_ref, s32[3]{0:T(128)S(1)} %convert_reduce_fusion.bound_ref, s32[32]{0:T(128)S(1)} %bitcast.15, bf16[1024,128]{1,0:T(8,128)(2,1)S(1)} %reduce_sum.35.q_ref, bf16[640,256]{1,0:T(8,128)(2,1)S(1)} %reduce_sum.34.refs_0_, ...), custom_call_target="tpu_custom_call" | custom-call | flops 1 | bytes 1 | tf_op jit(solution)/shard_map/pallas_call | solution.py:298
  94.1 0.7 collective-permute-start.23
  94.8 5.4 %collective-permute-start.24 = (bf16[256,128]{1,0:T(8,128)(2,1)S(1)}, bf16[256,128]{1,0:T(8,128)(2,1)S(1)}, u32[]{:S(2)}, u32[]{:S(2)}) collective-permute-start(bf16[256,128]{1,0:T(8,128)(2,1)S(1)} %get-tuple-element.63), channel_id=1, source_target_pairs={{0,1},{1,5},{2,9},{3,13},{4,2},{5,6},{6,10},{7,14},{8,3},{9,7},{10... | collective-permute-start | bytes 196616 | tf_op jit(solution)/shard_map/ppermute | solution.py:376
  100.1 4.5 %collective-permute-start.25 = (bf16[256,128]{1,0:T(8,128)(2,1)S(1)}, bf16[256,128]{1,0:T(8,128)(2,1)S(1)}, u32[]{:S(2)}, u32[]{:S(2)}) collective-permute-start(bf16[256,128]{1,0:T(8,128)(2,1)S(1)} %get-tuple-element.62), channel_id=1, source_target_pairs={{0,2},{1,6},{2,10},{3,14},{4,3},{5,7},{6,11},{7,15},{8,0},{9,4},{1... | collective-permute-start | bytes 196616 | tf_op jit(solution)/shard_map/ppermute | solution.py:376
  104.6 2.1 %collective-permute-start.26 = (bf16[256,128]{1,0:T(8,128)(2,1)S(1)}, bf16[256,128]{1,0:T(8,128)(2,1)S(1)}, u32[]{:S(2)}, u32[]{:S(2)}) collective-permute-start(bf16[256,128]{1,0:T(8,128)(2,1)S(1)} %get-tuple-element.61), channel_id=1, source_target_pairs={{0,3},{1,7},{2,11},{3,15},{4,0},{5,4},{6,8},{7,12},{8,1},{9,5},{10... | collective-permute-start | bytes 196616 | tf_op jit(solution)/shard_map/ppermute | solution.py:376
  106.7 1.0 collective-permute-done.24.refs_1_
  107.7 2.6 %collective-permute-done.26.refs_3_ = bf16[256,128]{1,0:T(8,128)(2,1)S(1)} collective-permute-done((bf16[256,128]{1,0:T(8,128)(2,1)S(1)}, bf16[256,128]{1,0:T(8,128)(2,1)S(1)}, u32[]{:S(2)}, u32[]{:S(2)}) %collective-permute-start.26) | collective-permute-done | bytes 65568 | tf_op jit(solution)/shard_map/ppermute | solution.py:376
  110.3 0.6 copy-done.11
  110.9 1.7 %shard_map.64 = (bf16[1024,128]{1,0:T(8,128)(2,1)}, bf16[1024,128]{1,0:T(8,128)(2,1)}) custom-call(s32[1]{0:T(128)} %bitcast.y_ref, bf16[256,128]{1,0:T(8,128)(2,1)} %copy-done.8, bf16[256,128]{1,0:T(8,128)(2,1)} %copy-done.9, bf16[256,128]{1,0:T(8,128)(2,1)} %copy-done.10, bf16[256,128]{1,0:T(8,128)(2,1)} %copy-done.11), custom_call_target="tpu_custom_call" | custom-call | tf_op jit(solution)/shard_map/pallas_call | solution.py:331
  112.7 15.0 %collective-permute-start.27 = (bf16[1,1024,128]{2,1,0:T(8,128)(2,1)}, bf16[1,1024,128]{2,1,0:T(8,128)(2,1)S(1)}, u32[]{:S(2)}, u32[]{:S(2)}) collective-permute-start(bf16[1,1024,128]{2,1,0:T(8,128)(2,1)} %bitcast.24), channel_id=1, source_target_pairs={{0,128},{128,0},{1,129},{129,1},{2,130},{130,2},{3,131},{131,3},{4... | collective-permute-start | bytes 786440 | tf_op jit(solution)/shard_map/ppermute | solution.py:29
  127.7 1.4 %collective-permute-done.27 = bf16[1,1024,128]{2,1,0:T(8,128)(2,1)S(1)} collective-permute-done((bf16[1,1024,128]{2,1,0:T(8,128)(2,1)}, bf16[1,1024,128]{2,1,0:T(8,128)(2,1)S(1)}, u32[]{:S(2)}, u32[]{:S(2)}) %collective-permute-start.27) | collective-permute-done | bytes 262176 | tf_op jit(solution)/shard_map/ppermute | solution.py:29
  129.0 0.7 copy.9
  (47 shorter events, 0.2 us)
Async XLA Ops:
  2.0 42.4 %copy-start.5 = (bf16[1664,128]{1,0:T(8,128)(2,1)}, bf16[1664,128]{1,0:T(8,128)(2,1)S(1)}, u32[]{:S(2)}) copy-start(bf16[1664,128]{1,0:T(8,128)(2,1)S(1)} %get-tuple-element.44.refs_8_) | copy-start | bytes 1277956
  2.0 3.5 %copy-start.4 = (bf16[1,128,1664]{2,1,0:T(8,128)(2,1)S(1)}, bf16[1,128,1664]{2,1,0:T(8,128)(2,1)}, u32[]{:S(2)}) copy-start(bf16[1,128,1664]{2,1,0:T(8,128)(2,1)} %param.4) | copy-start | bytes 1277956
  2.0 21.1 %copy-start.12 = (s32[1,4096]{1,0:T(1,128)S(1)}, s32[1,4096]{1,0:T(1,128)}, u32[]{:S(2)}) copy-start(s32[1,4096]{1,0:T(1,128)} %param.6) | copy-start | bytes 49156
  2.1 32.9 %copy-start.1 = (bf16[1664,256]{1,0:T(8,128)(2,1)}, bf16[1664,256]{1,0:T(8,128)(2,1)S(1)}, u32[]{:S(2)}) copy-start(bf16[1664,256]{1,0:T(8,128)(2,1)S(1)} %pad_maximum_fusion.refs_3_.refs_5_) | copy-start | bytes 2555908
  2.1 21.2 %collective-permute-start.7 = (bf16[1664,256]{1,0:T(8,128)(2,1)S(1)}, bf16[1664,256]{1,0:T(8,128)(2,1)S(1)}, u32[]{:S(2)}, u32[]{:S(2)}) collective-permute-start(bf16[1664,256]{1,0:T(8,128)(2,1)S(1)} %pad_maximum_fusion.refs_3_.refs_5_), channel_id=1, source_target_pairs={{0,12},{4,0},{8,4},{12,8},{1,13},{5,1},{9,5},{13,9},{2,14},{6,2},{... | collective-permute-start | bytes 2555912 | tf_op jit(solution)/shard_map/ppermute | solution.py:29
  5.5 14.9 %collective-permute-start.3 = (bf16[128,1664]{1,0:T(8,128)(2,1)S(1)}, bf16[128,1664]{1,0:T(8,128)(2,1)}, u32[]{:S(2)}, u32[]{:S(2)}) collective-permute-start(bf16[128,1664]{1,0:T(8,128)(2,1)S(1)} %bitcast.20), channel_id=1, source_target_pairs={{0,16},{16,32},{32,48},{48,64},{64,80},{80,96},{96,112},{112,0},{1... | collective-permute-start | bytes 1277960 | tf_op jit(solution)/shard_map/ppermute | solution.py:29
  7.2 13.3 %collective-permute-start = (bf16[128,1664]{1,0:T(8,128)(2,1)S(1)}, bf16[128,1664]{1,0:T(8,128)(2,1)}, u32[]{:S(2)}, u32[]{:S(2)}) collective-permute-start(bf16[128,1664]{1,0:T(8,128)(2,1)S(1)} %bitcast.21), channel_id=1, source_target_pairs={{0,112},{16,0},{32,16},{48,32},{64,48},{80,64},{96,80},{112,96},{1... | collective-permute-start | bytes 1277960 | tf_op jit(solution)/shard_map/ppermute | solution.py:29
  11.1 23.3 %collective-permute-start.9 = (bf16[1664,256]{1,0:T(8,128)(2,1)S(1)}, bf16[1664,256]{1,0:T(8,128)(2,1)S(1)}, u32[]{:S(2)}, u32[]{:S(2)}) collective-permute-start(bf16[1664,256]{1,0:T(8,128)(2,1)S(1)} %pad_maximum_fusion.refs_3_.refs_5_), channel_id=1, source_target_pairs={{0,4},{4,8},{8,12},{12,0},{1,5},{5,9},{9,13},{13,1},{2,6},{6,10},{... | collective-permute-start | bytes 2555912 | tf_op jit(solution)/shard_map/ppermute | solution.py:29
  20.4 11.3 %collective-permute-start.4 = (bf16[128,1664]{1,0:T(8,128)(2,1)}, bf16[128,1664]{1,0:T(8,128)(2,1)}, u32[]{:S(2)}, u32[]{:S(2)}) collective-permute-start(bf16[128,1664]{1,0:T(8,128)(2,1)} %collective-permute-done.3.refs_4_.refs_7_), channel_id=1, source_target_pairs={{0,16},{16,32},{32,48},{48,64},{64,80},{80,96},{96,112},{112,0},{1... | collective-permute-start | bytes 1277960 | tf_op jit(solution)/shard_map/ppermute | solution.py:29
  20.4 11.3 %collective-permute-start.1 = (bf16[128,1664]{1,0:T(8,128)(2,1)}, bf16[128,1664]{1,0:T(8,128)(2,1)S(1)}, u32[]{:S(2)}, u32[]{:S(2)}) collective-permute-start(bf16[128,1664]{1,0:T(8,128)(2,1)} %collective-permute-done.refs_1_), channel_id=1, source_target_pairs={{0,112},{16,0},{32,16},{48,32},{64,48},{80,64},{96,80},{112,96},{1... | collective-permute-start | bytes 1277960 | tf_op jit(solution)/shard_map/ppermute | solution.py:29
  23.3 11.7 %copy-start.2 = (bf16[1664,256]{1,0:T(8,128)(2,1)}, bf16[1664,256]{1,0:T(8,128)(2,1)S(1)}, u32[]{:S(2)}) copy-start(bf16[1664,256]{1,0:T(8,128)(2,1)S(1)} %collective-permute-done.7.refs_4_.refs_6_) | copy-start | bytes 2555908
  23.4 20.0 %collective-permute-start.8 = (bf16[896,256]{1,0:T(8,128)(2,1)S(1)}, bf16[896,256]{1,0:T(8,128)(2,1)S(1)}, u32[]{:S(2)}, u32[]{:S(2)}) collective-permute-start(bf16[896,256]{1,0:T(8,128)(2,1)S(1)} %slice.30), channel_id=1, source_target_pairs={{0,12},{4,0},{8,4},{12,8},{1,13},{5,1},{9,5},{13,9},{2,14},{6,2},{... | collective-permute-start | bytes 1376264 | tf_op jit(solution)/shard_map/ppermute | solution.py:29
  31.7 10.4 %collective-permute-start.5 = (bf16[128,1664]{1,0:T(8,128)(2,1)}, bf16[128,1664]{1,0:T(8,128)(2,1)}, u32[]{:S(2)}, u32[]{:S(2)}) collective-permute-start(bf16[128,1664]{1,0:T(8,128)(2,1)} %collective-permute-done.4.refs_3_.refs_6_), channel_id=1, source_target_pairs={{0,16},{16,32},{32,48},{48,64},{64,80},{80,96},{96,112},{112,0},{1... | collective-permute-start | bytes 1277960 | tf_op jit(solution)/shard_map/ppermute | solution.py:29
  31.7 3.3 %copy-start.6 = (bf16[128,1664]{1,0:T(8,128)(2,1)}, bf16[128,1664]{1,0:T(8,128)(2,1)S(1)}, u32[]{:S(2)}) copy-start(bf16[128,1664]{1,0:T(8,128)(2,1)S(1)} %collective-permute-done.1.refs_2_) | copy-start | bytes 1277956
  31.7 10.4 %collective-permute-start.2 = (bf16[128,1664]{1,0:T(8,128)(2,1)S(1)}, bf16[128,1664]{1,0:T(8,128)(2,1)S(1)}, u32[]{:S(2)}, u32[]{:S(2)}) collective-permute-start(bf16[128,1664]{1,0:T(8,128)(2,1)S(1)} %collective-permute-done.1.refs_2_), channel_id=1, source_target_pairs={{0,112},{16,0},{32,16},{48,32},{64,48},{80,64},{96,80},{112,96},{1... | collective-permute-start | bytes 1277960 | tf_op jit(solution)/shard_map/ppermute | solution.py:29
  34.4 0.9 copy-start.3
  34.4 9.0 %collective-permute-start.10 = (bf16[768,256]{1,0:T(8,128)(2,1)S(1)}, bf16[768,256]{1,0:T(8,128)(2,1)S(1)}, u32[]{:S(2)}, u32[]{:S(2)}) collective-permute-start(bf16[768,256]{1,0:T(8,128)(2,1)S(1)} %slice.31), channel_id=1, source_target_pairs={{0,4},{4,8},{8,12},{12,0},{1,5},{5,9},{9,13},{13,1},{2,6},{6,10},{... | collective-permute-start | bytes 1179656 | tf_op jit(solution)/shard_map/ppermute | solution.py:29
  42.1 6.8 %copy-start.14 = (bf16[128,1664]{1,0:T(8,128)(2,1)}, bf16[128,1664]{1,0:T(8,128)(2,1)S(1)}, u32[]{:S(2)}) copy-start(bf16[128,1664]{1,0:T(8,128)(2,1)S(1)} %collective-permute-done.2.refs_0_.refs_3_) | copy-start | bytes 1277956
  42.1 11.0 %collective-permute-start.6 = (bf16[128,1664]{1,0:T(8,128)(2,1)}, bf16[128,1664]{1,0:T(8,128)(2,1)S(1)}, u32[]{:S(2)}, u32[]{:S(2)}) collective-permute-start(bf16[128,1664]{1,0:T(8,128)(2,1)} %collective-permute-done.5.refs_2_.refs_5_), channel_id=1, source_target_pairs={{0,16},{16,32},{32,48},{48,64},{64,80},{80,96},{96,112},{112,0},{1... | collective-permute-start | bytes 1277960 | tf_op jit(solution)/shard_map/ppermute | solution.py:29
  43.4 1.6 %copy-start.16 = (bf16[768,256]{1,0:T(8,128)(2,1)}, bf16[768,256]{1,0:T(8,128)(2,1)S(1)}, u32[]{:S(2)}) copy-start(bf16[768,256]{1,0:T(8,128)(2,1)S(1)} %collective-permute-done.10.refs_7_.refs_6_) | copy-start | bytes 1179652
  43.4 1.5 %copy-start.13 = (bf16[896,256]{1,0:T(8,128)(2,1)}, bf16[896,256]{1,0:T(8,128)(2,1)S(1)}, u32[]{:S(2)}) copy-start(bf16[896,256]{1,0:T(8,128)(2,1)S(1)} %collective-permute-done.8.refs_6_.refs_5_) | copy-start | bytes 1376260
  43.4 9.7 %collective-permute-start.11 = (bf16[1664,128]{1,0:T(8,128)(2,1)S(1)}, bf16[1664,128]{1,0:T(8,128)(2,1)}, u32[]{:S(2)}, u32[]{:S(2)}) collective-permute-start(bf16[1664,128]{1,0:T(8,128)(2,1)S(1)} %get-tuple-element.44.refs_8_), channel_id=1, source_target_pairs={{0,12},{4,0},{8,4},{12,8},{1,13},{5,1},{9,5},{13,9},{2,14},{6,2},{... | collective-permute-start | bytes 1277960 | tf_op jit(solution)/shard_map/ppermute | solution.py:29
  44.3 22.2 %collective-permute-start.13 = (bf16[1664,128]{1,0:T(8,128)(2,1)S(1)}, bf16[1664,128]{1,0:T(8,128)(2,1)}, u32[]{:S(2)}, u32[]{:S(2)}) collective-permute-start(bf16[1664,128]{1,0:T(8,128)(2,1)S(1)} %get-tuple-element.44.refs_8_), channel_id=1, source_target_pairs={{0,4},{4,8},{8,12},{12,0},{1,5},{5,9},{9,13},{13,1},{2,6},{6,10},{... | collective-permute-start | bytes 1277960 | tf_op jit(solution)/shard_map/ppermute | solution.py:29
  48.9 17.2 %all-to-all-start = ((bf16[4,640,256]{2,1,0:T(8,128)(2,1)}), bf16[4,640,256]{2,1,0:T(8,128)(2,1)S(1)}, u32[]{:S(2)}, u32[]{:S(2)}) async-start(bf16[4,640,256]{2,1,0:T(8,128)(2,1)} %get-tuple-element.43), calls=%async_computation | async-start | bytes 2621440 | tf_op jit(solution)/shard_map/all_to_all | solution.py:218
  53.1 2.1 %copy-start.15 = (bf16[128,1664]{1,0:T(8,128)(2,1)}, bf16[128,1664]{1,0:T(8,128)(2,1)S(1)}, u32[]{:S(2)}) copy-start(bf16[128,1664]{1,0:T(8,128)(2,1)S(1)} %collective-permute-done.6.refs_1_.refs_4_) | copy-start | bytes 1277956
  53.1 15.8 %collective-permute-start.12 = (bf16[1664,128]{1,0:T(8,128)(2,1)}, bf16[1664,128]{1,0:T(8,128)(2,1)}, u32[]{:S(2)}, u32[]{:S(2)}) collective-permute-start(bf16[1664,128]{1,0:T(8,128)(2,1)} %collective-permute-done.11.refs_9_), channel_id=1, source_target_pairs={{0,12},{4,0},{8,4},{12,8},{1,13},{5,1},{9,5},{13,9},{2,14},{6,2},{... | collective-permute-start | bytes 1277960 | tf_op jit(solution)/shard_map/ppermute | solution.py:29
  61.0 15.0 %collective-permute-start.14 = (bf16[384,256]{1,0:T(8,128)(2,1)}, bf16[384,256]{1,0:T(8,128)(2,1)S(1)}, u32[]{:S(2)}, u32[]{:S(2)}) collective-permute-start(bf16[384,256]{1,0:T(8,128)(2,1)} %get-tuple-element.49), channel_id=1, source_target_pairs={{0,1},{1,2},{2,3},{3,0},{4,5},{5,6},{6,7},{7,4},{8,9},{9,10},{10,1... | collective-permute-start | bytes 589832 | tf_op jit(solution)/shard_map/ppermute | solution.py:29
  62.6 13.4 %collective-permute-start.15 = (bf16[384,256]{1,0:T(8,128)(2,1)}, bf16[384,256]{1,0:T(8,128)(2,1)S(1)}, u32[]{:S(2)}, u32[]{:S(2)}) collective-permute-start(bf16[384,256]{1,0:T(8,128)(2,1)} %get-tuple-element.50), channel_id=1, source_target_pairs={{0,2},{1,3},{2,0},{3,1},{4,6},{5,7},{6,4},{7,5},{8,10},{9,11},{10,... | collective-permute-start | bytes 589832 | tf_op jit(solution)/shard_map/ppermute | solution.py:29
  64.9 11.1 %collective-permute-start.16 = (bf16[384,256]{1,0:T(8,128)(2,1)}, bf16[384,256]{1,0:T(8,128)(2,1)S(1)}, u32[]{:S(2)}, u32[]{:S(2)}) collective-permute-start(bf16[384,256]{1,0:T(8,128)(2,1)} %get-tuple-element.51), channel_id=1, source_target_pairs={{0,3},{1,0},{2,1},{3,2},{4,7},{5,4},{6,5},{7,6},{8,11},{9,8},{10,9... | collective-permute-start | bytes 589832 | tf_op jit(solution)/shard_map/ppermute | solution.py:29
  66.5 9.6 %collective-permute-start.17 = (bf16[640,256]{1,0:T(8,128)(2,1)S(1)}, bf16[640,256]{1,0:T(8,128)(2,1)S(1)}, u32[]{:S(2)}, u32[]{:S(2)}) collective-permute-start(bf16[640,256]{1,0:T(8,128)(2,1)S(1)} %reduce_sum.34.refs_0_), channel_id=1, source_target_pairs={{0,12},{4,0},{8,4},{12,8},{1,13},{5,1},{9,5},{13,9},{2,14},{6,2},{... | collective-permute-start | bytes 983048 | tf_op jit(solution)/shard_map/ppermute | solution.py:29
  68.9 7.4 %collective-permute-start.18 = (bf16[640,256]{1,0:T(8,128)(2,1)S(1)}, bf16[640,256]{1,0:T(8,128)(2,1)S(1)}, u32[]{:S(2)}, u32[]{:S(2)}) collective-permute-start(bf16[640,256]{1,0:T(8,128)(2,1)S(1)} %reduce_sum.34.refs_0_), channel_id=1, source_target_pairs={{0,4},{4,8},{8,12},{12,0},{1,5},{5,9},{9,13},{13,1},{2,6},{6,10},{... | collective-permute-start | bytes 983048 | tf_op jit(solution)/shard_map/ppermute | solution.py:29
  68.9 7.1 %copy-start.7 = (bf16[384,256]{1,0:T(8,128)(2,1)S(1)}, bf16[384,256]{1,0:T(8,128)(2,1)}, u32[]{:S(2)}) copy-start(bf16[384,256]{1,0:T(8,128)(2,1)} %get-tuple-element.36) | copy-start | bytes 589828
  76.1 14.9 %copy-start = (s32[1,32]{1,0:T(1,128)S(1)}, s32[1,32]{1,0:T(1,128)}, u32[]{:S(2)}) copy-start(s32[1,32]{1,0:T(1,128)} %param.7) | copy-start | bytes 388
  76.3 14.2 %all-to-all-start.1 = ((bf16[4,1024,128]{2,1,0:T(8,128)(2,1)}), bf16[4,1024,128]{2,1,0:T(8,128)(2,1)S(1)}, u32[]{:S(2)}, u32[]{:S(2)}) async-start(bf16[4,1024,128]{2,1,0:T(8,128)(2,1)} %get-tuple-element.55), calls=%async_computation.1 | async-start | bytes 2097152 | tf_op jit(solution)/shard_map/all_to_all | solution.py:218
  80.8 10.2 %collective-permute-start.19 = (bf16[640,256]{1,0:T(8,128)(2,1)S(1)}, bf16[640,256]{1,0:T(8,128)(2,1)S(1)}, u32[]{:S(2)}, u32[]{:S(2)}) collective-permute-start(bf16[640,256]{1,0:T(8,128)(2,1)S(1)} %collective-permute-done.17.refs_1_), channel_id=1, source_target_pairs={{0,12},{4,0},{8,4},{12,8},{1,13},{5,1},{9,5},{13,9},{2,14},{6,2},{... | collective-permute-start | bytes 983048 | tf_op jit(solution)/shard_map/ppermute | solution.py:29
  82.6 8.4 %collective-permute-start.20 = (bf16[384,256]{1,0:T(8,128)(2,1)S(1)}, bf16[384,256]{1,0:T(8,128)(2,1)S(1)}, u32[]{:S(2)}, u32[]{:S(2)}) collective-permute-start(bf16[384,256]{1,0:T(8,128)(2,1)S(1)} %add_convert_fusion.refs_4_), channel_id=1, source_target_pairs={{0,12},{4,0},{8,4},{12,8},{1,13},{5,1},{9,5},{13,9},{2,14},{6,2},{... | collective-permute-start | bytes 589832 | tf_op jit(solution)/shard_map/ppermute | solution.py:29
  82.6 8.4 %collective-permute-start.21 = (bf16[384,256]{1,0:T(8,128)(2,1)S(1)}, bf16[384,256]{1,0:T(8,128)(2,1)S(1)}, u32[]{:S(2)}, u32[]{:S(2)}) collective-permute-start(bf16[384,256]{1,0:T(8,128)(2,1)S(1)} %add_convert_fusion.refs_4_), channel_id=1, source_target_pairs={{0,8},{4,12},{8,0},{12,4},{1,9},{5,13},{9,1},{13,5},{2,10},{6,14},... | collective-permute-start | bytes 589832 | tf_op jit(solution)/shard_map/ppermute | solution.py:29
  84.0 7.0 %collective-permute-start.22 = (bf16[384,256]{1,0:T(8,128)(2,1)S(1)}, bf16[384,256]{1,0:T(8,128)(2,1)S(1)}, u32[]{:S(2)}, u32[]{:S(2)}) collective-permute-start(bf16[384,256]{1,0:T(8,128)(2,1)S(1)} %add_convert_fusion.refs_4_), channel_id=1, source_target_pairs={{0,4},{4,8},{8,12},{12,0},{1,5},{5,9},{9,13},{13,1},{2,6},{6,10},{... | collective-permute-start | bytes 589832 | tf_op jit(solution)/shard_map/ppermute | solution.py:29
  94.1 12.6 %collective-permute-start.23 = (bf16[256,128]{1,0:T(8,128)(2,1)S(1)}, bf16[256,128]{1,0:T(8,128)(2,1)S(1)}, u32[]{:S(2)}, u32[]{:S(2)}) collective-permute-start(bf16[256,128]{1,0:T(8,128)(2,1)S(1)} %get-tuple-element.64), channel_id=1, source_target_pairs={{0,0},{1,4},{2,8},{3,12},{4,1},{5,5},{6,9},{7,13},{8,2},{9,6},{10,... | collective-permute-start | bytes 196616 | tf_op jit(solution)/shard_map/ppermute | solution.py:376
  94.8 12.9 %collective-permute-start.24 = (bf16[256,128]{1,0:T(8,128)(2,1)S(1)}, bf16[256,128]{1,0:T(8,128)(2,1)S(1)}, u32[]{:S(2)}, u32[]{:S(2)}) collective-permute-start(bf16[256,128]{1,0:T(8,128)(2,1)S(1)} %get-tuple-element.63), channel_id=1, source_target_pairs={{0,1},{1,5},{2,9},{3,13},{4,2},{5,6},{6,10},{7,14},{8,3},{9,7},{10... | collective-permute-start | bytes 196616 | tf_op jit(solution)/shard_map/ppermute | solution.py:376
  100.1 7.6 %collective-permute-start.25 = (bf16[256,128]{1,0:T(8,128)(2,1)S(1)}, bf16[256,128]{1,0:T(8,128)(2,1)S(1)}, u32[]{:S(2)}, u32[]{:S(2)}) collective-permute-start(bf16[256,128]{1,0:T(8,128)(2,1)S(1)} %get-tuple-element.62), channel_id=1, source_target_pairs={{0,2},{1,6},{2,10},{3,14},{4,3},{5,7},{6,11},{7,15},{8,0},{9,4},{1... | collective-permute-start | bytes 196616 | tf_op jit(solution)/shard_map/ppermute | solution.py:376
  104.6 5.6 %collective-permute-start.26 = (bf16[256,128]{1,0:T(8,128)(2,1)S(1)}, bf16[256,128]{1,0:T(8,128)(2,1)S(1)}, u32[]{:S(2)}, u32[]{:S(2)}) collective-permute-start(bf16[256,128]{1,0:T(8,128)(2,1)S(1)} %get-tuple-element.61), channel_id=1, source_target_pairs={{0,3},{1,7},{2,11},{3,15},{4,0},{5,4},{6,8},{7,12},{8,1},{9,5},{10... | collective-permute-start | bytes 196616 | tf_op jit(solution)/shard_map/ppermute | solution.py:376
  106.7 3.5 %copy-start.8 = (bf16[256,128]{1,0:T(8,128)(2,1)}, bf16[256,128]{1,0:T(8,128)(2,1)S(1)}, u32[]{:S(2)}) copy-start(bf16[256,128]{1,0:T(8,128)(2,1)S(1)} %collective-permute-done.23.refs_0_) | copy-start | bytes 196612
  107.7 2.6 %copy-start.9 = (bf16[256,128]{1,0:T(8,128)(2,1)}, bf16[256,128]{1,0:T(8,128)(2,1)S(1)}, u32[]{:S(2)}) copy-start(bf16[256,128]{1,0:T(8,128)(2,1)S(1)} %collective-permute-done.24.refs_1_) | copy-start | bytes 196612
  107.7 2.6 %copy-start.10 = (bf16[256,128]{1,0:T(8,128)(2,1)}, bf16[256,128]{1,0:T(8,128)(2,1)S(1)}, u32[]{:S(2)}) copy-start(bf16[256,128]{1,0:T(8,128)(2,1)S(1)} %collective-permute-done.25.refs_2_) | copy-start | bytes 196612
  110.3 0.6 copy-start.11
  112.7 16.4 %collective-permute-start.27 = (bf16[1,1024,128]{2,1,0:T(8,128)(2,1)}, bf16[1,1024,128]{2,1,0:T(8,128)(2,1)S(1)}, u32[]{:S(2)}, u32[]{:S(2)}) collective-permute-start(bf16[1,1024,128]{2,1,0:T(8,128)(2,1)} %bitcast.24), channel_id=1, source_target_pairs={{0,128},{128,0},{1,129},{129,1},{2,130},{130,2},{3,131},{131,3},{4... | collective-permute-start | bytes 786440 | tf_op jit(solution)/shard_map/ppermute | solution.py:29
